TPU v7x, 32 devices: a whole 2x2x4 slice. The times are simulated.
32 devices in a mesh: slab: 8 (over z, y), load: 4 (over x, core).
Axes of the slice: x: 2, y: 2, z: 4, core: 2. Of those that a mesh axis runs over, the one named last changes fastest.
Arguments:
- start_disp: float32 [8, 3, 8, 64, 128], P('load', None, 'slab'), may hold values from -10 to 10
- density: float32 [8, 64, 128], P('slab'), may hold values from 0.05 to 1
- design: int32 [8, 64, 128], P('slab'), may hold values from 0 to 1, as said below
- support: int32 [8, 64, 128], P('slab'), may hold values 0 or 1
- load_nodes: int32 [8, 2048], P('load'), may hold values from 0 to 65535
- load_forces: float32 [8, 3, 2048], P('load'), may hold values from -6 to 6
Outputs:
- displacement: float32 [8, 3, 8, 64, 128], P('load', None, 'slab')
- new_density: float32 [8, 64, 128], P('slab')
Inputs may be any that keep to these rules, and one draw needn't show every extreme that they name: 1 marks an element of the design domain, 0 a void element; at least one element is in the design domain. `support`: 1 marks a node held fixed. `load_nodes`: flat node index z * 64 * 128 + x * 128 + y; a node may carry several forces of one load case.
All inputs are finite; a program needn't handle non-finite values. No bound on the sum of `support` on one device may be relied on, other than what follows from the above.
Results may differ from a plain program's by a relative error of at most 0.00024.
Values sent between devices are 32-bit elements; how exact they have to be, the bound alone decides.
No kernel may reach another device: no remote copies, remote signals or barrier semaphores. Data moves between devices by JAX's collectives and lax.ppermute only.
A program may use at most 64 MiB of HBM per device.

v0:
```python
import jax
import jax.numpy as jnp
import numpy as np
from jax import lax
from jax.sharding import PartitionSpec as P

SWEEPS = 4
RADIUS = 2


POISSON = 0.3
STIFF_VOID = 0.001
UPPER_FACTOR = 1.2
LOWER_RATIO = 0.1
MOVE_LIMIT = 0.2
VOLUME_TARGET = 0.5
EPSILON = 1e-06
HIGHEST = lax.Precision.HIGHEST


def passed_along(value, axis, steps):
    count = lax.axis_size(axis)
    leading, last = (max(0, -steps), min(count, count - steps))
    return lax.ppermute(value, axis, [(source, source + steps) for source in range(leading, last)])


def hex_stiffness():
    lame_first = POISSON / ((1 + POISSON) * (1 - 2 * POISSON))
    lame_shear = 1 / (2 * (1 + POISSON))
    elastic = np.zeros((6, 6))
    elastic[:3, :3] = lame_first
    for axis_a in range(3):
        elastic[axis_a, axis_a] += 2 * lame_shear
        elastic[3 + axis_a, 3 + axis_a] = lame_shear
    shear_pairs = ((0, 1), (1, 2), (0, 2))
    gauss_point = 1 / np.sqrt(3)
    matrix = np.zeros((24, 24))
    for quad_index in range(8):
        quad_coords = [
            gauss_point * (2 * (quad_index >> 2 - axis_a & 1) - 1) for axis_a in range(3)
        ]
        shape_grads = np.zeros((8, 3))
        for corner in range(8):
            corner_signs = [2 * (corner >> 2 - axis_a & 1) - 1 for axis_a in range(3)]
            for axis_a in range(3):
                deriv_value = float(corner_signs[axis_a])
                for axis_b in range(3):
                    if axis_b != axis_a:
                        deriv_value *= (1 + corner_signs[axis_b] * quad_coords[axis_b]) / 2
                shape_grads[corner, axis_a] = deriv_value
        strain = np.zeros((6, 24))
        for corner in range(8):
            for axis_a in range(3):
                strain[axis_a, 3 * corner + axis_a] = shape_grads[corner, axis_a]
            for pair_index, shear_pair in enumerate(shear_pairs):
                strain[3 + pair_index, 3 * corner + shear_pair[0]] = shape_grads[
                    corner, shear_pair[1]
                ]
                strain[3 + pair_index, 3 * corner + shear_pair[1]] = shape_grads[
                    corner, shear_pair[0]
                ]
        matrix += strain.T @ elastic @ strain / 8
    return matrix.astype(np.float32)


def ahead(field, axis):
    length = field.shape[axis]
    zero_shape = list(field.shape)
    zero_shape[axis] = 1
    inner_part = lax.slice_in_dim(field, 1, length, axis=axis)
    return jnp.concatenate([inner_part, jnp.zeros(zero_shape, field.dtype)], axis)


def behind(field, axis):
    length = field.shape[axis]
    zero_shape = list(field.shape)
    zero_shape[axis] = 1
    inner_part = lax.slice_in_dim(field, 0, length - 1, axis=axis)
    return jnp.concatenate([jnp.zeros(zero_shape, field.dtype), inner_part], axis)


def corner_block(bottom, top):
    corner_parts = []
    for corner in range(8):
        corner_part = top if corner >> 2 & 1 else bottom
        if corner >> 1 & 1:
            corner_part = ahead(corner_part, corner_part.ndim - 2)
        if corner & 1:
            corner_part = ahead(corner_part, corner_part.ndim - 1)
        corner_parts.append(corner_part)
    stacked = jnp.stack(corner_parts, -4)
    return stacked.reshape(stacked.shape[:-4] + (24, stacked.shape[-2] * stacked.shape[-1]))


def spread_block(forces, rows_x, cols_y):
    shaped = forces.reshape(forces.shape[:-2] + (8, 3, rows_x, cols_y))
    to_bottom = jnp.zeros(shaped.shape[:-4] + (3, rows_x, cols_y), jnp.float32)
    to_top = to_bottom
    for corner in range(8):
        corner_part = shaped[..., corner, :, :, :]
        if corner >> 1 & 1:
            corner_part = behind(corner_part, corner_part.ndim - 2)
        if corner & 1:
            corner_part = behind(corner_part, corner_part.ndim - 1)
        if corner >> 2 & 1:
            to_top = to_top + corner_part
        else:
            to_bottom = to_bottom + corner_part
    return (to_bottom, to_top)


def gauss_table(count):
    offsets = (
        lax.broadcasted_iota(jnp.int32, (count, count), 0)
        - lax.broadcasted_iota(jnp.int32, (count, count), 1)
    ).astype(jnp.float32)
    return jnp.exp(-((offsets / RADIUS) ** 2))


def smooth_plane(field, table_x, table_y):
    mixed = jnp.einsum("zab,ia->zib", field, table_x, precision=HIGHEST)
    return jnp.einsum("zib,jb->zij", mixed, table_y, precision=HIGHEST)


def filter_depth(fields):
    pieces = (
        lax.all_to_all(fields[0], "slab", split_axis=1, concat_axis=0, tiled=True),
        lax.all_to_all(fields[1], "slab", split_axis=1, concat_axis=0, tiled=True),
    )
    depth_table = gauss_table(pieces[0].shape[0])
    mixed = tuple(
        (jnp.einsum("kz,zgw->kgw", depth_table, piece, precision=HIGHEST) for piece in pieces)
    )
    return lax.all_to_all(mixed, "slab", split_axis=0, concat_axis=1, tiled=True)


def revise(numer_f, denom_f, dens, mask, first_sum, second_sum):
    weighted = mask * (numer_f / denom_f)
    weighted_total, count = first_sum((jnp.sum(weighted), jnp.sum(mask)))
    ratio = weighted / (weighted_total / count + EPSILON)
    trial = jnp.clip(dens * jnp.sqrt(ratio), dens - MOVE_LIMIT, dens + MOVE_LIMIT)
    volume = second_sum(jnp.sum(mask * trial))
    scale = VOLUME_TARGET / (volume / count + EPSILON)
    return mask * jnp.minimum(scale * trial, 1.0)


def per_load(values):
    return values[:, None, None, None, None]


def shards(start_disp, density, design, support, load_nodes, load_forces):
    stiff_table = hex_stiffness()
    kmatrix = jnp.asarray(stiff_table)
    diag_entry = float(stiff_table[0, 0])
    loads_here = start_disp.shape[0]
    layers = start_disp.shape[2]
    rows_x = start_disp.shape[3]
    cols_y = start_disp.shape[4]
    plane_count = rows_x * cols_y
    design_mask = design.astype(jnp.float32)
    fixed_mask = support.astype(jnp.float32)
    free_mask = 1.0 - fixed_mask
    solid_part = design_mask * density
    stiffness = STIFF_VOID + (1.0 - STIFF_VOID) * solid_part**3
    stiff_below = passed_along(stiffness, "slab", 1)
    stiff_ext = jnp.concatenate([stiff_below, stiffness], 0)
    beside_all = stiff_ext[1:] + stiff_ext[:-1]
    beside_all = beside_all + behind(beside_all, 1)
    beside_all = beside_all + behind(beside_all, 2)
    diagonal = free_mask * diag_entry * beside_all + fixed_mask
    stiff_rows = stiff_ext.reshape(layers + 1, plane_count)

    def layer_forces(bottom, top, row_index):
        corner_vals = corner_block(bottom, top)
        forces = (
            jnp.einsum("ab,lbn->lan", kmatrix, corner_vals, precision=HIGHEST)
            * stiff_rows[row_index]
        )
        return spread_block(forces, rows_x, cols_y)

    def upper_layer(field):
        return passed_along(field[:, :, :1], "slab", -1)

    def apply_stiffness(field):
        node_layers = [field[:, :, 0]] + [upper_layer(field)[:, :, 0]]
        layer_sums = [jnp.zeros_like(node_layers[0]) for layer_index in range(layers + 1)]
        layer_index = 0
        to_bottom, to_top = layer_forces(
            node_layers[layer_index], node_layers[layer_index + 1], layer_index + 1
        )
        layer_sums[layer_index] = layer_sums[layer_index] + to_bottom
        layer_sums[layer_index + 1] = layer_sums[layer_index + 1] + to_top
        carried = passed_along(layer_sums[layers][:, :, None], "slab", 1)
        layer_sums[0] = layer_sums[0] + carried[:, :, 0]
        return jnp.stack(layer_sums[:layers], 2)

    def operate(field):
        return free_mask * apply_stiffness(free_mask * field) + fixed_mask * field

    node_count = layers * plane_count
    offset = lax.axis_index("slab") * node_count
    local_index = load_nodes - offset
    local_index = jnp.where(
        (local_index >= 0) & (local_index < node_count), local_index, node_count
    )

    def place_loads(indices, values):
        return jnp.zeros((3, node_count), jnp.float32).at[:, indices].add(values, mode="drop")

    right_side = (
        jax.vmap(place_loads)(local_index, load_forces).reshape(
            loads_here, 3, layers, rows_x, cols_y
        )
        * free_mask
    )
    residual = right_side - operate(start_disp)
    precond = residual / diagonal
    applied = operate(precond)
    curvature, weight_norm = lax.psum(
        (
            jnp.sum(precond * applied, axis=(1, 2, 3, 4)),
            jnp.sum(precond * residual, axis=(1, 2, 3, 4)),
        ),
        "slab",
    )
    upper_bound = UPPER_FACTOR * curvature / weight_norm
    lower_bound = LOWER_RATIO * upper_bound
    center = per_load(0.5 * (upper_bound + lower_bound))
    half_width = per_load(0.5 * (upper_bound - lower_bound))
    spread_ratio = center / half_width
    factor = 1.0 / spread_ratio
    update = precond / center
    solution = start_disp
    for sweep_index in range(SWEEPS):
        solution = solution + update
        if sweep_index < SWEEPS - 1:
            if sweep_index == 0:
                product = applied / center
            else:
                product = operate(update)
            residual = residual - product
            factor_next = 1.0 / (2.0 * spread_ratio - factor)
            update = factor_next * factor * update + 2.0 * factor_next / half_width * (
                residual / diagonal
            )
            factor = factor_next
    free_part = free_mask * solution
    node_layers = [free_part[:, :, 0]] + [upper_layer(free_part)[:, :, 0]]
    layer_index = 0
    corner_vals = corner_block(node_layers[layer_index], node_layers[layer_index + 1])
    forces = jnp.einsum("ab,lbn->lan", kmatrix, corner_vals, precision=HIGHEST)
    energies = [jnp.sum(corner_vals * forces, axis=(0, 1))]
    energy_here = jnp.stack(energies, 0).reshape(layers, rows_x, cols_y)
    weight_term = density * (3.0 * (1.0 - STIFF_VOID)) * solid_part**2
    table_x = gauss_table(rows_x)
    table_y = gauss_table(cols_y)
    slab_count = lax.axis_size("slab")
    energy_sum = lax.psum(energy_here, "load")
    width = plane_count // slab_count
    numer = smooth_plane(weight_term * energy_sum, table_x, table_y).reshape(layers, -1, width)
    denom = smooth_plane(density, table_x, table_y).reshape(layers, -1, width)
    numer_f, denom_f = filter_depth((numer, denom))
    revised = revise(
        numer_f,
        denom_f,
        density.reshape(layers, -1, width),
        design_mask.reshape(layers, -1, width),
        lambda stat_pair: lax.psum(stat_pair, "slab"),
        lambda vol_part: lax.psum(vol_part, "slab"),
    )
    new_density = revised.reshape(layers, rows_x, cols_y)
    return (solution, new_density)


def solution(mesh):
    return jax.shard_map(
        shards,
        mesh=mesh,
        in_specs=(
            P("load", None, "slab", None, None),
            P("slab", None, None),
            P("slab", None, None),
            P("slab", None, None),
            P("load", None),
            P("load", None, None),
        ),
        out_specs=(P("load", None, "slab", None, None), P("slab", None, None)),
        check_vma=False,
    )
```

profile of v0, /device:TPU:0, one launch (start us, length us, event | category | flops | bytes accessed | tf_op | source)
XLA Modules:
  0.0 249.2 jit_solution(15569362746721799437)
XLA Ops:
  0.6 0.8 fusion.62
  1.4 4.9 %collective-permute-start.2 = (f32[1,64,128]{2,1,0:T(8,128)S(1)}, f32[1,64,128]{2,1,0:T(8,128)S(1)}, u32[]{:S(2)}, u32[]{:S(2)}) collective-permute-start(f32[1,64,128]{2,1,0:T(8,128)S(1)} %fusion.62), channel_id=1, source_target_pairs={{0,4},{4,8},{8,12},{12,16},{16,20},{20,24},{24,28},{1,5},{5,9},{9,... | collective-permute-start | bytes 98312 | tf_op jit(solution)/shard_map/ppermute | solution.py:24
  6.3 0.7 fusion.77
  7.1 0.8 multiply_reduce_fusion.2
  7.8 0.8 and_reduce_fusion
  8.6 0.8 convert_bitcast_fusion
  9.4 1.4 copy.141
  10.8 26.1 %scatter_custom_fusion = f32[3,16384]{0,1:T(8,128)} fusion(s32[4096]{0:T(1024)S(1)} %bitcast.521, f32[4096,3]{1,0:T(8,128)S(1)} %bitcast.464, f32[]{:T(128)} %constant.18.clone.1), kind=kCustom, calls=%fused_computation.7 | custom fusion | flops 12288 | bytes 196612
  36.9 5.3 %copy.95 = f32[3,2,8192]{2,1,0:T(2,128)S(1)} copy(f32[3,2,8192]{0,2,1:T(8,128)} %bitcast.455) | data formatting | bytes 393216
  42.1 0.9 reshape.221
  43.3 1.3 collective-permute-start
  44.8 6.8 %collective-permute-done = f32[2,3,1,64,128]{4,3,0,1,2:T(8,128)S(1)} collective-permute-done((f32[2,3,1,64,128]{4,3,0,1,2:T(8,128)S(1)}, f32[2,3,1,64,128]{4,3,0,1,2:T(8,128)S(1)}, u32[]{:S(2)}, u32[]{:S(2)}) %collective-permute-start) | collective-permute-done | bytes 196640 | tf_op jit(solution)/shard_map/ppermute | solution.py:24
  51.9 0.9 reshape.248
  52.8 2.3 convolution_multiply_fusion.3
  55.2 0.3 copy.182
  55.9 4.3 %collective-permute-start.1 = (f32[2,3,1,64,128]{4,3,0,1,2:T(8,128)S(1)}, f32[2,3,1,64,128]{4,3,0,1,2:T(8,128)S(1)}, u32[]{:S(2)}, u32[]{:S(2)}) collective-permute-start(f32[2,3,1,64,128]{4,3,0,1,2:T(8,128)S(1)} %fusion.50), channel_id=1, source_target_pairs={{0,4},{4,8},{8,12},{12,16},{16,20},{20,24},{24,28},{1,5},{5,9},{9,... | collective-permute-start | bytes 589832 | tf_op jit(solution)/shard_map/ppermute | solution.py:24
  60.4 3.1 %collective-permute-done.1 = f32[2,3,1,64,128]{4,3,0,1,2:T(8,128)S(1)} collective-permute-done((f32[2,3,1,64,128]{4,3,0,1,2:T(8,128)S(1)}, f32[2,3,1,64,128]{4,3,0,1,2:T(8,128)S(1)}, u32[]{:S(2)}, u32[]{:S(2)}) %collective-permute-start.1) | collective-permute-done | bytes 196640 | tf_op jit(solution)/shard_map/ppermute | solution.py:24
  63.8 1.5 collective-permute-start.3
  65.4 6.4 %collective-permute-done.3 = f32[2,3,1,64,128]{4,3,0,1,2:T(8,128)S(1)} collective-permute-done((f32[2,3,1,64,128]{4,3,0,1,2:T(8,128)S(1)}, f32[2,3,1,64,128]{4,3,0,1,2:T(8,128)S(1)}, u32[]{:S(2)}, u32[]{:S(2)}) %collective-permute-start.3) | collective-permute-done | bytes 196640 | tf_op jit(solution)/shard_map/ppermute | solution.py:24
  72.2 0.9 reshape.249
  73.0 2.3 convolution_multiply_fusion.2
  75.4 0.3 copy.183
  76.1 4.8 %collective-permute-start.4 = (f32[2,3,1,64,128]{4,3,0,1,2:T(8,128)S(1)}, f32[2,3,1,64,128]{4,3,0,1,2:T(8,128)S(1)}, u32[]{:S(2)}, u32[]{:S(2)}) collective-permute-start(f32[2,3,1,64,128]{4,3,0,1,2:T(8,128)S(1)} %fusion.39), channel_id=1, source_target_pairs={{0,4},{4,8},{8,12},{12,16},{16,20},{20,24},{24,28},{1,5},{5,9},{9,... | collective-permute-start | bytes 589832 | tf_op jit(solution)/shard_map/ppermute | solution.py:24
  81.1 3.1 %collective-permute-done.4 = f32[2,3,1,64,128]{4,3,0,1,2:T(8,128)S(1)} collective-permute-done((f32[2,3,1,64,128]{4,3,0,1,2:T(8,128)S(1)}, f32[2,3,1,64,128]{4,3,0,1,2:T(8,128)S(1)}, u32[]{:S(2)}, u32[]{:S(2)}) %collective-permute-start.4) | collective-permute-done | bytes 196640 | tf_op jit(solution)/shard_map/ppermute | solution.py:24
  84.1 0.3 multiply_reduce_fusion.1
  84.4 20.3 %all-reduce.65 = (f32[2]{0:T(128)S(1)}, f32[2]{0:T(128)S(1)}) all-reduce(f32[2]{0:T(128)S(1)} %get-tuple-element.7, f32[2]{0:T(128)S(1)} %get-tuple-element.6), channel_id=1, replica_groups=mesh['slab'=8,'load'=4] {'slab'}, use_global_device_ids=true, to_apply=%region_4.5 | all-reduce | flops 4 | bytes 32 | tf_op jit(solution)/shard_map/psum | solution.py:219
  104.7 0.5 fusion.94
  105.3 0.6 multiply_divide_fusion.1
  105.9 0.8 bitcast_dynamic-update-slice_fusion.23
  106.8 1.3 collective-permute-start.5
  108.3 6.1 %collective-permute-done.5 = f32[2,3,1,64,128]{4,3,0,1,2:T(8,128)S(1)} collective-permute-done((f32[2,3,1,64,128]{4,3,0,1,2:T(8,128)S(1)}, f32[2,3,1,64,128]{4,3,0,1,2:T(8,128)S(1)}, u32[]{:S(2)}, u32[]{:S(2)}) %collective-permute-start.5) | collective-permute-done | bytes 196640 | tf_op jit(solution)/shard_map/ppermute | solution.py:24
  114.8 0.9 reshape.250
  115.6 2.3 convolution_multiply_fusion.1
  118.0 0.3 copy.184
  118.8 3.5 %collective-permute-start.6 = (f32[2,3,1,64,128]{4,3,0,1,2:T(8,128)S(1)}, f32[2,3,1,64,128]{4,3,0,1,2:T(8,128)S(1)}, u32[]{:S(2)}, u32[]{:S(2)}) collective-permute-start(f32[2,3,1,64,128]{4,3,0,1,2:T(8,128)S(1)} %fusion.27), channel_id=1, source_target_pairs={{0,4},{4,8},{8,12},{12,16},{16,20},{20,24},{24,28},{1,5},{5,9},{9,... | collective-permute-start | bytes 589832 | tf_op jit(solution)/shard_map/ppermute | solution.py:24
  122.5 3.4 %collective-permute-done.6 = f32[2,3,1,64,128]{4,3,0,1,2:T(8,128)S(1)} collective-permute-done((f32[2,3,1,64,128]{4,3,0,1,2:T(8,128)S(1)}, f32[2,3,1,64,128]{4,3,0,1,2:T(8,128)S(1)}, u32[]{:S(2)}, u32[]{:S(2)}) %collective-permute-start.6) | collective-permute-done | bytes 196640 | tf_op jit(solution)/shard_map/ppermute | solution.py:24
  126.0 0.9 bitcast_dynamic-update-slice_fusion.15
  127.0 1.5 collective-permute-start.7
  128.7 6.3 %collective-permute-done.7 = f32[2,3,1,64,128]{4,3,0,1,2:T(8,128)S(1)} collective-permute-done((f32[2,3,1,64,128]{4,3,0,1,2:T(8,128)S(1)}, f32[2,3,1,64,128]{4,3,0,1,2:T(8,128)S(1)}, u32[]{:S(2)}, u32[]{:S(2)}) %collective-permute-start.7) | collective-permute-done | bytes 196640 | tf_op jit(solution)/shard_map/ppermute | solution.py:24
  135.4 0.9 reshape.251
  136.3 2.3 convolution_multiply_fusion
  138.6 0.3 copy.185
  139.4 5.7 %collective-permute-start.8 = (f32[2,3,1,64,128]{4,3,0,1,2:T(8,128)S(1)}, f32[2,3,1,64,128]{4,3,0,1,2:T(8,128)}, u32[]{:S(2)}, u32[]{:S(2)}) collective-permute-start(f32[2,3,1,64,128]{4,3,0,1,2:T(8,128)S(1)} %fusion.14), channel_id=1, source_target_pairs={{0,4},{4,8},{8,12},{12,16},{16,20},{20,24},{24,28},{1,5},{5,9},{9,... | collective-permute-start | bytes 589832 | tf_op jit(solution)/shard_map/ppermute | solution.py:24
  145.1 0.9 fusion.59
  146.0 3.3 %all-to-all-start.2 = ((f32[1,8,1024]{2,0,1:T(1,128)}), f32[1,8,1024]{2,0,1:T(1,128)S(1)}, u32[]{:S(2)}, u32[]{:S(2)}) async-start(f32[1,8,1024]{2,0,1:T(1,128)} %bitcast.114), calls=%async_computation.2 | async-start | bytes 65536 | tf_op jit(solution)/shard_map/all_to_all | solution.py:128
  149.5 1.9 bitcast_dynamic-update-slice_fusion.7
  151.5 1.3 collective-permute-start.9
  153.0 6.1 %collective-permute-done.9 = f32[2,3,1,64,128]{4,3,0,1,2:T(8,128)S(1)} collective-permute-done((f32[2,3,1,64,128]{4,3,0,1,2:T(8,128)S(1)}, f32[2,3,1,64,128]{4,3,0,1,2:T(8,128)S(1)}, u32[]{:S(2)}, u32[]{:S(2)}) %collective-permute-start.9) | collective-permute-done | bytes 196640 | tf_op jit(solution)/shard_map/ppermute | solution.py:24
  159.4 0.9 reshape.252
  160.3 3.1 %fusion.8 = f32[8192]{0:T(1024)S(1)} fusion(f32[24,24,1]{1,0,2:T(8,128)S(1)} %copy-done.12, f32[2,24,8192]{2,0,1:T(2,128)S(1)} %reshape.252), kind=kOutput, calls=%fused_computation.14 | convolution fusion | flops 114024448 | bytes 1607936 | tf_op jit(solution)/shard_map/ab,lbn->lan/dot_general | solution.py:251
  163.5 10.3 %psum.44 = f32[1,64,128]{2,1,0:T(8,128)S(1)} all-reduce(f32[1,64,128]{2,1,0:T(8,128)S(1)} %bitcast.519), channel_id=1, replica_groups=mesh['slab'=8,'load'=4] {'load'}, use_global_device_ids=true, to_apply=%region_6.7 | all-reduce | flops 8192 | bytes 65536 | tf_op jit(solution)/shard_map/psum | solution.py:258
  173.9 0.9 fusion.60
  174.8 5.9 %all-to-all-start = ((f32[1,8,1024]{2,0,1:T(1,128)}), f32[1,8,1024]{2,0,1:T(1,128)S(1)}, u32[]{:S(2)}, u32[]{:S(2)}) async-start(f32[1,8,1024]{2,0,1:T(1,128)} %bitcast.111), calls=%async_computation | async-start | bytes 65536 | tf_op jit(solution)/shard_map/all_to_all | solution.py:127
  180.9 0.7 copy.139
  181.5 5.9 %all-to-all-done = f32[1,8,1024]{2,0,1:T(1,128)S(1)} async-done(((f32[1,8,1024]{2,0,1:T(1,128)}), f32[1,8,1024]{2,0,1:T(1,128)S(1)}, u32[]{:S(2)}, u32[]{:S(2)}) %all-to-all-start) | async-done | bytes 32800 | tf_op jit(solution)/shard_map/all_to_all | solution.py:127
  187.4 3.3 %all-to-all-start.3 = ((f32[8,1,1024]{2,1,0:T(1,128)}), f32[8,1,1024]{2,1,0:T(1,128)S(1)}, u32[]{:S(2)}, u32[]{:S(2)}) async-start(f32[8,1,1024]{2,1,0:T(1,128)} %copy.139), calls=%async_computation.3 | async-start | bytes 65536 | tf_op jit(solution)/shard_map/all_to_all | solution.py:134
  190.9 6.4 %all-to-all-done.3 = f32[8,1,1024]{2,1,0:T(1,128)S(1)} async-done(((f32[8,1,1024]{2,1,0:T(1,128)}), f32[8,1,1024]{2,1,0:T(1,128)S(1)}, u32[]{:S(2)}, u32[]{:S(2)}) %all-to-all-start.3) | async-done | bytes 32800 | tf_op jit(solution)/shard_map/all_to_all | solution.py:134
  197.3 9.0 %all_to_all.16 = f32[8,1,1024]{2,1,0:T(1,128)S(1)} all-to-all(f32[8,1,1024]{2,1,0:T(1,128)S(1)} %copy.137), channel_id=1, replica_groups=mesh['slab'=8,'load'=4] {'slab'}, dimensions={0} | all-to-all | bytes 65536 | tf_op jit(solution)/shard_map/all_to_all | solution.py:134
  206.4 0.6 convert_reduce_fusion
  207.1 18.4 %all-reduce.64 = (f32[]{:T(128)}, f32[]{:T(128)}) all-reduce(f32[]{:T(128)} %get-tuple-element.9, f32[]{:T(128)} %get-tuple-element.8), channel_id=1, replica_groups=mesh['slab'=8,'load'=4] {'slab'}, use_global_device_ids=true, to_apply=%region_8.9 | all-reduce | flops 2 | bytes 16 | tf_op jit(solution)/shard_map/psum | solution.py:268
  226.7 0.6 multiply_reduce_fusion.3
  227.4 0.7 copy.140
  228.1 19.1 %psum.47 = f32[]{:T(128)} all-reduce(f32[]{:T(128)} %multiply_reduce_fusion.3), channel_id=1, replica_groups=mesh['slab'=8,'load'=4] {'slab'}, use_global_device_ids=true, to_apply=%region_12.13 | all-reduce | flops 1 | bytes 8 | tf_op jit(solution)/shard_map/psum | solution.py:269
  248.6 0.6 minimum_multiply_fusion
  (153 shorter events, 6.0 us)
Async XLA Ops:
  1.4 41.6 %collective-permute-start.2 = (f32[1,64,128]{2,1,0:T(8,128)S(1)}, f32[1,64,128]{2,1,0:T(8,128)S(1)}, u32[]{:S(2)}, u32[]{:S(2)}) collective-permute-start(f32[1,64,128]{2,1,0:T(8,128)S(1)} %fusion.62), channel_id=1, source_target_pairs={{0,4},{4,8},{8,12},{12,16},{16,20},{20,24},{24,28},{1,5},{5,9},{9,... | collective-permute-start | bytes 98312 | tf_op jit(solution)/shard_map/ppermute | solution.py:24
  36.9 6.2 %copy-start.13 = (s32[1,64,128]{2,1,0:T(8,128)S(1)}, s32[1,64,128]{2,1,0:T(8,128)}, u32[]{:S(2)}) copy-start(s32[1,64,128]{2,1,0:T(8,128)} %param.10) | copy-start | bytes 98308
  36.9 6.3 %copy-start = (f32[2,3,1,64,128]{4,3,2,1,0:T(8,128)S(1)}, f32[2,3,1,64,128]{4,3,2,1,0:T(8,128)}, u32[]{:S(2)}) copy-start(f32[2,3,1,64,128]{4,3,2,1,0:T(8,128)} %param.7) | copy-start | bytes 589828
  43.3 8.3 %collective-permute-start = (f32[2,3,1,64,128]{4,3,0,1,2:T(8,128)S(1)}, f32[2,3,1,64,128]{4,3,0,1,2:T(8,128)S(1)}, u32[]{:S(2)}, u32[]{:S(2)}) collective-permute-start(f32[2,3,1,64,128]{4,3,0,1,2:T(8,128)S(1)} %get-tuple-element.35), channel_id=1, source_target_pairs={{4,0},{8,4},{12,8},{16,12},{20,16},{24,20},{28,24},{5,1},{9,5},{13... | collective-permute-start | bytes 589832 | tf_op jit(solution)/shard_map/ppermute | solution.py:24
  51.9 0.9 copy-start.12
  55.7 7.7 %copy-start.1 = (f32[2,3,1,64,128]{4,3,2,1,0:T(8,128)S(1)}, f32[2,3,1,64,128]{4,3,2,1,0:T(8,128)}, u32[]{:S(2)}) copy-start(f32[2,3,1,64,128]{4,3,2,1,0:T(8,128)} %param.7) | copy-start | bytes 589828
  55.7 7.7 %copy-start.11 = (f32[2,3,1,64,128]{4,3,0,1,2:T(8,128)S(1)}, f32[2,3,1,64,128]{4,3,0,1,2:T(8,128)}, u32[]{:S(2)}) copy-start(f32[2,3,1,64,128]{4,3,0,1,2:T(8,128)} %reshape.221) | copy-start | bytes 589828
  55.9 7.5 %collective-permute-start.1 = (f32[2,3,1,64,128]{4,3,0,1,2:T(8,128)S(1)}, f32[2,3,1,64,128]{4,3,0,1,2:T(8,128)S(1)}, u32[]{:S(2)}, u32[]{:S(2)}) collective-permute-start(f32[2,3,1,64,128]{4,3,0,1,2:T(8,128)S(1)} %fusion.50), channel_id=1, source_target_pairs={{0,4},{4,8},{8,12},{12,16},{16,20},{20,24},{24,28},{1,5},{5,9},{9,... | collective-permute-start | bytes 589832 | tf_op jit(solution)/shard_map/ppermute | solution.py:24
  63.8 8.0 %collective-permute-start.3 = (f32[2,3,1,64,128]{4,3,0,1,2:T(8,128)S(1)}, f32[2,3,1,64,128]{4,3,0,1,2:T(8,128)S(1)}, u32[]{:S(2)}, u32[]{:S(2)}) collective-permute-start(f32[2,3,1,64,128]{4,3,0,1,2:T(8,128)S(1)} %get-tuple-element.32), channel_id=1, source_target_pairs={{4,0},{8,4},{12,8},{16,12},{20,16},{24,20},{28,24},{5,1},{9,5},{13... | collective-permute-start | bytes 589832 | tf_op jit(solution)/shard_map/ppermute | solution.py:24
  76.1 8.0 %collective-permute-start.4 = (f32[2,3,1,64,128]{4,3,0,1,2:T(8,128)S(1)}, f32[2,3,1,64,128]{4,3,0,1,2:T(8,128)S(1)}, u32[]{:S(2)}, u32[]{:S(2)}) collective-permute-start(f32[2,3,1,64,128]{4,3,0,1,2:T(8,128)S(1)} %fusion.39), channel_id=1, source_target_pairs={{0,4},{4,8},{8,12},{12,16},{16,20},{20,24},{24,28},{1,5},{5,9},{9,... | collective-permute-start | bytes 589832 | tf_op jit(solution)/shard_map/ppermute | solution.py:24
  84.4 23.9 %copy-start.5 = (f32[2,3,1,64,128]{4,3,0,1,2:T(8,128)}, f32[2,3,1,64,128]{4,3,0,1,2:T(8,128)S(1)}, u32[]{:S(2)}) copy-start(f32[2,3,1,64,128]{4,3,0,1,2:T(8,128)S(1)} %get-tuple-element.30) | copy-start | bytes 589828
  106.8 7.6 %collective-permute-start.5 = (f32[2,3,1,64,128]{4,3,0,1,2:T(8,128)S(1)}, f32[2,3,1,64,128]{4,3,0,1,2:T(8,128)S(1)}, u32[]{:S(2)}, u32[]{:S(2)}) collective-permute-start(f32[2,3,1,64,128]{4,3,0,1,2:T(8,128)S(1)} %get-tuple-element.26), channel_id=1, source_target_pairs={{4,0},{8,4},{12,8},{16,12},{20,16},{24,20},{28,24},{5,1},{9,5},{13... | collective-permute-start | bytes 589832 | tf_op jit(solution)/shard_map/ppermute | solution.py:24
  118.4 3.8 %copy-start.7 = (f32[1,64,128]{2,1,0:T(8,128)S(1)}, f32[1,64,128]{2,1,0:T(8,128)}, u32[]{:S(2)}) copy-start(f32[1,64,128]{2,1,0:T(8,128)} %param.8) | copy-start | bytes 98308
  118.5 7.4 %copy-start.3 = (f32[2,3,1,64,128]{4,3,0,1,2:T(8,128)S(1)}, f32[2,3,1,64,128]{4,3,0,1,2:T(8,128)}, u32[]{:S(2)}) copy-start(f32[2,3,1,64,128]{4,3,0,1,2:T(8,128)} %get-tuple-element.27) | copy-start | bytes 589828
  118.5 7.4 %copy-start.6 = (f32[2,3,1,64,128]{4,3,0,1,2:T(8,128)S(1)}, f32[2,3,1,64,128]{4,3,0,1,2:T(8,128)}, u32[]{:S(2)}) copy-start(f32[2,3,1,64,128]{4,3,0,1,2:T(8,128)} %copy-done.5) | copy-start | bytes 589828
  118.6 7.4 %copy-start.14 = (f32[2]{0:T(128)S(1)}, f32[2]{0:T(128)}, u32[]{:S(2)}) copy-start(f32[2]{0:T(128)} %get-tuple-element.71) | copy-start | bytes 28
  118.6 7.4 %copy-start.15 = (f32[2]{0:T(128)S(1)}, f32[2]{0:T(128)}, u32[]{:S(2)}) copy-start(f32[2]{0:T(128)} %get-tuple-element.72) | copy-start | bytes 28
  118.8 7.2 %collective-permute-start.6 = (f32[2,3,1,64,128]{4,3,0,1,2:T(8,128)S(1)}, f32[2,3,1,64,128]{4,3,0,1,2:T(8,128)S(1)}, u32[]{:S(2)}, u32[]{:S(2)}) collective-permute-start(f32[2,3,1,64,128]{4,3,0,1,2:T(8,128)S(1)} %fusion.27), channel_id=1, source_target_pairs={{0,4},{4,8},{8,12},{12,16},{16,20},{20,24},{24,28},{1,5},{5,9},{9,... | collective-permute-start | bytes 589832 | tf_op jit(solution)/shard_map/ppermute | solution.py:24
  127.0 8.0 %collective-permute-start.7 = (f32[2,3,1,64,128]{4,3,0,1,2:T(8,128)S(1)}, f32[2,3,1,64,128]{4,3,0,1,2:T(8,128)S(1)}, u32[]{:S(2)}, u32[]{:S(2)}) collective-permute-start(f32[2,3,1,64,128]{4,3,0,1,2:T(8,128)S(1)} %get-tuple-element.23), channel_id=1, source_target_pairs={{4,0},{8,4},{12,8},{16,12},{20,16},{24,20},{28,24},{5,1},{9,5},{13... | collective-permute-start | bytes 589832 | tf_op jit(solution)/shard_map/ppermute | solution.py:24
  139.2 10.3 %copy-start.2 = (f32[2,3,1,64,128]{4,3,2,1,0:T(8,128)S(1)}, f32[2,3,1,64,128]{4,3,2,1,0:T(8,128)}, u32[]{:S(2)}) copy-start(f32[2,3,1,64,128]{4,3,2,1,0:T(8,128)} %param.7) | copy-start | bytes 589828
  139.2 10.3 %copy-start.4 = (f32[2,3,1,64,128]{4,3,0,1,2:T(8,128)S(1)}, f32[2,3,1,64,128]{4,3,0,1,2:T(8,128)}, u32[]{:S(2)}) copy-start(f32[2,3,1,64,128]{4,3,0,1,2:T(8,128)} %get-tuple-element.27) | copy-start | bytes 589828
  139.2 10.3 %copy-start.9 = (f32[2,3,1,64,128]{4,3,0,1,2:T(8,128)S(1)}, f32[2,3,1,64,128]{4,3,0,1,2:T(8,128)}, u32[]{:S(2)}) copy-start(f32[2,3,1,64,128]{4,3,0,1,2:T(8,128)} %get-tuple-element.24) | copy-start | bytes 589828
  139.4 10.0 %collective-permute-start.8 = (f32[2,3,1,64,128]{4,3,0,1,2:T(8,128)S(1)}, f32[2,3,1,64,128]{4,3,0,1,2:T(8,128)}, u32[]{:S(2)}, u32[]{:S(2)}) collective-permute-start(f32[2,3,1,64,128]{4,3,0,1,2:T(8,128)S(1)} %fusion.14), channel_id=1, source_target_pairs={{0,4},{4,8},{8,12},{12,16},{16,20},{20,24},{24,28},{1,5},{5,9},{9,... | collective-permute-start | bytes 589832 | tf_op jit(solution)/shard_map/ppermute | solution.py:24
  146.0 28.8 %all-to-all-start.2 = ((f32[1,8,1024]{2,0,1:T(1,128)}), f32[1,8,1024]{2,0,1:T(1,128)S(1)}, u32[]{:S(2)}, u32[]{:S(2)}) async-start(f32[1,8,1024]{2,0,1:T(1,128)} %bitcast.114), calls=%async_computation.2 | async-start | bytes 65536 | tf_op jit(solution)/shard_map/all_to_all | solution.py:128
  151.5 7.6 %collective-permute-start.9 = (f32[2,3,1,64,128]{4,3,0,1,2:T(8,128)S(1)}, f32[2,3,1,64,128]{4,3,0,1,2:T(8,128)S(1)}, u32[]{:S(2)}, u32[]{:S(2)}) collective-permute-start(f32[2,3,1,64,128]{4,3,0,1,2:T(8,128)S(1)} %get-tuple-element.15), channel_id=1, source_target_pairs={{4,0},{8,4},{12,8},{16,12},{20,16},{24,20},{28,24},{5,1},{9,5},{13... | collective-permute-start | bytes 589832 | tf_op jit(solution)/shard_map/ppermute | solution.py:24
  160.3 13.4 %copy-start.8 = (s32[1,64,128]{2,1,0:T(8,128)S(1)}, s32[1,64,128]{2,1,0:T(8,128)}, u32[]{:S(2)}) copy-start(s32[1,64,128]{2,1,0:T(8,128)} %param.9) | copy-start | bytes 98308
  160.3 67.1 %copy-start.10 = (f32[2,3,1,64,128]{4,3,0,1,2:T(8,128)S(1)}, f32[2,3,1,64,128]{4,3,0,1,2:T(8,128)}, u32[]{:S(2)}) copy-start(f32[2,3,1,64,128]{4,3,0,1,2:T(8,128)} %get-tuple-element.16) | copy-start | bytes 589828
  174.8 12.6 %all-to-all-start = ((f32[1,8,1024]{2,0,1:T(1,128)}), f32[1,8,1024]{2,0,1:T(1,128)S(1)}, u32[]{:S(2)}, u32[]{:S(2)}) async-start(f32[1,8,1024]{2,0,1:T(1,128)} %bitcast.111), calls=%async_computation | async-start | bytes 65536 | tf_op jit(solution)/shard_map/all_to_all | solution.py:127
  187.4 10.0 %all-to-all-start.3 = ((f32[8,1,1024]{2,1,0:T(1,128)}), f32[8,1,1024]{2,1,0:T(1,128)S(1)}, u32[]{:S(2)}, u32[]{:S(2)}) async-start(f32[8,1,1024]{2,1,0:T(1,128)} %copy.139), calls=%async_computation.3 | async-start | bytes 65536 | tf_op jit(solution)/shard_map/all_to_all | solution.py:134
where the time goes:
time: 250 us; the launch traced here: 249 us
  blocking collectives  77.2 us (31%)
  waiting for transfers between devices  53.4 us (21%)
  starting transfers between devices  42.7 us (17%)
  other arithmetic  37.9 us (15%)
  local copies, waits for them, and re-layouts  18.6 us (7%)
  matrix products  14.9 us (6%)
  between operations  4.56 us (2%)
    ppermute x10, waiting for transfers between devices, passed_along(): lax.ppermute(value, axis, [(source, source + steps) for source in range(l...  41.1 us
    unnamed x9, other arithmetic  31.4 us
    ppermute x10, starting transfers between devices, passed_along(): lax.ppermute(value, axis, [(source, source + steps) for source in range(l...  30.1 us
    psum x1, blocking collectives, shards(): lax.psum((jnp.sum(precond * applied, axis=(1, 2, 3, 4)), jnp.sum(precond...  20.3 us
    psum x1, blocking collectives, shards(): lax.psum(vol_part, 'slab')  19.1 us
    psum x1, blocking collectives, shards(): lax.psum(stat_pair, 'slab')  18.4 us
    psum x1, blocking collectives, shards(): energy_sum = lax.psum(energy_here, 'load')  10.3 us
    unnamed x91, local copies, waits for them, and re-layouts  9.39 us
  transfers between devices with their start and end apart: 13, of which 10 were waited for; matrix products, arithmetic and copies ran while one was open for 19% of the time, Pallas kernels for 0%

commit v1 on v0

v1 whole, which is shorter than its diff:
```python
import functools

import jax
import jax.numpy as jnp
import numpy as np
from jax import lax
from jax.experimental import pallas as pl
from jax.experimental.pallas import tpu as pltpu
from jax.sharding import PartitionSpec as P

RADIUS = 2
POISSON = 0.3
STIFF_VOID = 0.001
UPPER_FACTOR = 1.2
LOWER_RATIO = 0.1
MOVE_LIMIT = 0.2
VOLUME_TARGET = 0.5
EPSILON = 1e-06
HIGHEST = lax.Precision.HIGHEST
F32 = jnp.float32

HALO_LOW = 4
HALO_HIGH = 5
HALO = HALO_LOW + HALO_HIGH
VMEM_LIMIT = 24 * 1024 * 1024
UNROLL = 4


def hex_stiffness():
    lame_first = POISSON / ((1 + POISSON) * (1 - 2 * POISSON))
    lame_shear = 1 / (2 * (1 + POISSON))
    elastic = np.zeros((6, 6))
    elastic[:3, :3] = lame_first
    for axis_a in range(3):
        elastic[axis_a, axis_a] += 2 * lame_shear
        elastic[3 + axis_a, 3 + axis_a] = lame_shear
    shear_pairs = ((0, 1), (1, 2), (0, 2))
    gauss_point = 1 / np.sqrt(3)
    matrix = np.zeros((24, 24))
    for quad_index in range(8):
        quad_coords = [
            gauss_point * (2 * (quad_index >> 2 - axis_a & 1) - 1) for axis_a in range(3)
        ]
        shape_grads = np.zeros((8, 3))
        for corner in range(8):
            corner_signs = [2 * (corner >> 2 - axis_a & 1) - 1 for axis_a in range(3)]
            for axis_a in range(3):
                deriv_value = float(corner_signs[axis_a])
                for axis_b in range(3):
                    if axis_b != axis_a:
                        deriv_value *= (1 + corner_signs[axis_b] * quad_coords[axis_b]) / 2
                shape_grads[corner, axis_a] = deriv_value
        strain = np.zeros((6, 24))
        for corner in range(8):
            for axis_a in range(3):
                strain[axis_a, 3 * corner + axis_a] = shape_grads[corner, axis_a]
            for pair_index, shear_pair in enumerate(shear_pairs):
                strain[3 + pair_index, 3 * corner + shear_pair[0]] = shape_grads[
                    corner, shear_pair[1]
                ]
                strain[3 + pair_index, 3 * corner + shear_pair[1]] = shape_grads[
                    corner, shear_pair[0]
                ]
        matrix += strain.T @ elastic @ strain / 8
    return matrix.astype(np.float32)


def mode_stiffness():
    signs = np.zeros((8, 8))
    for mode in range(8):
        for corner in range(8):
            flips = bin(mode & ~corner & 7).count("1")
            signs[mode, corner] = -1.0 if flips & 1 else 1.0
    spread = np.kron(signs, np.eye(3))
    return spread @ hex_stiffness().astype(np.float64) @ spread.T / 64


MODES = mode_stiffness()
DIAG_ENTRY = float(hex_stiffness()[0, 0])


def entry(mode_a, comp_a, mode_b, comp_b):
    return float(MODES[3 * mode_a + comp_a, 3 * mode_b + comp_b])


NORMAL = ((4, 0), (2, 1), (1, 2))
SHEAR = (((2, 0), (4, 1)), ((1, 0), (4, 2)), ((1, 1), (2, 2)))
TWIST = ((3, 0), (5, 1), (6, 2))
BEND = (((3, 1), (5, 0)), ((3, 2), (6, 0)), ((5, 2), (6, 1)))
WARP = ((7, 0), (7, 1), (7, 2))
NORMAL_ON = entry(4, 0, 4, 0)
NORMAL_OFF = entry(4, 0, 2, 1)
SHEAR_ON = entry(2, 0, 4, 1)
TWIST_ON = entry(3, 0, 3, 0)
TWIST_OFF = entry(3, 0, 5, 1)
BEND_ON = entry(3, 1, 3, 1)
BEND_OFF = entry(3, 1, 5, 0)
WARP_ON = entry(7, 0, 7, 0)


def smoother_factors():
    sigma = (1 + LOWER_RATIO) / (1 - LOWER_RATIO)
    factor = 1 / sigma
    residual = np.array([1.0, 0.0, 0.0, 0.0])
    update = np.array([1.0, 0.0, 0.0, 0.0])
    total = np.zeros(4)
    for sweep in range(4):
        total = total + update
        if sweep < 3:
            residual = residual - np.concatenate([[0.0], update[:3]])
            factor_next = 1 / (2 * sigma - factor)
            update = factor_next * factor * update + 2 * factor_next * sigma * residual
            factor = factor_next
    return [float(value) for value in total]


def iota(shape, axis):
    return lax.broadcasted_iota(jnp.int32, shape, axis)


def gauss(offsets):
    return jnp.exp(-((offsets.astype(F32) / RADIUS) ** 2))


def gauss_table(count):
    return gauss(iota((count, count), 0) - iota((count, count), 1))


def shifts(shape):
    inner = {}
    for axis in (0, 1):
        index = iota(shape, axis)
        inner[axis] = (index < shape[axis] - 1, index > 0)

    def above(value, axis):
        moved = pltpu.roll(value, shape[axis] - 1, axis)
        return jnp.where(inner[axis][0], moved, 0.0)

    def below(value, axis):
        moved = pltpu.roll(value, 1, axis)
        return jnp.where(inner[axis][1], moved, 0.0)

    return above, below


def row_modes(values, above):
    modes = {}
    for comp, value in enumerate(values):
        ahead = above(value, 0)
        for bit, part in ((0, value + ahead), (4, ahead - value)):
            beside = above(part, 1)
            modes[bit, comp] = part + beside
            modes[bit + 1, comp] = beside - part
    return modes


def element_modes(low, high):
    modes = {}
    for (bits, comp), value in low.items():
        other = high[bits, comp]
        if bits:
            modes[bits, comp] = value + other
        modes[bits + 2, comp] = other - value
    return modes


def element_forces(modes, scale):
    forces = {}
    total = modes[NORMAL[0]] + modes[NORMAL[1]] + modes[NORMAL[2]]
    shared = (scale * NORMAL_OFF) * total
    own = scale * (NORMAL_ON - NORMAL_OFF)
    for key in NORMAL:
        forces[key] = shared + own * modes[key]
    shear = scale * SHEAR_ON
    for key_a, key_b in SHEAR:
        forces[key_a] = forces[key_b] = shear * (modes[key_a] + modes[key_b])
    total = modes[TWIST[0]] + modes[TWIST[1]] + modes[TWIST[2]]
    shared = (scale * TWIST_OFF) * total
    own = scale * (TWIST_ON - TWIST_OFF)
    for key in TWIST:
        forces[key] = shared + own * modes[key]
    bend_on = scale * BEND_ON
    bend_off = scale * BEND_OFF
    for key_a, key_b in BEND:
        forces[key_a] = bend_on * modes[key_a] + bend_off * modes[key_b]
        forces[key_b] = bend_on * modes[key_b] + bend_off * modes[key_a]
    warp = scale * WARP_ON
    for key in WARP:
        forces[key] = warp * modes[key]
    return forces


def element_energy(modes):
    total = modes[NORMAL[0]] + modes[NORMAL[1]] + modes[NORMAL[2]]
    squares = sum(modes[key] * modes[key] for key in NORMAL)
    energy = NORMAL_OFF * (total * total) + (NORMAL_ON - NORMAL_OFF) * squares
    shear = 0.0
    for key_a, key_b in SHEAR:
        both = modes[key_a] + modes[key_b]
        shear = shear + both * both
    energy = energy + SHEAR_ON * shear
    total = modes[TWIST[0]] + modes[TWIST[1]] + modes[TWIST[2]]
    squares = sum(modes[key] * modes[key] for key in TWIST)
    energy = energy + TWIST_OFF * (total * total) + (TWIST_ON - TWIST_OFF) * squares
    squares = sum(modes[key] * modes[key] for pair in BEND for key in pair)
    crossed = sum(modes[key_a] * modes[key_b] for key_a, key_b in BEND)
    energy = energy + BEND_ON * squares + (2 * BEND_OFF) * crossed
    squares = sum(modes[key] * modes[key] for key in WARP)
    return energy + WARP_ON * squares


ROW_KEYS = [(bits, comp) for comp in range(3) for bits in (0, 1, 4, 5)]


def split_forces(forces):
    here, there = {}, {}
    for bits, comp in ROW_KEYS:
        change = forces[bits + 2, comp]
        if bits:
            common = forces[bits, comp]
            here[bits, comp] = common - change
            there[bits, comp] = common + change
        else:
            here[bits, comp] = -change
            there[bits, comp] = change
    return here, there


def node_forces(modes, below):
    values = []
    for comp in range(3):
        parts = []
        for bit in (0, 4):
            common, change = modes[bit, comp], modes[bit + 1, comp]
            parts.append((common - change) + below(common + change, 1))
        values.append((parts[0] - parts[1]) + below(parts[0] + parts[1], 0))
    return values


def apply_rows(first, last, load_row, scale_row, emit, above, below, carry=None):
    def advance(index, low, pending):
        high = row_modes(load_row(index + 1), above)
        forces = element_forces(element_modes(low, high), scale_row(index))
        here, there = split_forces(forces)
        return high, {key: pending[key] + here[key] for key in ROW_KEYS}, there

    def pack(low, pending):
        return tuple(low[key] for key in ROW_KEYS) + tuple(pending[key] for key in ROW_KEYS)

    def unpack(state):
        count = len(ROW_KEYS)
        return dict(zip(ROW_KEYS, state[:count])), dict(zip(ROW_KEYS, state[count:]))

    low = row_modes(load_row(first), above)
    zero = {key: jnp.zeros_like(low[key]) for key in ROW_KEYS}
    low, _, pending = advance(first, low, zero)

    def step(index, state):
        carried, (low, pending) = state[0], unpack(state[1])
        low, modes, pending = advance(index, low, pending)
        carried = emit(index, node_forces(modes, below), carried)
        return carried, pack(low, pending)

    carried, _ = lax.fori_loop(
        first + 1, last, step, (carry, pack(low, pending)), unroll=UNROLL
    )
    return carried


def own_table(count):
    return gauss_table(count)


def call(body, outs, *args, scratch=(), name=None, flops=0):
    return pl.pallas_call(
        body,
        out_shape=outs,
        in_specs=[pl.BlockSpec(memory_space=pltpu.VMEM)] * len(args),
        out_specs=jax.tree.map(lambda _: pl.BlockSpec(memory_space=pltpu.VMEM), outs),
        scratch_shapes=list(scratch),
        compiler_params=pltpu.CompilerParams(vmem_limit_bytes=VMEM_LIMIT),
        cost_estimate=pl.CostEstimate(flops=flops, bytes_accessed=1 << 20, transcendentals=0),
        name=name,
    )(*args)


def exchange(message, axes, pieces):
    rows = message.shape[0]
    return lax.all_to_all(
        message.reshape(rows, 1, message.shape[1]), axes, split_axis=0, concat_axis=0, tiled=True
    ).reshape(message.shape)


def shards(start_disp, density, design, support, load_nodes, load_forces):
    slabs = lax.axis_size("slab")
    parts = lax.axis_size("load")
    loads, comps, layers, rows_x, cols_y = start_disp.shape
    points = load_nodes.shape[1]
    depth = slabs * layers
    strip = rows_x // slabs
    span = strip + HALO
    fields = loads * comps
    plane = (depth, cols_y)
    in_rows = (fields + 2) * span + rows_x
    sum_rows = 1 + strip
    out_rows = 1 + fields * strip
    row_block = lambda count: jax.ShapeDtypeStruct((count, span) + plane, F32)
    flat = lambda rows: jax.ShapeDtypeStruct((rows, cols_y), F32)
    smoother = smoother_factors()

    def pack_body(disp_ref, dens_ref, design_ref, support_ref, out_ref, pad_ref):
        solid = design_ref[0].astype(F32) * dens_ref[0]
        planes = [
            (disp_ref[load, comp, 0], 0.0) for load in range(loads) for comp in range(comps)
        ]
        planes += [(solid * solid * solid, -1.0), (support_ref[0].astype(F32), 1.0)]
        for field, (value, fill) in enumerate(planes):
            pad_ref[field, 0:HALO_LOW] = jnp.full((HALO_LOW, cols_y), fill, F32)
            pad_ref[field, HALO_LOW : HALO_LOW + rows_x] = value
            pad_ref[field, HALO_LOW + rows_x : HALO + rows_x] = jnp.full(
                (HALO_HIGH, cols_y), fill, F32
            )
        for target in range(slabs):
            base = target * in_rows
            for field in range(fields + 2):
                out_ref[base + field * span : base + (field + 1) * span] = pad_ref[
                    field, target * strip : target * strip + span
                ]
            out_ref[base + (fields + 2) * span : base + in_rows] = dens_ref[0]

    message = call(
        pack_body,
        flat(slabs * in_rows),
        start_disp,
        density,
        design,
        support,
        scratch=[pltpu.VMEM((fields + 2, rows_x + 2 * 8, cols_y), F32)],
        name="pack",
    )
    received = exchange(message, "slab", slabs)

    cells = -(-span * depth // 16) * 16
    chunk = min(256, points)

    def loads_body(nodes_ref, forces_ref, out_ref):
        first = lax.axis_index("slab") * strip - HALO_LOW
        out_ref[...] = jnp.zeros_like(out_ref)
        for load in range(loads):
            for start in range(0, points, chunk):
                part = slice(start, start + chunk)
                node = nodes_ref[load : load + 1, part]
                column = node % cols_y
                row = (node // cols_y) % rows_x - first
                layer = node // (cols_y * rows_x)
                cell = jnp.where((row >= 0) & (row < span), row * depth + layer, -1)
                hit = iota((cells, chunk), 0) == cell
                spot = (iota((cols_y, chunk), 0) == column).astype(F32).astype(jnp.bfloat16)
                for comp in range(comps):
                    rest = forces_ref[load, comp : comp + 1, part]
                    for piece in range(3):
                        rounded = rest.astype(jnp.bfloat16).astype(F32)
                        rest = rest - rounded
                        picked = jnp.where(hit, rounded, 0.0).astype(jnp.bfloat16)
                        out_ref[load * comps + comp] += lax.dot_general(
                            picked, spot, (((1,), (1,)), ((), ())), preferred_element_type=F32
                        )

    right_side = call(
        loads_body,
        jax.ShapeDtypeStruct((fields, cells, cols_y), F32),
        load_nodes,
        load_forces,
        name="point_loads",
        flops=1 << 28,
    )

    def residual_body(
        in_ref, rhs_ref, design_ref, disp_ref, cube_ref, geo_ref, zero_ref, one_ref, dens_ref, sum_ref
    ):
        above, below = shifts(plane)
        for row in range(span):
            pick = lambda field: in_ref[pl.ds(field * span + row, depth, stride=in_rows), :]
            for field in range(fields):
                disp_ref[field, row] = pick(field)
            cube = pick(fields)
            cube_ref[0, row] = cube
            geo_ref[0, row] = jnp.where(
                cube < 0.0, 0.0, STIFF_VOID + (1.0 - STIFF_VOID) * cube
            )
            geo_ref[1, row] = 1.0 - pick(fields + 1)
        diags = {}
        for row in range(1, span - 1):
            beside = geo_ref[0, row] + geo_ref[0, row - 1]
            beside = beside + below(beside, 0)
            beside = beside + below(beside, 1)
            free = geo_ref[1, row]
            geo_ref[2, row] = 1.0 / (free * DIAG_ENTRY * beside + (1.0 - free))

        scale_row = lambda row: geo_ref[0, row]
        lane = iota((1, cols_y), 1)
        sums = jnp.zeros((1, cols_y), F32)
        whole = lambda value: jnp.sum(jnp.sum(value, 0, keepdims=True), 1, keepdims=True)

        for load in range(loads):
            keys = range(load * comps, (load + 1) * comps)

            def start_row(row):
                free = geo_ref[1, row]
                return [free * disp_ref[key, row] for key in keys]

            def emit_residual(row, forces, carried):
                free, inverse = geo_ref[1, row], geo_ref[2, row]
                total = jnp.zeros(plane, F32)
                for key, force in zip(keys, forces):
                    load_row = rhs_ref[key, pl.ds(pl.multiple_of(row * depth, depth), depth), :]
                    rest = free * (load_row - force) - (1.0 - free) * disp_ref[key, row]
                    value = rest * inverse
                    zero_ref[key, row] = value
                    total = total + value * rest
                own = (row >= HALO_LOW) & (row < HALO_LOW + strip)
                return carried + jnp.where(own, total, 0.0)

            weight = apply_rows(
                0, span - 1, start_row, scale_row, emit_residual, above, below,
                jnp.zeros(plane, F32),
            )

            def zero_row(row):
                free = geo_ref[1, row]
                return [free * zero_ref[key, row] for key in keys]

            def emit_one(row, forces, carried):
                free, inverse = geo_ref[1, row], geo_ref[2, row]
                total = jnp.zeros(plane, F32)
                for key, force in zip(keys, forces):
                    value = zero_ref[key, row]
                    applied = free * force + (1.0 - free) * value
                    one_ref[key, row] = applied * inverse
                    total = total + value * applied
                own = (row >= HALO_LOW) & (row < HALO_LOW + strip)
                return carried + jnp.where(own, total, 0.0)

            curve = apply_rows(
                1, span - 2, zero_row, scale_row, emit_one, above, below, jnp.zeros(plane, F32)
            )
            sums = jnp.where(lane == 2 * load, whole(curve), sums)
            sums = jnp.where(lane == 2 * load + 1, whole(weight), sums)

        here = lax.axis_index("slab")
        mixed = jnp.zeros((rows_x, cols_y), F32)
        for layer in range(depth):
            weight = gauss(jnp.full((1, cols_y), here - layer, jnp.int32))
            base = layer * in_rows + (fields + 2) * span
            mixed = mixed + weight * in_ref[base : base + rows_x]
        table_x = gauss_table(rows_x)
        mixed = jnp.dot(table_x, mixed, precision=HIGHEST, preferred_element_type=F32)
        filtered = jnp.dot(
            mixed, gauss_table(cols_y), precision=HIGHEST, preferred_element_type=F32
        )
        dens_ref[...] = filtered
        mask = design_ref[0].astype(F32)
        sums = jnp.where(lane == 2 * loads, whole(mask), sums)
        share = jnp.dot(
            table_x, mask / filtered, precision=HIGHEST, preferred_element_type=F32
        )
        for target in range(slabs):
            base = target * sum_rows
            sum_ref[base : base + 1] = sums
            sum_ref[base + 1 : base + sum_rows] = share[target * strip : (target + 1) * strip]

    disp, cube, geometry, zeroth, first, dens_filtered, sums = call(
        residual_body,
        (
            row_block(fields),
            row_block(1),
            row_block(3),
            row_block(fields),
            row_block(fields),
            flat(rows_x),
            flat(slabs * sum_rows),
        ),
        received,
        right_side,
        design,
        name="residual",
        flops=1 << 26,
    )
    all_sums = exchange(sums, "slab", slabs)

    def powers_body(geo_ref, one_ref, two_ref, three_ref):
        above, below = shifts(plane)
        scale_row = lambda row: geo_ref[0, row]
        for load in range(loads):
            keys = range(load * comps, (load + 1) * comps)
            for source, target, edge in ((one_ref, two_ref, 2), (two_ref, three_ref, 3)):

                def load_row(row):
                    free = geo_ref[1, row]
                    return [free * source[key, row] for key in keys]

                def emit(row, forces, carried):
                    free, inverse = geo_ref[1, row], geo_ref[2, row]
                    for key, force in zip(keys, forces):
                        target[key, row] = (
                            free * force + (1.0 - free) * source[key, row]
                        ) * inverse
                    return carried

                apply_rows(
                    edge, span - 1 - edge, load_row, scale_row, emit, above, below,
                    jnp.zeros((1, 1), F32),
                )

    second, third = call(
        powers_body,
        (row_block(fields), row_block(fields)),
        geometry,
        first,
        name="powers",
        flops=1 << 26,
    )

    def energy_body(
        sums_ref, disp_ref, cube_ref, geo_ref, zero_ref, one_ref, two_ref, three_ref,
        disp_out_ref, numer_ref, count_ref, weak_ref,
    ):
        above, below = shifts(plane)
        lane = iota((1, cols_y), 1)
        sums = jnp.zeros((1, cols_y), F32)
        for layer in range(slabs):
            sums = sums + sums_ref[layer * sum_rows : layer * sum_rows + 1]
        take = lambda index: jnp.sum(jnp.where(lane == index, sums, 0.0), 1, keepdims=True)
        count_ref[...] = jnp.broadcast_to(take(2 * loads), (8, cols_y))
        inverses = []
        for load in range(loads):
            upper = UPPER_FACTOR * take(2 * load) / take(2 * load + 1)
            inverses.append(
                jnp.broadcast_to(1.0 / (0.5 * (upper + LOWER_RATIO * upper)), plane)
            )
        lower = [None] * loads
        for row in range(HALO_LOW, HALO_LOW + strip + 1):
            free = geo_ref[1, row]
            energy = 0.0
            for load in range(loads):
                inverse = inverses[load]
                values = []
                for comp in range(comps):
                    key = load * comps + comp
                    value = smoother[3] * three_ref[key, row]
                    value = smoother[2] * two_ref[key, row] + inverse * value
                    value = smoother[1] * one_ref[key, row] + inverse * value
                    value = smoother[0] * zero_ref[key, row] + inverse * value
                    value = disp_ref[key, row] + inverse * value
                    if row < HALO_LOW + strip:
                        place = key * strip + row - HALO_LOW
                        disp_out_ref[pl.ds(place, depth, stride=out_rows), :] = value
                    values.append(free * value)
                modes = row_modes(values, above)
                if lower[load] is not None:
                    energy = energy + element_energy(element_modes(lower[load], modes))
                lower[load] = modes
            if row > HALO_LOW:
                weak_ref[(row - 1 - HALO_LOW) * depth : (row - HALO_LOW) * depth] = (
                    (3.0 * (1.0 - STIFF_VOID)) * cube_ref[0, row - 1] * energy
                )
        disp_out_ref[pl.ds(out_rows - 1, depth, stride=out_rows), :] = jnp.zeros(plane, F32)
        size = strip * depth
        across = jnp.dot(
            weak_ref[...], gauss_table(cols_y), precision=HIGHEST, preferred_element_type=F32
        )
        to, source = iota((size, size), 0), iota((size, size), 1)
        table = jnp.where(
            to % strip == source // depth, gauss(to // strip - source % depth), 0.0
        )
        smooth = jnp.dot(table, across, precision=HIGHEST, preferred_element_type=F32)
        weighted = jnp.zeros((1, cols_y), F32)
        for layer in range(depth):
            piece = smooth[layer * strip : (layer + 1) * strip]
            base = layer * sum_rows
            weighted = weighted + jnp.sum(
                piece * sums_ref[base + 1 : base + sum_rows], 0, keepdims=True
            )
        for layer in range(depth):
            piece = smooth[layer * strip : (layer + 1) * strip]
            for part in range(parts):
                base = (part * slabs + layer) * sum_rows
                numer_ref[base : base + strip] = piece
                numer_ref[base + strip : base + sum_rows] = weighted

    disp_message, numer_message, count = call(
        energy_body,
        (flat(slabs * out_rows), flat(parts * slabs * sum_rows), flat(8)),
        all_sums,
        disp,
        cube,
        geometry,
        zeroth,
        first,
        second,
        third,
        scratch=[pltpu.VMEM((strip * depth, cols_y), F32)],
        name="energy",
        flops=1 << 24,
    )
    numer_pieces = exchange(numer_message, ("load", "slab"), parts * slabs)

    def trial_body(
        numer_ref, dens_ref, filtered_ref, design_ref, count_ref, disp_ref, trial_ref, out_ref, plane_ref
    ):
        weighted_row = jnp.zeros((1, cols_y), F32)
        for source in range(slabs):
            total = jnp.zeros((strip, cols_y), F32)
            for part in range(parts):
                base = (part * slabs + source) * sum_rows
                total = total + numer_ref[base : base + strip]
                weighted_row = weighted_row + numer_ref[base + strip : base + sum_rows]
            plane_ref[source * strip : (source + 1) * strip] = total
        weighted_total = jnp.sum(weighted_row, 1, keepdims=True)
        mean = weighted_total / count_ref[0:1] + EPSILON
        numer = jnp.dot(
            gauss_table(rows_x), plane_ref[...], precision=HIGHEST, preferred_element_type=F32
        )
        mask = design_ref[0].astype(F32)
        dens = dens_ref[0]
        ratio = mask * (numer / filtered_ref[...]) / mean
        trial = jnp.clip(dens * jnp.sqrt(ratio), dens - MOVE_LIMIT, dens + MOVE_LIMIT)
        trial_ref[...] = trial
        out_ref[...] = disp_ref[...]
        volume = jnp.sum(mask * trial, 0, keepdims=True)
        for target in range(slabs):
            base = (target + 1) * out_rows - 1
            out_ref[base : base + 1] = volume

    trial, out_message = call(
        trial_body,
        (flat(rows_x), flat(slabs * out_rows)),
        numer_pieces,
        density,
        dens_filtered,
        design,
        count,
        disp_message,
        scratch=[pltpu.VMEM((rows_x, cols_y), F32)],
        name="trial",
    )
    out_pieces = exchange(out_message, "slab", slabs)

    def final_body(pieces_ref, trial_ref, design_ref, count_ref, disp_ref, dens_ref):
        volume = jnp.zeros((1, cols_y), F32)
        for source in range(slabs):
            base = (source + 1) * out_rows
            volume = volume + pieces_ref[base - 1 : base]
        volume = jnp.sum(volume, 1, keepdims=True)
        scale = VOLUME_TARGET / (volume / count_ref[0:1] + EPSILON)
        mask = design_ref[0].astype(F32)
        dens_ref[0] = mask * jnp.minimum(scale * trial_ref[...], 1.0)
        for source in range(slabs):
            rows = slice(source * strip, (source + 1) * strip)
            for key in range(fields):
                base = source * out_rows + key * strip
                disp_ref[key // comps, key % comps, 0, rows] = pieces_ref[base : base + strip]

    return call(
        final_body,
        (
            jax.ShapeDtypeStruct(start_disp.shape, F32),
            jax.ShapeDtypeStruct(density.shape, F32),
        ),
        out_pieces,
        trial,
        design,
        count,
        name="final",
    )


def solution(mesh):
    return jax.shard_map(
        shards,
        mesh=mesh,
        in_specs=(
            P("load", None, "slab", None, None),
            P("slab", None, None),
            P("slab", None, None),
            P("slab", None, None),
            P("load", None),
            P("load", None, None),
        ),
        out_specs=(P("load", None, "slab", None, None), P("slab", None, None)),
        check_vma=False,
    )
```

time: 250 us -> 73.5 us (0.29)
  blocking collectives: 77.2 us -> 21.9 us
  other arithmetic: 37.9 us -> 0 us
  waiting for transfers between devices: 53.4 us -> 20.4 us
  starting transfers between devices: 42.7 us -> 10.9 us
  matrix products: 14.9 us -> 0 us
  Pallas kernels: 0 us -> 14.8 us
  local copies, waits for them, and re-layouts: 18.6 us -> 3.91 us
  between operations: 4.56 us -> 0.7 us
    psum x4 -> x0, blocking collectives: 68.1 us -> none  [the longest x1 20.3 us: shards(): lax.psum((jnp.sum(precond * applied, axis=(1, 2, 3, 4)), jnp.sum(precond...]
    ppermute x10 -> x0, waiting for transfers between devices: 41.1 us -> none  [passed_along(): lax.ppermute(value, axis, [(source, source + steps) for source in range(l...]
    unnamed x9 -> x0, other arithmetic: 31.4 us -> none
    ppermute x10 -> x0, starting transfers between devices: 30.1 us -> none  [passed_along(): lax.ppermute(value, axis, [(source, source + steps) for source in range(l...]
    dot_general x11 -> x0, matrix products: 14.9 us -> none  [the longest x4 9.39 us: layer_forces(): jnp.einsum('ab,lbn->lan', kmatrix, corner_vals, precision=HIGHEST)]
    pallas_call x0 -> x7, Pallas kernels: none -> 14.8 us  [call(): pl.pallas_call(body, out_shape=outs, in_specs=[pl.BlockSpec(memory_space=...]
    all_to_all x1 -> x2, blocking collectives: 9.05 us -> 21.9 us  [exchange(): lax.all_to_all(message.reshape(rows, 1, message.shape[1]), axes, split_ax...]
    all_to_all x3 -> x2, waiting for transfers between devices: 12.3 us -> 20.4 us  [exchange(): lax.all_to_all(message.reshape(rows, 1, message.shape[1]), axes, split_ax...]
  transfers between devices with their start and end apart: 13 -> 2, of which waited for: 10 -> 2; matrix products, arithmetic and copies ran while one was open for 19% -> 0% of each run, Pallas kernels for 0% -> 9%
where the time goes in v1:
time: 73.5 us; the launch traced here: 72.8 us
  blocking collectives  21.9 us (30%)
  waiting for transfers between devices  20.4 us (28%)
  Pallas kernels  14.8 us (20%)
  starting transfers between devices  10.9 us (15%)
  local copies, waits for them, and re-layouts  3.91 us (5%)
    all_to_all x2, blocking collectives, exchange(): lax.all_to_all(message.reshape(rows, 1, message.shape[1]), axes, split_ax...  21.9 us
    all_to_all x2, waiting for transfers between devices, exchange(): lax.all_to_all(message.reshape(rows, 1, message.shape[1]), axes, split_ax...  20.4 us
    pallas_call x7, Pallas kernels, call(): pl.pallas_call(body, out_shape=outs, in_specs=[pl.BlockSpec(memory_space=...  14.8 us
    all_to_all x2, starting transfers between devices, exchange(): lax.all_to_all(message.reshape(rows, 1, message.shape[1]), axes, split_ax...  10.9 us
    unnamed x17, local copies, waits for them, and re-layouts  3.91 us
  transfers between devices with their start and end apart: 2, of which 2 were waited for; matrix products, arithmetic and copies ran while one was open for 0% of the time, Pallas kernels for 9%

profile of v1, /device:TPU:0, one launch (start us, length us, event | category | flops | bytes accessed | tf_op | source)
XLA Modules:
  0.0 72.8 jit_solution(52804024352931633)
XLA Ops:
  0.6 0.0 copy-start
  0.6 0.7 %copy-done = s32[1,64,128]{2,1,0:T(8,128)S(1)} copy-done((s32[1,64,128]{2,1,0:T(8,128)S(1)}, s32[1,64,128]{2,1,0:T(8,128)}, u32[]{:S(2)}) %copy-start) | copy-done | bytes 32792
  1.4 0.0 copy-start.2
  1.4 0.9 %copy-done.2 = f32[2,3,1,64,128]{4,3,2,1,0:T(8,128)S(1)} copy-done((f32[2,3,1,64,128]{4,3,2,1,0:T(8,128)S(1)}, f32[2,3,1,64,128]{4,3,2,1,0:T(8,128)}, u32[]{:S(2)}) %copy-start.2) | copy-done | bytes 196632
  2.3 0.0 copy-start.3
  2.3 0.8 %copy-done.3 = f32[1,64,128]{2,1,0:T(8,128)S(1)} copy-done((f32[1,64,128]{2,1,0:T(8,128)S(1)}, f32[1,64,128]{2,1,0:T(8,128)}, u32[]{:S(2)}) %copy-start.3) | copy-done | bytes 32792
  3.1 0.0 copy-start.5
  3.1 0.8 %copy-done.5 = s32[1,64,128]{2,1,0:T(8,128)S(1)} copy-done((s32[1,64,128]{2,1,0:T(8,128)S(1)}, s32[1,64,128]{2,1,0:T(8,128)}, u32[]{:S(2)}) %copy-start.5) | copy-done | bytes 32792
  3.8 1.0 %pack.1 = f32[1600,128]{1,0:T(8,128)} custom-call(f32[2,3,1,64,128]{4,3,2,1,0:T(8,128)S(1)} %copy-done.2, f32[1,64,128]{2,1,0:T(8,128)S(1)} %copy-done.3, s32[1,64,128]{2,1,0:T(8,128)S(1)} %copy-done, s32[1,64,128]{2,1,0:T(8,128)S(1)} %copy-done.5), custom_call_target="tpu_custom_call" | custom-call | bytes 1048576 | tf_op jit(solution)/shard_map/pack/pallas_call | solution.py:275
  4.8 0.0 copy-start.7
  4.8 7.4 %all-to-all-start = ((f32[1600,1,128]{2,1,0:T(1,128)}), f32[1600,1,128]{2,1,0:T(1,128)S(1)}, u32[]{:S(2)}, u32[]{:S(2)}) async-start(f32[1600,1,128]{2,1,0:T(1,128)} %bitcast.1), calls=%async_computation | async-start | bytes 1638400 | tf_op jit(solution)/shard_map/all_to_all | solution.py:289
  12.3 0.0 copy-done.7
  12.3 0.0 copy-start.6
  12.3 0.7 copy-done.6
  13.0 0.0 copy-start.1
  13.0 2.9 %point_loads.1.rhs_ref = f32[6,144,128]{2,1,0:T(8,128)S(1)} custom-call(s32[2,2048]{1,0:T(2,128)S(1)} %copy-done.6, f32[2,3,2048]{2,1,0:T(4,128)S(1)} %copy.10.forces_ref), custom_call_target="tpu_custom_call" | custom-call | flops 268435456 | bytes 1048576 | tf_op jit(solution)/shard_map/point_loads/pallas_call | solution.py:275
  15.9 17.3 %all-to-all-done = f32[1600,1,128]{2,1,0:T(1,128)S(1)} async-done(((f32[1600,1,128]{2,1,0:T(1,128)}), f32[1600,1,128]{2,1,0:T(1,128)S(1)}, u32[]{:S(2)}, u32[]{:S(2)}) %all-to-all-start) | async-done | bytes 819232 | tf_op jit(solution)/shard_map/all_to_all | solution.py:289
  33.2 0.0 copy-done.1
  33.2 5.6 %residual.1 = (f32[6,17,8,128]{3,2,1,0:T(8,128)S(1)}, f32[1,17,8,128]{3,2,1,0:T(8,128)S(1)}, f32[3,17,8,128]{3,2,1,0:T(8,128)S(1)}, f32[6,17,8,128]{3,2,1,0:T(8,...) custom-call(f32[1600,128]{1,0:T(8,128)S(1)} %bitcast.16, ...), custom_call_target="tpu_custom_call" | custom-call | flops 67108864 | bytes 1048576 | tf_op jit(solution)/shard_map/residual/pallas_call | solution.py:275
  38.8 3.5 %all-to-all-start.1 = ((f32[72,1,128]{2,1,0:T(1,128)}), f32[72,1,128]{2,1,0:T(1,128)S(1)}, u32[]{:S(2)}, u32[]{:S(2)}) async-start(f32[72,1,128]{2,1,0:T(1,128)} %bitcast.4), calls=%async_computation.1 | async-start | bytes 73728 | tf_op jit(solution)/shard_map/all_to_all | solution.py:289
  42.3 3.5 %powers.1 = (f32[6,17,8,128]{3,2,1,0:T(8,128)S(1)}, f32[6,17,8,128]{3,2,1,0:T(8,128)S(1)}) custom-call(f32[3,17,8,128]{3,2,1,0:T(8,128)S(1)} %get-tuple-element.19.geo_ref, f32[6,17,8,128]{3,2,1,0:T(8,128)S(1)} %get-tuple-element.21.one_ref), custom_call_target="tpu_custom_call" | custom-call | flops 67108864 | bytes 1048576 | tf_op jit(solution)/shard_map/powers/pallas_call | solution.py:275
  45.9 3.2 %all-to-all-done.1 = f32[72,1,128]{2,1,0:T(1,128)S(1)} async-done(((f32[72,1,128]{2,1,0:T(1,128)}), f32[72,1,128]{2,1,0:T(1,128)S(1)}, u32[]{:S(2)}, u32[]{:S(2)}) %all-to-all-start.1) | async-done | bytes 36896 | tf_op jit(solution)/shard_map/all_to_all | solution.py:289
  49.0 0.8 %energy.1 = (f32[392,128]{1,0:T(8,128)S(1)}, f32[288,128]{1,0:T(8,128)S(1)}, f32[8,128]{1,0:T(8,128)S(1)}) custom-call(f32[72,128]{1,0:T(8,128)S(1)} %bitcast.21, f32[6,17,8,128]{3,2,1,0:T(8,128)S(1)} %get-tuple-element.17.disp_ref, f32[1,17,8,128]{3,2,1,0:T(8,128)S(1)} %get-tuple-element.18.cube_ref, f32[3,17,8,128]{3,2,1,0:T(8,128)S(1)} %get-tuple-element.19.geo_ref, ...), custom_call_target="tpu_custom_call" | custom-call | flops 16777216 | bytes 1048576 | tf_op jit(solution)/shard_map/energy/pallas_call | solution.py:275
  49.9 0.0 copy-start.4
  49.9 10.5 %all_to_all.20 = f32[288,1,128]{2,1,0:T(1,128)S(1)} all-to-all(f32[288,1,128]{2,1,0:T(1,128)S(1)} %bitcast.20), channel_id=1, replica_groups=mesh['slab'=8,'load'=4] {'load','slab'}, dimensions={0} | all-to-all | bytes 294912 | tf_op jit(solution)/shard_map/all_to_all | solution.py:289
  60.4 0.0 copy-done.4
  60.4 0.2 trial.1
  60.6 11.5 %all_to_all.21 = f32[392,1,128]{2,1,0:T(1,128)S(1)} all-to-all(f32[392,1,128]{2,1,0:T(1,128)S(1)} %bitcast.19), channel_id=1, replica_groups=mesh['slab'=8,'load'=4] {'slab'}, dimensions={0} | all-to-all | bytes 401408 | tf_op jit(solution)/shard_map/all_to_all | solution.py:289
  72.1 0.7 final.1
  (1 shorter events, 0.0 us)
Async XLA Ops:
  0.6 0.8 %copy-start = (s32[1,64,128]{2,1,0:T(8,128)S(1)}, s32[1,64,128]{2,1,0:T(8,128)}, u32[]{:S(2)}) copy-start(s32[1,64,128]{2,1,0:T(8,128)} %design_ref.7) | copy-start | bytes 98308
  1.4 0.9 %copy-start.2 = (f32[2,3,1,64,128]{4,3,2,1,0:T(8,128)S(1)}, f32[2,3,1,64,128]{4,3,2,1,0:T(8,128)}, u32[]{:S(2)}) copy-start(f32[2,3,1,64,128]{4,3,2,1,0:T(8,128)} %disp_ref.1) | copy-start | bytes 589828
  2.3 0.8 %copy-start.3 = (f32[1,64,128]{2,1,0:T(8,128)S(1)}, f32[1,64,128]{2,1,0:T(8,128)}, u32[]{:S(2)}) copy-start(f32[1,64,128]{2,1,0:T(8,128)} %dens_ref.3) | copy-start | bytes 98308
  3.1 0.8 %copy-start.5 = (s32[1,64,128]{2,1,0:T(8,128)S(1)}, s32[1,64,128]{2,1,0:T(8,128)}, u32[]{:S(2)}) copy-start(s32[1,64,128]{2,1,0:T(8,128)} %support_ref.1) | copy-start | bytes 98308
  4.8 7.4 %copy-start.7 = (f32[2,3,2048]{2,0,1:T(2,128)S(1)}, f32[2,3,2048]{2,0,1:T(2,128)}, u32[]{:S(2)}) copy-start(f32[2,3,2048]{2,0,1:T(2,128)} %param.11) | copy-start | bytes 147460
  4.8 28.3 %all-to-all-start = ((f32[1600,1,128]{2,1,0:T(1,128)}), f32[1600,1,128]{2,1,0:T(1,128)S(1)}, u32[]{:S(2)}, u32[]{:S(2)}) async-start(f32[1600,1,128]{2,1,0:T(1,128)} %bitcast.1), calls=%async_computation | async-start | bytes 1638400 | tf_op jit(solution)/shard_map/all_to_all | solution.py:289
  12.3 0.7 copy-start.6
  13.0 20.2 %copy-start.1 = (s32[1,64,128]{2,1,0:T(8,128)S(1)}, s32[1,64,128]{2,1,0:T(8,128)}, u32[]{:S(2)}) copy-start(s32[1,64,128]{2,1,0:T(8,128)} %design_ref.7) | copy-start | bytes 98308
  38.8 10.2 %all-to-all-start.1 = ((f32[72,1,128]{2,1,0:T(1,128)}), f32[72,1,128]{2,1,0:T(1,128)S(1)}, u32[]{:S(2)}, u32[]{:S(2)}) async-start(f32[72,1,128]{2,1,0:T(1,128)} %bitcast.4), calls=%async_computation.1 | async-start | bytes 73728 | tf_op jit(solution)/shard_map/all_to_all | solution.py:289
  49.9 10.5 %copy-start.4 = (f32[1,64,128]{2,1,0:T(8,128)S(1)}, f32[1,64,128]{2,1,0:T(8,128)}, u32[]{:S(2)}) copy-start(f32[1,64,128]{2,1,0:T(8,128)} %dens_ref.3) | copy-start | bytes 98308

commit v2 on v1

v2 whole, which is shorter than its diff:
```python
import functools

import jax
import jax.numpy as jnp
import numpy as np
from jax import lax
from jax.experimental import pallas as pl
from jax.experimental.pallas import tpu as pltpu
from jax.sharding import PartitionSpec as P

RADIUS = 2
POISSON = 0.3
STIFF_VOID = 0.001
UPPER_FACTOR = 1.2
LOWER_RATIO = 0.1
MOVE_LIMIT = 0.2
VOLUME_TARGET = 0.5
EPSILON = 1e-06
HIGHEST = lax.Precision.HIGHEST
F32 = jnp.float32

HALO_LOW = 4
HALO_HIGH = 5
HALO = HALO_LOW + HALO_HIGH
VMEM_LIMIT = 24 * 1024 * 1024
UNROLL = 4


def hex_stiffness():
    lame_first = POISSON / ((1 + POISSON) * (1 - 2 * POISSON))
    lame_shear = 1 / (2 * (1 + POISSON))
    elastic = np.zeros((6, 6))
    elastic[:3, :3] = lame_first
    for axis_a in range(3):
        elastic[axis_a, axis_a] += 2 * lame_shear
        elastic[3 + axis_a, 3 + axis_a] = lame_shear
    shear_pairs = ((0, 1), (1, 2), (0, 2))
    gauss_point = 1 / np.sqrt(3)
    matrix = np.zeros((24, 24))
    for quad_index in range(8):
        quad_coords = [
            gauss_point * (2 * (quad_index >> 2 - axis_a & 1) - 1) for axis_a in range(3)
        ]
        shape_grads = np.zeros((8, 3))
        for corner in range(8):
            corner_signs = [2 * (corner >> 2 - axis_a & 1) - 1 for axis_a in range(3)]
            for axis_a in range(3):
                deriv_value = float(corner_signs[axis_a])
                for axis_b in range(3):
                    if axis_b != axis_a:
                        deriv_value *= (1 + corner_signs[axis_b] * quad_coords[axis_b]) / 2
                shape_grads[corner, axis_a] = deriv_value
        strain = np.zeros((6, 24))
        for corner in range(8):
            for axis_a in range(3):
                strain[axis_a, 3 * corner + axis_a] = shape_grads[corner, axis_a]
            for pair_index, shear_pair in enumerate(shear_pairs):
                strain[3 + pair_index, 3 * corner + shear_pair[0]] = shape_grads[
                    corner, shear_pair[1]
                ]
                strain[3 + pair_index, 3 * corner + shear_pair[1]] = shape_grads[
                    corner, shear_pair[0]
                ]
        matrix += strain.T @ elastic @ strain / 8
    return matrix.astype(np.float32)


def mode_stiffness():
    signs = np.zeros((8, 8))
    for mode in range(8):
        for corner in range(8):
            flips = bin(mode & ~corner & 7).count("1")
            signs[mode, corner] = -1.0 if flips & 1 else 1.0
    spread = np.kron(signs, np.eye(3))
    return spread @ hex_stiffness().astype(np.float64) @ spread.T / 64


MODES = mode_stiffness()
DIAG_ENTRY = float(hex_stiffness()[0, 0])


def entry(mode_a, comp_a, mode_b, comp_b):
    return float(MODES[3 * mode_a + comp_a, 3 * mode_b + comp_b])


NORMAL = ((4, 0), (2, 1), (1, 2))
SHEAR = (((2, 0), (4, 1)), ((1, 0), (4, 2)), ((1, 1), (2, 2)))
TWIST = ((3, 0), (5, 1), (6, 2))
BEND = (((3, 1), (5, 0)), ((3, 2), (6, 0)), ((5, 2), (6, 1)))
WARP = ((7, 0), (7, 1), (7, 2))
NORMAL_ON = entry(4, 0, 4, 0)
NORMAL_OFF = entry(4, 0, 2, 1)
SHEAR_ON = entry(2, 0, 4, 1)
TWIST_ON = entry(3, 0, 3, 0)
TWIST_OFF = entry(3, 0, 5, 1)
BEND_ON = entry(3, 1, 3, 1)
BEND_OFF = entry(3, 1, 5, 0)
WARP_ON = entry(7, 0, 7, 0)


def smoother_factors():
    sigma = (1 + LOWER_RATIO) / (1 - LOWER_RATIO)
    factor = 1 / sigma
    residual = np.array([1.0, 0.0, 0.0, 0.0])
    update = np.array([1.0, 0.0, 0.0, 0.0])
    total = np.zeros(4)
    for sweep in range(4):
        total = total + update
        if sweep < 3:
            residual = residual - np.concatenate([[0.0], update[:3]])
            factor_next = 1 / (2 * sigma - factor)
            update = factor_next * factor * update + 2 * factor_next * sigma * residual
            factor = factor_next
    return [float(value) for value in total]


def iota(shape, axis):
    return lax.broadcasted_iota(jnp.int32, shape, axis)


def gauss(offsets):
    return jnp.exp(-((offsets.astype(F32) / RADIUS) ** 2))


def gauss_table(count):
    return gauss(iota((count, count), 0) - iota((count, count), 1))


def shifts(shape, rows_x):
    inner = {}
    for axis, count in ((0, shape[0]), (1, rows_x)):
        index = iota(shape, axis) % count
        inner[axis] = (index < count - 1, index > 0)

    def above(value, axis):
        moved = pltpu.roll(value, shape[axis] - 1, axis)
        return jnp.where(inner[axis][0], moved, 0.0)

    def below(value, axis):
        moved = pltpu.roll(value, 1, axis)
        return jnp.where(inner[axis][1], moved, 0.0)

    return above, below


def row_modes(values, above):
    modes = {}
    for comp, value in enumerate(values):
        ahead = above(value, 0)
        for bit, part in ((0, value + ahead), (4, ahead - value)):
            beside = above(part, 1)
            modes[bit, comp] = part + beside
            modes[bit + 2, comp] = beside - part
    return modes


def element_modes(low, high):
    modes = {}
    for (bits, comp), value in low.items():
        other = high[bits, comp]
        if bits:
            modes[bits, comp] = value + other
        modes[bits + 1, comp] = other - value
    return modes


def element_forces(modes, scale):
    forces = {}
    total = modes[NORMAL[0]] + modes[NORMAL[1]] + modes[NORMAL[2]]
    shared = (scale * NORMAL_OFF) * total
    own = scale * (NORMAL_ON - NORMAL_OFF)
    for key in NORMAL:
        forces[key] = shared + own * modes[key]
    shear = scale * SHEAR_ON
    for key_a, key_b in SHEAR:
        forces[key_a] = forces[key_b] = shear * (modes[key_a] + modes[key_b])
    total = modes[TWIST[0]] + modes[TWIST[1]] + modes[TWIST[2]]
    shared = (scale * TWIST_OFF) * total
    own = scale * (TWIST_ON - TWIST_OFF)
    for key in TWIST:
        forces[key] = shared + own * modes[key]
    bend_on = scale * BEND_ON
    bend_off = scale * BEND_OFF
    for key_a, key_b in BEND:
        forces[key_a] = bend_on * modes[key_a] + bend_off * modes[key_b]
        forces[key_b] = bend_on * modes[key_b] + bend_off * modes[key_a]
    warp = scale * WARP_ON
    for key in WARP:
        forces[key] = warp * modes[key]
    return forces


def element_energy(modes):
    total = modes[NORMAL[0]] + modes[NORMAL[1]] + modes[NORMAL[2]]
    squares = sum(modes[key] * modes[key] for key in NORMAL)
    energy = NORMAL_OFF * (total * total) + (NORMAL_ON - NORMAL_OFF) * squares
    shear = 0.0
    for key_a, key_b in SHEAR:
        both = modes[key_a] + modes[key_b]
        shear = shear + both * both
    energy = energy + SHEAR_ON * shear
    total = modes[TWIST[0]] + modes[TWIST[1]] + modes[TWIST[2]]
    squares = sum(modes[key] * modes[key] for key in TWIST)
    energy = energy + TWIST_OFF * (total * total) + (TWIST_ON - TWIST_OFF) * squares
    squares = sum(modes[key] * modes[key] for pair in BEND for key in pair)
    crossed = sum(modes[key_a] * modes[key_b] for key_a, key_b in BEND)
    energy = energy + BEND_ON * squares + (2 * BEND_OFF) * crossed
    squares = sum(modes[key] * modes[key] for key in WARP)
    return energy + WARP_ON * squares


ROW_KEYS = [(bits, comp) for comp in range(3) for bits in (0, 2, 4, 6)]


def split_forces(forces):
    here, there = {}, {}
    for bits, comp in ROW_KEYS:
        change = forces[bits + 1, comp]
        if bits:
            common = forces[bits, comp]
            here[bits, comp] = common - change
            there[bits, comp] = common + change
        else:
            here[bits, comp] = -change
            there[bits, comp] = change
    return here, there


def node_forces(modes, below):
    values = []
    for comp in range(3):
        parts = []
        for bit in (0, 4):
            common, change = modes[bit, comp], modes[bit + 2, comp]
            parts.append((common - change) + below(common + change, 1))
        values.append((parts[0] - parts[1]) + below(parts[0] + parts[1], 0))
    return values


def apply_rows(first, last, load_row, scale_row, emit, above, below, carry=None):
    def advance(index, low, pending):
        high = row_modes(load_row(index + 1), above)
        forces = element_forces(element_modes(low, high), scale_row(index))
        here, there = split_forces(forces)
        return high, {key: pending[key] + here[key] for key in ROW_KEYS}, there

    def pack(low, pending):
        return tuple(low[key] for key in ROW_KEYS) + tuple(pending[key] for key in ROW_KEYS)

    def unpack(state):
        count = len(ROW_KEYS)
        return dict(zip(ROW_KEYS, state[:count])), dict(zip(ROW_KEYS, state[count:]))

    low = row_modes(load_row(first), above)
    zero = {key: jnp.zeros_like(low[key]) for key in ROW_KEYS}
    low, _, pending = advance(first, low, zero)

    def step(index, state):
        carried, (low, pending) = state[0], unpack(state[1])
        low, modes, pending = advance(index, low, pending)
        carried = emit(index, node_forces(modes, below), carried)
        return carried, pack(low, pending)

    carried, _ = lax.fori_loop(
        first + 1, last, step, (carry, pack(low, pending)), unroll=UNROLL
    )
    return carried


def dot(left, right):
    return jnp.dot(left, right, precision=HIGHEST, preferred_element_type=F32)


def call(body, outs, *args, scratch=(), name=None, flops=0, space=pltpu.VMEM):
    return pl.pallas_call(
        body,
        out_shape=outs,
        in_specs=[pl.BlockSpec(memory_space=space)] * len(args),
        out_specs=jax.tree.map(lambda _: pl.BlockSpec(memory_space=pltpu.VMEM), outs),
        scratch_shapes=list(scratch),
        compiler_params=pltpu.CompilerParams(vmem_limit_bytes=VMEM_LIMIT),
        cost_estimate=pl.CostEstimate(flops=flops, bytes_accessed=1 << 20, transcendentals=0),
        name=name,
    )(*args)


def exchange(message, axes):
    rows = message.shape[0]
    return lax.all_to_all(
        message.reshape(rows, 1, message.shape[1]), axes, split_axis=0, concat_axis=0, tiled=True
    ).reshape(message.shape)


def shards(start_disp, density, design, support, load_nodes, load_forces):
    slabs = lax.axis_size("slab")
    parts = lax.axis_size("load")
    loads, comps, layers, rows_x, cols_y = start_disp.shape
    points = load_nodes.shape[1]
    depth = slabs * layers
    strip = cols_y // slabs
    span = strip + HALO
    width = loads * rows_x
    half = strip * rows_x // width
    plane = (depth, width)
    in_rows = (comps + 1) * span + rows_x
    sum_rows = 3 + half
    numer_rows = half + 1
    out_rows = comps * strip + 1
    block = lambda count: jax.ShapeDtypeStruct((count, span) + plane, F32)
    flat = lambda rows: jax.ShapeDtypeStruct((rows, width), F32)
    smoother = smoother_factors()

    def pack_body(
        disp_ref, dens_ref, design_ref, support_ref, out_ref,
        stage_ref, dens_in, design_in, support_in, pad_ref, sems,
    ):
        copies = [
            pltpu.make_async_copy(dens_ref.at[0], dens_in, sems.at[0]),
            pltpu.make_async_copy(design_ref.at[0], design_in, sems.at[1]),
            pltpu.make_async_copy(support_ref.at[0], support_in, sems.at[2]),
        ]
        for load in range(loads):
            copies.append(
                pltpu.make_async_copy(
                    disp_ref.at[load, :, 0],
                    stage_ref.at[:, load * rows_x : (load + 1) * rows_x],
                    sems.at[3 + load],
                )
            )
        for copy in copies:
            copy.start()
        cube_side = iota((1, width), 1) < rows_x
        for field in range(comps + 1):
            fill = jnp.zeros((1, width), F32) if field < comps else jnp.where(cube_side, -1.0, 1.0)
            pad_ref[field, 0:HALO_LOW] = jnp.broadcast_to(fill, (HALO_LOW, width))
            pad_ref[field, HALO_LOW + cols_y : HALO + cols_y] = jnp.broadcast_to(
                fill, (HALO_HIGH, width)
            )
        for copy in copies[:3]:
            copy.wait()
        solid = design_in[...].astype(F32) * dens_in[...]
        both = jnp.concatenate([solid * solid * solid, support_in[...].astype(F32)], 0)
        pad_ref[comps, HALO_LOW : HALO_LOW + cols_y] = both.T
        for copy in copies[3:]:
            copy.wait()
        for comp in range(comps):
            pad_ref[comp, HALO_LOW : HALO_LOW + cols_y] = stage_ref[comp].T
        for target in range(slabs):
            base = target * in_rows
            for field in range(comps + 1):
                out_ref[base + field * span : base + (field + 1) * span] = pad_ref[
                    field, target * strip : target * strip + span
                ]
            out_ref[base + (comps + 1) * span : base + in_rows] = dens_in[...]

    message = call(
        pack_body,
        flat(slabs * in_rows),
        start_disp,
        density,
        design,
        support,
        scratch=[
            pltpu.VMEM((comps, width, cols_y), F32),
            pltpu.VMEM((rows_x, cols_y), F32),
            pltpu.VMEM((rows_x, cols_y), jnp.int32),
            pltpu.VMEM((rows_x, cols_y), jnp.int32),
            pltpu.VMEM((comps + 1, cols_y + 2 * 8, width), F32),
            pltpu.SemaphoreType.DMA((3 + loads,)),
        ],
        name="pack",
        space=pl.ANY,
    )
    received = exchange(message, "slab")

    cells = -(-span * depth // 16) * 16
    chunk = min(256, points)

    def loads_body(nodes_ref, forces_ref, out_ref):
        first = lax.axis_index("slab") * strip - HALO_LOW
        out_ref[...] = jnp.zeros_like(out_ref)
        for load in range(loads):
            for start in range(0, points, chunk):
                part = slice(start, start + chunk)
                node = nodes_ref[load : load + 1, part]
                row = node % cols_y - first
                lane = load * rows_x + (node // cols_y) % rows_x
                layer = node // (cols_y * rows_x)
                cell = jnp.where((row >= 0) & (row < span), row * depth + layer, -1)
                hit = iota((cells, chunk), 0) == cell
                spot = (iota((width, chunk), 0) == lane).astype(F32).astype(jnp.bfloat16)
                for comp in range(comps):
                    rest = forces_ref[load, comp : comp + 1, part]
                    for piece in range(3):
                        rounded = rest.astype(jnp.bfloat16).astype(F32)
                        rest = rest - rounded
                        picked = jnp.where(hit, rounded, 0.0).astype(jnp.bfloat16)
                        out_ref[comp] += lax.dot_general(
                            picked, spot, (((1,), (1,)), ((), ())), preferred_element_type=F32
                        )

    right_side = call(
        loads_body,
        jax.ShapeDtypeStruct((comps, cells, width), F32),
        load_nodes,
        load_forces,
        name="point_loads",
        flops=1 << 28,
    )

    def own_row(row):
        return (row >= HALO_LOW) & (row < HALO_LOW + strip)

    def packed_table(part):
        shape = (slabs * half, cols_y)
        row = iota(shape, 0)
        return gauss(row // half * strip + part * half + row % half - iota(shape, 1))

    def residual_body(
        in_ref, rhs_ref, design_ref, disp_ref, cube_ref, geo_ref, zero_ref, one_ref, dens_ref, sum_ref
    ):
        above, below = shifts(plane, rows_x)
        cube_side = iota(plane, 1) < rows_x
        for row in range(span):
            pick = lambda field: in_ref[pl.ds(field * span + row, depth, stride=in_rows), :]
            for comp in range(comps):
                disp_ref[comp, row] = pick(comp)
            both = pick(comps)
            other = pltpu.roll(both, rows_x, 1)
            cube = jnp.where(cube_side, both, other)
            cube_ref[0, row] = cube
            geo_ref[0, row] = jnp.where(
                cube < 0.0, 0.0, STIFF_VOID + (1.0 - STIFF_VOID) * cube
            )
            geo_ref[1, row] = 1.0 - jnp.where(cube_side, other, both)
        for row in range(1, span - 1):
            beside = geo_ref[0, row] + geo_ref[0, row - 1]
            beside = beside + below(beside, 0)
            beside = beside + below(beside, 1)
            free = geo_ref[1, row]
            geo_ref[2, row] = 1.0 / (free * DIAG_ENTRY * beside + (1.0 - free))

        scale_row = lambda row: geo_ref[0, row]

        def start_row(row):
            free = geo_ref[1, row]
            return [free * disp_ref[comp, row] for comp in range(comps)]

        def emit_residual(row, forces, carried):
            free, inverse = geo_ref[1, row], geo_ref[2, row]
            total = jnp.zeros(plane, F32)
            for comp, force in enumerate(forces):
                load_row = rhs_ref[comp, pl.ds(pl.multiple_of(row * depth, depth), depth), :]
                rest = free * (load_row - force) - (1.0 - free) * disp_ref[comp, row]
                value = rest * inverse
                zero_ref[comp, row] = value
                total = total + value * rest
            return carried + jnp.where(own_row(row), total, 0.0)

        weight = apply_rows(
            0, span - 1, start_row, scale_row, emit_residual, above, below,
            jnp.zeros(plane, F32),
        )

        def zero_row(row):
            free = geo_ref[1, row]
            return [free * zero_ref[comp, row] for comp in range(comps)]

        def emit_one(row, forces, carried):
            free, inverse = geo_ref[1, row], geo_ref[2, row]
            total = jnp.zeros(plane, F32)
            for comp, force in enumerate(forces):
                value = zero_ref[comp, row]
                applied = free * force + (1.0 - free) * value
                one_ref[comp, row] = applied * inverse
                total = total + value * applied
            return carried + jnp.where(own_row(row), total, 0.0)

        curve = apply_rows(
            1, span - 2, zero_row, scale_row, emit_one, above, below, jnp.zeros(plane, F32)
        )

        here = lax.axis_index("slab")
        mixed = jnp.zeros((rows_x, cols_y), F32)
        for layer in range(depth):
            weight_z = gauss(jnp.full((1, cols_y), here - layer, jnp.int32))
            base = layer * in_rows + (comps + 1) * span
            mixed = mixed + weight_z * in_ref[base : base + rows_x]
        mixed = dot(gauss_table(rows_x), mixed)
        filtered = dot(mixed, gauss_table(cols_y))
        dens_ref[...] = filtered
        mask = design_ref[0].astype(F32)
        share = (mask / filtered).T
        share = jnp.concatenate(
            [dot(packed_table(part), share) for part in range(strip // half)], 1
        )
        down = lambda value: jnp.sum(value, 0, keepdims=True)
        sums = [down(curve), down(weight), down(mask)]
        for target in range(slabs):
            base = target * sum_rows
            for index, value in enumerate(sums):
                sum_ref[base + index : base + index + 1] = value
            sum_ref[base + 3 : base + sum_rows] = share[target * half : (target + 1) * half]

    disp, cube, geometry, zeroth, first, dens_filtered, sums = call(
        residual_body,
        (
            block(comps),
            block(1),
            block(3),
            block(comps),
            block(comps),
            flat(rows_x),
            flat(slabs * sum_rows),
        ),
        received,
        right_side,
        design,
        name="residual",
        flops=1 << 26,
    )
    all_sums = exchange(sums, "slab")

    def powers_body(geo_ref, one_ref, two_ref, three_ref):
        above, below = shifts(plane, rows_x)
        scale_row = lambda row: geo_ref[0, row]
        for source, target, edge in ((one_ref, two_ref, 2), (two_ref, three_ref, 3)):

            def load_row(row):
                free = geo_ref[1, row]
                return [free * source[comp, row] for comp in range(comps)]

            def emit(row, forces, carried):
                free, inverse = geo_ref[1, row], geo_ref[2, row]
                for comp, force in enumerate(forces):
                    target[comp, row] = (
                        free * force + (1.0 - free) * source[comp, row]
                    ) * inverse
                return carried

            apply_rows(
                edge, span - 1 - edge, load_row, scale_row, emit, above, below,
                jnp.zeros((1, 1), F32),
            )

    second, third = call(
        powers_body,
        (block(comps), block(comps)),
        geometry,
        first,
        name="powers",
        flops=1 << 26,
    )

    def energy_body(
        sums_ref, disp_ref, cube_ref, geo_ref, zero_ref, one_ref, two_ref, three_ref,
        disp_out_ref, numer_ref, count_ref, weak_ref,
    ):
        above, below = shifts(plane, rows_x)
        gather = lambda index: sum(
            sums_ref[layer * sum_rows + index : layer * sum_rows + index + 1]
            for layer in range(slabs)
        )
        curve, weight, count = gather(0), gather(1), gather(2)
        across = lambda value: jnp.sum(value, 1, keepdims=True)
        count_ref[...] = jnp.broadcast_to(across(count), (8, width))
        owner = iota((1, width), 1) // rows_x
        inverse = jnp.zeros((1, width), F32)
        for load in range(loads):
            mine = owner == load
            upper = UPPER_FACTOR * (
                across(jnp.where(mine, curve, 0.0)) / across(jnp.where(mine, weight, 0.0))
            )
            inverse = jnp.where(mine, 1.0 / (0.5 * (upper + LOWER_RATIO * upper)), inverse)
        inverse = jnp.broadcast_to(inverse, plane)
        lower = None
        for row in range(HALO_LOW, HALO_LOW + strip + 1):
            free = geo_ref[1, row]
            values = []
            for comp in range(comps):
                value = smoother[3] * three_ref[comp, row]
                value = smoother[2] * two_ref[comp, row] + inverse * value
                value = smoother[1] * one_ref[comp, row] + inverse * value
                value = smoother[0] * zero_ref[comp, row] + inverse * value
                value = disp_ref[comp, row] + inverse * value
                if row < HALO_LOW + strip:
                    place = comp * strip + row - HALO_LOW
                    disp_out_ref[pl.ds(place, depth, stride=out_rows), :] = value
                values.append(free * value)
            modes = row_modes(values, above)
            if lower is not None:
                weak_ref[(row - 1 - HALO_LOW) * depth : (row - HALO_LOW) * depth] = (
                    (3.0 * (1.0 - STIFF_VOID))
                    * cube_ref[0, row - 1]
                    * element_energy(element_modes(lower, modes))
                )
            lower = modes
        disp_out_ref[pl.ds(out_rows - 1, depth, stride=out_rows), :] = jnp.zeros(plane, F32)
        weak = weak_ref[...]
        smooth = jnp.zeros((depth * half, width), F32)
        for part in range(strip // half):
            shape = (depth * half, strip * depth)
            to, source = iota(shape, 0), iota(shape, 1)
            table = jnp.where(
                to % half + part * half == source // depth,
                gauss(to // half - source % depth),
                0.0,
            )
            shape = (width, width)
            to, source = iota(shape, 1), iota(shape, 0)
            table_x = jnp.where(
                to // rows_x == part, gauss(to % rows_x - source % rows_x), 0.0
            )
            smooth = smooth + dot(dot(table, weak), table_x)
        weighted = jnp.zeros((1, width), F32)
        for layer in range(depth):
            piece = smooth[layer * half : (layer + 1) * half]
            base = layer * sum_rows
            weighted = weighted + jnp.sum(
                piece * sums_ref[base + 3 : base + sum_rows], 0, keepdims=True
            )
        for layer in range(depth):
            piece = smooth[layer * half : (layer + 1) * half]
            for part in range(parts):
                base = (part * slabs + layer) * numer_rows
                numer_ref[base : base + half] = piece
                numer_ref[base + half : base + numer_rows] = weighted

    disp_message, numer_message, count = call(
        energy_body,
        (flat(slabs * out_rows), flat(parts * slabs * numer_rows), flat(8)),
        all_sums,
        disp,
        cube,
        geometry,
        zeroth,
        first,
        second,
        third,
        scratch=[pltpu.VMEM((strip * depth, width), F32)],
        name="energy",
        flops=1 << 24,
    )
    numer_pieces = exchange(numer_message, ("load", "slab"))

    def trial_body(
        numer_ref, dens_ref, filtered_ref, design_ref, count_ref, disp_ref, trial_ref, out_ref, plane_ref
    ):
        weighted = jnp.zeros((1, width), F32)
        for source in range(slabs):
            total = jnp.zeros((half, width), F32)
            for part in range(parts):
                base = (part * slabs + source) * numer_rows
                total = total + numer_ref[base : base + half]
                weighted = weighted + numer_ref[base + half : base + numer_rows]
            plane_ref[source * half : (source + 1) * half] = total
        mean = jnp.sum(weighted, 1, keepdims=True) / count_ref[0:1] + EPSILON
        packed = plane_ref[...].T
        numer = jnp.zeros((rows_x, cols_y), F32)
        for part in range(strip // half):
            shape = (slabs * half, cols_y)
            row = iota(shape, 0)
            table = gauss(row // half * strip + part * half + row % half - iota(shape, 1))
            numer = numer + dot(packed[part * rows_x : (part + 1) * rows_x], table)
        mask = design_ref[0].astype(F32)
        dens = dens_ref[0]
        ratio = mask * (numer / filtered_ref[...]) / mean
        trial = jnp.clip(dens * jnp.sqrt(ratio), dens - MOVE_LIMIT, dens + MOVE_LIMIT)
        trial_ref[...] = trial
        out_ref[...] = disp_ref[...]
        volume = jnp.sum(mask * trial, 0, keepdims=True)
        for target in range(slabs):
            base = (target + 1) * out_rows - 1
            out_ref[base : base + 1] = volume

    trial, out_message = call(
        trial_body,
        (flat(rows_x), flat(slabs * out_rows)),
        numer_pieces,
        density,
        dens_filtered,
        design,
        count,
        disp_message,
        scratch=[pltpu.VMEM((slabs * half, width), F32)],
        name="trial",
    )
    out_pieces = exchange(out_message, "slab")

    def final_body(pieces_ref, trial_ref, design_ref, count_ref, disp_ref, dens_ref, whole_ref):
        volume = jnp.zeros((1, width), F32)
        for source in range(slabs):
            base = (source + 1) * out_rows
            volume = volume + pieces_ref[base - 1 : base]
            for comp in range(comps):
                base = source * out_rows + comp * strip
                whole_ref[comp, source * strip : (source + 1) * strip] = pieces_ref[
                    base : base + strip
                ]
        volume = jnp.sum(volume, 1, keepdims=True)
        scale = VOLUME_TARGET / (volume / count_ref[0:1] + EPSILON)
        mask = design_ref[0].astype(F32)
        dens_ref[0] = mask * jnp.minimum(scale * trial_ref[...], 1.0)
        for comp in range(comps):
            turned = whole_ref[comp].T
            for load in range(loads):
                disp_ref[load, comp, 0] = turned[load * rows_x : (load + 1) * rows_x]

    return call(
        final_body,
        (
            jax.ShapeDtypeStruct(start_disp.shape, F32),
            jax.ShapeDtypeStruct(density.shape, F32),
        ),
        out_pieces,
        trial,
        design,
        count,
        scratch=[pltpu.VMEM((comps, cols_y, width), F32)],
        name="final",
    )


def solution(mesh):
    return jax.shard_map(
        shards,
        mesh=mesh,
        in_specs=(
            P("load", None, "slab", None, None),
            P("slab", None, None),
            P("slab", None, None),
            P("slab", None, None),
            P("load", None),
            P("load", None, None),
        ),
        out_specs=(P("load", None, "slab", None, None), P("slab", None, None)),
        check_vma=False,
    )
```

time: 73.5 us -> 69.3 us (0.943)
  waiting for transfers between devices: 20.4 us -> 16.8 us
  blocking collectives: 21.9 us -> 21.1 us
    all_to_all x2, waiting for transfers between devices: 20.4 us -> 16.8 us  [exchange(): lax.all_to_all(message.reshape(rows, 1, message.shape[1]), axes, split_ax...]
    all_to_all x2, blocking collectives: 21.9 us -> 21.1 us  [exchange(): lax.all_to_all(message.reshape(rows, 1, message.shape[1]), axes, split_ax...]
  transfers between devices with their start and end apart: 2 -> 2, of which waited for: 2 -> 2; matrix products, arithmetic and copies ran while one was open for 0% -> 0% of each run, Pallas kernels for 9% -> 10%
where the time goes in v2:
time: 69.3 us; the launch traced here: 68.6 us
  blocking collectives  21.1 us (30%)
  waiting for transfers between devices  16.8 us (24%)
  Pallas kernels  15 us (22%)
  starting transfers between devices  11.1 us (16%)
  local copies, waits for them, and re-layouts  3.92 us (6%)
  between operations  0.71 us (1%)
    all_to_all x2, blocking collectives, exchange(): lax.all_to_all(message.reshape(rows, 1, message.shape[1]), axes, split_ax...  21.1 us
    all_to_all x2, waiting for transfers between devices, exchange(): lax.all_to_all(message.reshape(rows, 1, message.shape[1]), axes, split_ax...  16.8 us
    pallas_call x7, Pallas kernels, call(): pl.pallas_call(body, out_shape=outs, in_specs=[pl.BlockSpec(memory_space=...  15 us
    all_to_all x2, starting transfers between devices, exchange(): lax.all_to_all(message.reshape(rows, 1, message.shape[1]), axes, split_ax...  11.1 us
    unnamed x17, local copies, waits for them, and re-layouts  3.92 us
  transfers between devices with their start and end apart: 2, of which 2 were waited for; matrix products, arithmetic and copies ran while one was open for 0% of the time, Pallas kernels for 10%

profile of v2, /device:TPU:0, one launch (start us, length us, event | category | flops | bytes accessed | tf_op | source)
XLA Modules:
  0.0 68.6 jit_solution(13075668740310728455)
XLA Ops:
  0.6 0.0 copy-start
  0.6 0.7 %copy-done = s32[1,64,128]{2,1,0:T(8,128)S(1)} copy-done((s32[1,64,128]{2,1,0:T(8,128)S(1)}, s32[1,64,128]{2,1,0:T(8,128)}, u32[]{:S(2)}) %copy-start) | copy-done | bytes 32792
  1.4 0.0 copy-start.2
  1.4 0.9 %copy-done.2 = f32[2,3,1,64,128]{4,3,2,1,0:T(8,128)S(1)} copy-done((f32[2,3,1,64,128]{4,3,2,1,0:T(8,128)S(1)}, f32[2,3,1,64,128]{4,3,2,1,0:T(8,128)}, u32[]{:S(2)}) %copy-start.2) | copy-done | bytes 196632
  2.3 0.0 copy-start.3
  2.3 0.8 %copy-done.3 = f32[1,64,128]{2,1,0:T(8,128)S(1)} copy-done((f32[1,64,128]{2,1,0:T(8,128)S(1)}, f32[1,64,128]{2,1,0:T(8,128)}, u32[]{:S(2)}) %copy-start.3) | copy-done | bytes 32792
  3.1 0.0 copy-start.5
  3.1 0.8 %copy-done.5 = s32[1,64,128]{2,1,0:T(8,128)S(1)} copy-done((s32[1,64,128]{2,1,0:T(8,128)S(1)}, s32[1,64,128]{2,1,0:T(8,128)}, u32[]{:S(2)}) %copy-start.5) | copy-done | bytes 32792
  3.8 1.4 %pack.1 = f32[1312,128]{1,0:T(8,128)} custom-call(f32[2,3,1,64,128]{4,3,2,1,0:T(8,128)S(1)} %copy-done.2, f32[1,64,128]{2,1,0:T(8,128)S(1)} %copy-done.3, s32[1,64,128]{2,1,0:T(8,128)S(1)} %copy-done, s32[1,64,128]{2,1,0:T(8,128)S(1)} %copy-done.5), custom_call_target="tpu_custom_call" | custom-call | bytes 1048576 | tf_op jit(solution)/shard_map/pack/pallas_call | solution.py:275
  5.2 0.0 copy-start.7
  5.2 7.4 %all-to-all-start = ((f32[1312,1,128]{2,1,0:T(1,128)}), f32[1312,1,128]{2,1,0:T(1,128)S(1)}, u32[]{:S(2)}, u32[]{:S(2)}) async-start(f32[1312,1,128]{2,1,0:T(1,128)} %bitcast.1), calls=%async_computation | async-start | bytes 1343488 | tf_op jit(solution)/shard_map/all_to_all | solution.py:289
  12.6 0.0 copy-done.7
  12.6 0.0 copy-start.6
  12.7 0.7 copy-done.6
  13.4 0.0 copy-start.1
  13.4 4.2 %point_loads.1.rhs_ref = f32[3,208,128]{2,1,0:T(8,128)S(1)} custom-call(s32[2,2048]{1,0:T(2,128)S(1)} %copy-done.6, f32[2,3,2048]{2,1,0:T(4,128)S(1)} %copy.10.forces_ref), custom_call_target="tpu_custom_call" | custom-call | flops 268435456 | bytes 1048576 | tf_op jit(solution)/shard_map/point_loads/pallas_call | solution.py:275
  17.5 12.8 %all-to-all-done = f32[1312,1,128]{2,1,0:T(1,128)S(1)} async-done(((f32[1312,1,128]{2,1,0:T(1,128)}), f32[1312,1,128]{2,1,0:T(1,128)S(1)}, u32[]{:S(2)}, u32[]{:S(2)}) %all-to-all-start) | async-done | bytes 671776 | tf_op jit(solution)/shard_map/all_to_all | solution.py:289
  30.3 0.0 copy-done.1
  30.3 4.5 %residual.1 = (f32[3,25,8,128]{3,2,1,0:T(8,128)S(1)}, f32[1,25,8,128]{3,2,1,0:T(8,128)S(1)}, f32[3,25,8,128]{3,2,1,0:T(8,128)S(1)}, f32[3,25,8,128]{3,2,1,0:T(8,...) custom-call(f32[1312,128]{1,0:T(8,128)S(1)} %bitcast.16, ...), custom_call_target="tpu_custom_call" | custom-call | flops 67108864 | bytes 1048576 | tf_op jit(solution)/shard_map/residual/pallas_call | solution.py:275
  34.8 3.6 %all-to-all-start.1 = ((f32[88,1,128]{2,1,0:T(1,128)}), f32[88,1,128]{2,1,0:T(1,128)S(1)}, u32[]{:S(2)}, u32[]{:S(2)}) async-start(f32[88,1,128]{2,1,0:T(1,128)} %bitcast.4), calls=%async_computation.1 | async-start | bytes 90112 | tf_op jit(solution)/shard_map/all_to_all | solution.py:289
  38.5 2.7 %powers.1 = (f32[3,25,8,128]{3,2,1,0:T(8,128)S(1)}, f32[3,25,8,128]{3,2,1,0:T(8,128)S(1)}) custom-call(f32[3,25,8,128]{3,2,1,0:T(8,128)S(1)} %get-tuple-element.19.geo_ref, f32[3,25,8,128]{3,2,1,0:T(8,128)S(1)} %get-tuple-element.21.one_ref), custom_call_target="tpu_custom_call" | custom-call | flops 67108864 | bytes 1048576 | tf_op jit(solution)/shard_map/powers/pallas_call | solution.py:275
  41.2 4.0 %all-to-all-done.1 = f32[88,1,128]{2,1,0:T(1,128)S(1)} async-done(((f32[88,1,128]{2,1,0:T(1,128)}), f32[88,1,128]{2,1,0:T(1,128)S(1)}, u32[]{:S(2)}, u32[]{:S(2)}) %all-to-all-start.1) | async-done | bytes 45088 | tf_op jit(solution)/shard_map/all_to_all | solution.py:289
  45.2 1.1 %energy.1 = (f32[392,128]{1,0:T(8,128)S(1)}, f32[288,128]{1,0:T(8,128)S(1)}, f32[8,128]{1,0:T(8,128)S(1)}) custom-call(f32[88,128]{1,0:T(8,128)S(1)} %bitcast.20, f32[3,25,8,128]{3,2,1,0:T(8,128)S(1)} %get-tuple-element.17.disp_ref, f32[1,25,8,128]{3,2,1,0:T(8,128)S(1)} %get-tuple-element.18.cube_ref, f32[3,25,8,128]{3,2,1,0:T(8,128)S(1)} %get-tuple-element.19.geo_ref, ...), custom_call_target="tpu_custom_call" | custom-call | flops 16777216 | bytes 1048576 | tf_op jit(solution)/shard_map/energy/pallas_call | solution.py:275
  46.3 0.0 copy-start.4
  46.4 9.7 %all_to_all.20 = f32[288,1,128]{2,1,0:T(1,128)S(1)} all-to-all(f32[288,1,128]{2,1,0:T(1,128)S(1)} %bitcast.21), channel_id=1, replica_groups=mesh['slab'=8,'load'=4] {'load','slab'}, dimensions={0} | all-to-all | bytes 294912 | tf_op jit(solution)/shard_map/all_to_all | solution.py:289
  56.0 0.0 copy-done.4
  56.0 0.3 trial.1
  56.3 11.5 %all_to_all.21 = f32[392,1,128]{2,1,0:T(1,128)S(1)} all-to-all(f32[392,1,128]{2,1,0:T(1,128)S(1)} %bitcast.19), channel_id=1, replica_groups=mesh['slab'=8,'load'=4] {'slab'}, dimensions={0} | all-to-all | bytes 401408 | tf_op jit(solution)/shard_map/all_to_all | solution.py:289
  67.8 0.8 %final.1 = (f32[2,3,1,64,128]{4,3,2,1,0:T(8,128)}, f32[1,64,128]{2,1,0:T(8,128)}) custom-call(f32[392,128]{1,0:T(8,128)S(1)} %bitcast.17, f32[64,128]{1,0:T(8,128)S(1)} %get-tuple-element.29.trial_ref, s32[1,64,128]{2,1,0:T(8,128)S(1)} %copy-done.1, f32[8,128]{1,0:T(8,128)S(1)} %get-tuple-element.26.count_ref), custom_call_target="tpu_custom_call" | custom-call | bytes 1048576 | tf_op jit(solution)/shard_map/final/pallas_call | solution.py:275
  (1 shorter events, 0.0 us)
Async XLA Ops:
  0.6 0.8 %copy-start = (s32[1,64,128]{2,1,0:T(8,128)S(1)}, s32[1,64,128]{2,1,0:T(8,128)}, u32[]{:S(2)}) copy-start(s32[1,64,128]{2,1,0:T(8,128)} %design_ref.7) | copy-start | bytes 98308
  1.4 0.9 %copy-start.2 = (f32[2,3,1,64,128]{4,3,2,1,0:T(8,128)S(1)}, f32[2,3,1,64,128]{4,3,2,1,0:T(8,128)}, u32[]{:S(2)}) copy-start(f32[2,3,1,64,128]{4,3,2,1,0:T(8,128)} %disp_ref.1) | copy-start | bytes 589828
  2.3 0.8 %copy-start.3 = (f32[1,64,128]{2,1,0:T(8,128)S(1)}, f32[1,64,128]{2,1,0:T(8,128)}, u32[]{:S(2)}) copy-start(f32[1,64,128]{2,1,0:T(8,128)} %dens_ref.3) | copy-start | bytes 98308
  3.1 0.8 %copy-start.5 = (s32[1,64,128]{2,1,0:T(8,128)S(1)}, s32[1,64,128]{2,1,0:T(8,128)}, u32[]{:S(2)}) copy-start(s32[1,64,128]{2,1,0:T(8,128)} %support_ref.1) | copy-start | bytes 98308
  5.2 7.4 %copy-start.7 = (f32[2,3,2048]{2,0,1:T(2,128)S(1)}, f32[2,3,2048]{2,0,1:T(2,128)}, u32[]{:S(2)}) copy-start(f32[2,3,2048]{2,0,1:T(2,128)} %param.11) | copy-start | bytes 147460
  5.2 25.1 %all-to-all-start = ((f32[1312,1,128]{2,1,0:T(1,128)}), f32[1312,1,128]{2,1,0:T(1,128)S(1)}, u32[]{:S(2)}, u32[]{:S(2)}) async-start(f32[1312,1,128]{2,1,0:T(1,128)} %bitcast.1), calls=%async_computation | async-start | bytes 1343488 | tf_op jit(solution)/shard_map/all_to_all | solution.py:289
  12.6 0.7 %copy-start.6 = (s32[2,2048]{1,0:T(2,128)S(1)}, s32[2,2048]{1,0:T(2,128)}, u32[]{:S(2)}) copy-start(s32[2,2048]{1,0:T(2,128)} %nodes_ref.1) | copy-start | bytes 49156
  13.4 16.9 %copy-start.1 = (s32[1,64,128]{2,1,0:T(8,128)S(1)}, s32[1,64,128]{2,1,0:T(8,128)}, u32[]{:S(2)}) copy-start(s32[1,64,128]{2,1,0:T(8,128)} %design_ref.7) | copy-start | bytes 98308
  34.8 10.4 %all-to-all-start.1 = ((f32[88,1,128]{2,1,0:T(1,128)}), f32[88,1,128]{2,1,0:T(1,128)S(1)}, u32[]{:S(2)}, u32[]{:S(2)}) async-start(f32[88,1,128]{2,1,0:T(1,128)} %bitcast.4), calls=%async_computation.1 | async-start | bytes 90112 | tf_op jit(solution)/shard_map/all_to_all | solution.py:289
  46.3 9.7 %copy-start.4 = (f32[1,64,128]{2,1,0:T(8,128)S(1)}, f32[1,64,128]{2,1,0:T(8,128)}, u32[]{:S(2)}) copy-start(f32[1,64,128]{2,1,0:T(8,128)} %dens_ref.3) | copy-start | bytes 98308

commit v3 on v2

--- a/solution.py
+++ b/solution.py
@@ -23,7 +23,6 @@
 HALO_HIGH = 5
 HALO = HALO_LOW + HALO_HIGH
 VMEM_LIMIT = 24 * 1024 * 1024
-UNROLL = 4
 
 
 def hex_stiffness():
@@ -146,11 +145,11 @@
 def row_modes(values, above):
     modes = {}
     for comp, value in enumerate(values):
-        ahead = above(value, 0)
-        for bit, part in ((0, value + ahead), (4, ahead - value)):
-            beside = above(part, 1)
-            modes[bit, comp] = part + beside
-            modes[bit + 2, comp] = beside - part
+        beside = above(value, 1)
+        for bit, part in ((0, value + beside), (2, beside - value)):
+            ahead = above(part, 0)
+            modes[bit, comp] = part + ahead
+            modes[bit + 4, comp] = ahead - part
     return modes
 
 
@@ -230,10 +229,10 @@
     values = []
     for comp in range(3):
         parts = []
-        for bit in (0, 4):
-            common, change = modes[bit, comp], modes[bit + 2, comp]
-            parts.append((common - change) + below(common + change, 1))
-        values.append((parts[0] - parts[1]) + below(parts[0] + parts[1], 0))
+        for bit in (0, 2):
+            common, change = modes[bit, comp], modes[bit + 4, comp]
+            parts.append((common - change) + below(common + change, 0))
+        values.append((parts[0] - parts[1]) + below(parts[0] + parts[1], 1))
     return values
 
 
@@ -261,10 +260,10 @@
         carried = emit(index, node_forces(modes, below), carried)
         return carried, pack(low, pending)
 
-    carried, _ = lax.fori_loop(
-        first + 1, last, step, (carry, pack(low, pending)), unroll=UNROLL
-    )
-    return carried
+    for index in range(first + 1, last):
+        low, modes, pending = advance(index, low, pending)
+        carry = emit(index, node_forces(modes, below), carry)
+    return carry
 
 
 def dot(left, right):
@@ -356,10 +355,10 @@
     message = call(
         pack_body,
         flat(slabs * in_rows),
-        start_disp,
-        density,
-        design,
-        support,
+        *(
+            pltpu.with_memory_space_constraint(value, pltpu.HBM)
+            for value in (start_disp, density, design, support)
+        ),
         scratch=[
             pltpu.VMEM((comps, width, cols_y), F32),
             pltpu.VMEM((rows_x, cols_y), F32),
@@ -369,7 +368,7 @@
             pltpu.SemaphoreType.DMA((3 + loads,)),
         ],
         name="pack",
-        space=pl.ANY,
+        space=pltpu.HBM,
     )
     received = exchange(message, "slab")
 
@@ -450,12 +449,12 @@
             free, inverse = geo_ref[1, row], geo_ref[2, row]
             total = jnp.zeros(plane, F32)
             for comp, force in enumerate(forces):
-                load_row = rhs_ref[comp, pl.ds(pl.multiple_of(row * depth, depth), depth), :]
+                load_row = rhs_ref[comp, pl.ds(row * depth, depth), :]
                 rest = free * (load_row - force) - (1.0 - free) * disp_ref[comp, row]
                 value = rest * inverse
                 zero_ref[comp, row] = value
                 total = total + value * rest
-            return carried + jnp.where(own_row(row), total, 0.0)
+            return carried + total if own_row(row) else carried
 
         weight = apply_rows(
             0, span - 1, start_row, scale_row, emit_residual, above, below,
@@ -474,7 +473,7 @@
                 applied = free * force + (1.0 - free) * value
                 one_ref[comp, row] = applied * inverse
                 total = total + value * applied
-            return carried + jnp.where(own_row(row), total, 0.0)
+            return carried + total if own_row(row) else carried
 
         curve = apply_rows(
             1, span - 2, zero_row, scale_row, emit_one, above, below, jnp.zeros(plane, F32)

time: 69.3 us -> 64.4 us (0.929)
  local copies, waits for them, and re-layouts: 3.92 us -> 0.72 us
  Pallas kernels: 15 us -> 12 us
  waiting for transfers between devices: 16.8 us -> 18.3 us
    unnamed x17 -> x9, local copies, waits for them, and re-layouts: 3.92 us -> 0.72 us
    pallas_call x7, Pallas kernels: 15 us -> 12 us  [call(): pl.pallas_call(body, out_shape=outs, in_specs=[pl.BlockSpec(memory_space=...]
    all_to_all x2, waiting for transfers between devices: 16.8 us -> 18.3 us  [exchange(): lax.all_to_all(message.reshape(rows, 1, message.shape[1]), axes, split_ax...]
  transfers between devices with their start and end apart: 2 -> 2, of which waited for: 2 -> 2; matrix products, arithmetic and copies ran while one was open for 0% -> 0% of each run, Pallas kernels for 10% -> 8%
where the time goes in v3:
time: 64.4 us; the launch traced here: 63.9 us
  blocking collectives  21.1 us (33%)
  waiting for transfers between devices  18.3 us (28%)
  Pallas kernels  12 us (19%)
  starting transfers between devices  11.1 us (17%)
  local copies, waits for them, and re-layouts  0.72 us (1%)
  between operations  0.7 us (1%)
    all_to_all x2, blocking collectives, exchange(): lax.all_to_all(message.reshape(rows, 1, message.shape[1]), axes, split_ax...  21.1 us
    all_to_all x2, waiting for transfers between devices, exchange(): lax.all_to_all(message.reshape(rows, 1, message.shape[1]), axes, split_ax...  18.3 us
    pallas_call x7, Pallas kernels, call(): pl.pallas_call(body, out_shape=outs, in_specs=[pl.BlockSpec(memory_space=...  12 us
    all_to_all x2, starting transfers between devices, exchange(): lax.all_to_all(message.reshape(rows, 1, message.shape[1]), axes, split_ax...  11.1 us
  transfers between devices with their start and end apart: 2, of which 2 were waited for; matrix products, arithmetic and copies ran while one was open for 0% of the time, Pallas kernels for 8%

profile of v3, /device:TPU:0, one launch (start us, length us, event | category | flops | bytes accessed | tf_op | source)
XLA Modules:
  0.0 63.9 jit_solution(2472976675500102083)
XLA Ops:
  0.6 2.1 %pack.1 = f32[1312,128]{1,0:T(8,128)} custom-call(f32[2,3,1,64,128]{4,3,2,1,0:T(8,128)} %disp_ref.1, f32[1,64,128]{2,1,0:T(8,128)} %dens_ref.3, s32[1,64,128]{2,1,0:T(8,128)} %design_ref.7, s32[1,64,128]{2,1,0:T(8,128)} %support_ref.1), custom_call_target="tpu_custom_call" | custom-call | bytes 1048576 | tf_op jit(solution)/shard_map/pack/pallas_call | solution.py:274
  2.7 0.0 copy-start.3
  2.7 7.4 %all-to-all-start = ((f32[1312,1,128]{2,1,0:T(1,128)}), f32[1312,1,128]{2,1,0:T(1,128)S(1)}, u32[]{:S(2)}, u32[]{:S(2)}) async-start(f32[1312,1,128]{2,1,0:T(1,128)} %bitcast.1), calls=%async_computation | async-start | bytes 1343488 | tf_op jit(solution)/shard_map/all_to_all | solution.py:288
  10.1 0.0 copy-done.3
  10.1 0.0 copy-start.2
  10.2 0.7 %copy-done.2 = s32[2,2048]{1,0:T(2,128)S(1)} copy-done((s32[2,2048]{1,0:T(2,128)S(1)}, s32[2,2048]{1,0:T(2,128)}, u32[]{:S(2)}) %copy-start.2) | copy-done | bytes 16408
  10.9 0.0 copy-start
  10.9 4.2 %point_loads.1.rhs_ref = f32[3,208,128]{2,1,0:T(8,128)S(1)} custom-call(s32[2,2048]{1,0:T(2,128)S(1)} %copy-done.2, f32[2,3,2048]{2,1,0:T(4,128)S(1)} %copy.10.forces_ref), custom_call_target="tpu_custom_call" | custom-call | flops 268435456 | bytes 1048576 | tf_op jit(solution)/shard_map/point_loads/pallas_call | solution.py:274
  15.0 12.8 %all-to-all-done = f32[1312,1,128]{2,1,0:T(1,128)S(1)} async-done(((f32[1312,1,128]{2,1,0:T(1,128)}), f32[1312,1,128]{2,1,0:T(1,128)S(1)}, u32[]{:S(2)}, u32[]{:S(2)}) %all-to-all-start) | async-done | bytes 671776 | tf_op jit(solution)/shard_map/all_to_all | solution.py:288
  27.8 0.0 copy-done
  27.8 2.3 %residual.1 = (f32[3,25,8,128]{3,2,1,0:T(8,128)S(1)}, f32[1,25,8,128]{3,2,1,0:T(8,128)S(1)}, f32[3,25,8,128]{3,2,1,0:T(8,128)S(1)}, f32[3,25,8,128]{3,2,1,0:T(8,...) custom-call(f32[1312,128]{1,0:T(8,128)S(1)} %bitcast.16, ...), custom_call_target="tpu_custom_call" | custom-call | flops 67108864 | bytes 1048576 | tf_op jit(solution)/shard_map/residual/pallas_call | solution.py:274
  30.1 3.6 %all-to-all-start.1 = ((f32[88,1,128]{2,1,0:T(1,128)}), f32[88,1,128]{2,1,0:T(1,128)S(1)}, u32[]{:S(2)}, u32[]{:S(2)}) async-start(f32[88,1,128]{2,1,0:T(1,128)} %bitcast.4), calls=%async_computation.1 | async-start | bytes 90112 | tf_op jit(solution)/shard_map/all_to_all | solution.py:288
  33.8 1.3 %powers.1 = (f32[3,25,8,128]{3,2,1,0:T(8,128)S(1)}, f32[3,25,8,128]{3,2,1,0:T(8,128)S(1)}) custom-call(f32[3,25,8,128]{3,2,1,0:T(8,128)S(1)} %get-tuple-element.19.geo_ref, f32[3,25,8,128]{3,2,1,0:T(8,128)S(1)} %get-tuple-element.21.one_ref), custom_call_target="tpu_custom_call" | custom-call | flops 67108864 | bytes 1048576 | tf_op jit(solution)/shard_map/powers/pallas_call | solution.py:274
  35.0 5.5 %all-to-all-done.1 = f32[88,1,128]{2,1,0:T(1,128)S(1)} async-done(((f32[88,1,128]{2,1,0:T(1,128)}), f32[88,1,128]{2,1,0:T(1,128)S(1)}, u32[]{:S(2)}, u32[]{:S(2)}) %all-to-all-start.1) | async-done | bytes 45088 | tf_op jit(solution)/shard_map/all_to_all | solution.py:288
  40.5 1.1 %energy.1 = (f32[392,128]{1,0:T(8,128)S(1)}, f32[288,128]{1,0:T(8,128)S(1)}, f32[8,128]{1,0:T(8,128)S(1)}) custom-call(f32[88,128]{1,0:T(8,128)S(1)} %bitcast.20, f32[3,25,8,128]{3,2,1,0:T(8,128)S(1)} %get-tuple-element.17.disp_ref, f32[1,25,8,128]{3,2,1,0:T(8,128)S(1)} %get-tuple-element.18.cube_ref, f32[3,25,8,128]{3,2,1,0:T(8,128)S(1)} %get-tuple-element.19.geo_ref, ...), custom_call_target="tpu_custom_call" | custom-call | flops 16777216 | bytes 1048576 | tf_op jit(solution)/shard_map/energy/pallas_call | solution.py:274
  41.6 0.0 copy-start.1
  41.6 9.7 %all_to_all.20 = f32[288,1,128]{2,1,0:T(1,128)S(1)} all-to-all(f32[288,1,128]{2,1,0:T(1,128)S(1)} %bitcast.21), channel_id=1, replica_groups=mesh['slab'=8,'load'=4] {'load','slab'}, dimensions={0} | all-to-all | bytes 294912 | tf_op jit(solution)/shard_map/all_to_all | solution.py:288
  51.3 0.0 copy-done.1
  51.3 0.3 trial.1
  51.6 11.5 %all_to_all.21 = f32[392,1,128]{2,1,0:T(1,128)S(1)} all-to-all(f32[392,1,128]{2,1,0:T(1,128)S(1)} %bitcast.19), channel_id=1, replica_groups=mesh['slab'=8,'load'=4] {'slab'}, dimensions={0} | all-to-all | bytes 401408 | tf_op jit(solution)/shard_map/all_to_all | solution.py:288
  63.1 0.8 %final.1 = (f32[2,3,1,64,128]{4,3,2,1,0:T(8,128)}, f32[1,64,128]{2,1,0:T(8,128)}) custom-call(f32[392,128]{1,0:T(8,128)S(1)} %bitcast.17, f32[64,128]{1,0:T(8,128)S(1)} %get-tuple-element.29.trial_ref, s32[1,64,128]{2,1,0:T(8,128)S(1)} %copy-done, f32[8,128]{1,0:T(8,128)S(1)} %get-tuple-element.26.count_ref), custom_call_target="tpu_custom_call" | custom-call | bytes 1048576 | tf_op jit(solution)/shard_map/final/pallas_call | solution.py:274
  (1 shorter events, 0.0 us)
Async XLA Ops:
  2.7 7.4 %copy-start.3 = (f32[2,3,2048]{2,0,1:T(2,128)S(1)}, f32[2,3,2048]{2,0,1:T(2,128)}, u32[]{:S(2)}) copy-start(f32[2,3,2048]{2,0,1:T(2,128)} %param.11) | copy-start | bytes 147460
  2.7 25.1 %all-to-all-start = ((f32[1312,1,128]{2,1,0:T(1,128)}), f32[1312,1,128]{2,1,0:T(1,128)S(1)}, u32[]{:S(2)}, u32[]{:S(2)}) async-start(f32[1312,1,128]{2,1,0:T(1,128)} %bitcast.1), calls=%async_computation | async-start | bytes 1343488 | tf_op jit(solution)/shard_map/all_to_all | solution.py:288
  10.1 0.7 %copy-start.2 = (s32[2,2048]{1,0:T(2,128)S(1)}, s32[2,2048]{1,0:T(2,128)}, u32[]{:S(2)}) copy-start(s32[2,2048]{1,0:T(2,128)} %nodes_ref.1) | copy-start | bytes 49156
  10.9 16.9 %copy-start = (s32[1,64,128]{2,1,0:T(8,128)S(1)}, s32[1,64,128]{2,1,0:T(8,128)}, u32[]{:S(2)}) copy-start(s32[1,64,128]{2,1,0:T(8,128)} %design_ref.7) | copy-start | bytes 98308
  30.1 10.4 %all-to-all-start.1 = ((f32[88,1,128]{2,1,0:T(1,128)}), f32[88,1,128]{2,1,0:T(1,128)S(1)}, u32[]{:S(2)}, u32[]{:S(2)}) async-start(f32[88,1,128]{2,1,0:T(1,128)} %bitcast.4), calls=%async_computation.1 | async-start | bytes 90112 | tf_op jit(solution)/shard_map/all_to_all | solution.py:288
  41.6 9.7 %copy-start.1 = (f32[1,64,128]{2,1,0:T(8,128)S(1)}, f32[1,64,128]{2,1,0:T(8,128)}, u32[]{:S(2)}) copy-start(f32[1,64,128]{2,1,0:T(8,128)} %dens_ref.3) | copy-start | bytes 98308

commit v4 on v3

--- a/solution.py
+++ b/solution.py
@@ -16,7 +16,6 @@
 MOVE_LIMIT = 0.2
 VOLUME_TARGET = 0.5
 EPSILON = 1e-06
-HIGHEST = lax.Precision.HIGHEST
 F32 = jnp.float32
 
 HALO_LOW = 4
@@ -243,22 +242,9 @@
         here, there = split_forces(forces)
         return high, {key: pending[key] + here[key] for key in ROW_KEYS}, there
 
-    def pack(low, pending):
-        return tuple(low[key] for key in ROW_KEYS) + tuple(pending[key] for key in ROW_KEYS)
-
-    def unpack(state):
-        count = len(ROW_KEYS)
-        return dict(zip(ROW_KEYS, state[:count])), dict(zip(ROW_KEYS, state[count:]))
-
     low = row_modes(load_row(first), above)
     zero = {key: jnp.zeros_like(low[key]) for key in ROW_KEYS}
     low, _, pending = advance(first, low, zero)
-
-    def step(index, state):
-        carried, (low, pending) = state[0], unpack(state[1])
-        low, modes, pending = advance(index, low, pending)
-        carried = emit(index, node_forces(modes, below), carried)
-        return carried, pack(low, pending)
 
     for index in range(first + 1, last):
         low, modes, pending = advance(index, low, pending)
@@ -266,8 +252,45 @@
     return carry
 
 
-def dot(left, right):
-    return jnp.dot(left, right, precision=HIGHEST, preferred_element_type=F32)
+def dot(left, right, turned=False):
+    dims = (((1,), (1 if turned else 0,)), ((), ()))
+
+    def halves(value):
+        high = value.astype(jnp.bfloat16)
+        return high, (value - high.astype(F32)).astype(jnp.bfloat16)
+
+    def product(a, b):
+        return lax.dot_general(a, b, dims, preferred_element_type=F32)
+
+    left_high, left_low = halves(left)
+    right_high, right_low = halves(right)
+    return product(left_high, right_high) + (
+        product(left_high, right_low) + product(left_low, right_high)
+    )
+
+
+def swap_blocks(values, block):
+    values = list(values)
+    lanes = values[0].shape[1]
+    place = iota(values[0].shape, 1) // block
+    bit = 1
+    while bit < len(values):
+        lower = (place & bit) == 0
+        for index in range(len(values)):
+            if not index & bit:
+                low, high = values[index], values[index + bit]
+                values[index] = jnp.where(lower, low, pltpu.roll(high, bit * block, 1))
+                values[index + bit] = jnp.where(
+                    lower, pltpu.roll(low, lanes - bit * block, 1), high
+                )
+        bit *= 2
+    return values
+
+
+def depth_table(depth, inner):
+    shape = (depth * inner, depth * inner)
+    to, source = iota(shape, 0), iota(shape, 1)
+    return jnp.where(to % inner == source % inner, gauss(to // inner - source // inner), 0.0)
 
 
 def call(body, outs, *args, scratch=(), name=None, flops=0, space=pltpu.VMEM):
@@ -299,10 +322,10 @@
     strip = cols_y // slabs
     span = strip + HALO
     width = loads * rows_x
-    half = strip * rows_x // width
+    half = rows_x // slabs
     plane = (depth, width)
-    in_rows = (comps + 1) * span + rows_x
-    sum_rows = 3 + half
+    in_rows = (comps + 1) * span + 2 * half
+    sum_rows = 3 + 2 * half
     numer_rows = half + 1
     out_rows = comps * strip + 1
     block = lambda count: jax.ShapeDtypeStruct((count, span) + plane, F32)
@@ -337,6 +360,7 @@
             )
         for copy in copies[:3]:
             copy.wait()
+        spread = dot(gauss_table(rows_x), dens_in[...])
         solid = design_in[...].astype(F32) * dens_in[...]
         both = jnp.concatenate([solid * solid * solid, support_in[...].astype(F32)], 0)
         pad_ref[comps, HALO_LOW : HALO_LOW + cols_y] = both.T
@@ -350,7 +374,10 @@
                 out_ref[base + field * span : base + (field + 1) * span] = pad_ref[
                     field, target * strip : target * strip + span
                 ]
-            out_ref[base + (comps + 1) * span : base + in_rows] = dens_in[...]
+            rows = slice(target * half, (target + 1) * half)
+            base = base + (comps + 1) * span
+            out_ref[base : base + half] = spread[rows]
+            out_ref[base + half : base + 2 * half] = design_in[rows].astype(F32)
 
     message = call(
         pack_body,
@@ -410,13 +437,8 @@
     def own_row(row):
         return (row >= HALO_LOW) & (row < HALO_LOW + strip)
 
-    def packed_table(part):
-        shape = (slabs * half, cols_y)
-        row = iota(shape, 0)
-        return gauss(row // half * strip + part * half + row % half - iota(shape, 1))
-
     def residual_body(
-        in_ref, rhs_ref, design_ref, disp_ref, cube_ref, geo_ref, zero_ref, one_ref, dens_ref, sum_ref
+        in_ref, rhs_ref, disp_ref, cube_ref, geo_ref, zero_ref, one_ref, sum_ref
     ):
         above, below = shifts(plane, rows_x)
         cube_side = iota(plane, 1) < rows_x
@@ -479,19 +501,23 @@
             1, span - 2, zero_row, scale_row, emit_one, above, below, jnp.zeros(plane, F32)
         )
 
-        here = lax.axis_index("slab")
-        mixed = jnp.zeros((rows_x, cols_y), F32)
-        for layer in range(depth):
-            weight_z = gauss(jnp.full((1, cols_y), here - layer, jnp.int32))
-            base = layer * in_rows + (comps + 1) * span
-            mixed = mixed + weight_z * in_ref[base : base + rows_x]
-        mixed = dot(gauss_table(rows_x), mixed)
-        filtered = dot(mixed, gauss_table(cols_y))
-        dens_ref[...] = filtered
-        mask = design_ref[0].astype(F32)
-        share = (mask / filtered).T
-        share = jnp.concatenate(
-            [dot(packed_table(part), share) for part in range(strip // half)], 1
+        def gather(offset):
+            offset = offset + (comps + 1) * span
+            return jnp.concatenate(
+                [
+                    in_ref[layer * in_rows + offset : layer * in_rows + offset + half]
+                    for layer in range(depth)
+                ],
+                0,
+            )
+
+        table_z = depth_table(depth, half)
+        table_y = gauss_table(cols_y)
+        mask = gather(half)
+        filtered = dot(table_z, dot(gather(0), table_y))
+        share = dot(table_z, dot(mask / filtered, table_y))
+        share = swap_blocks(
+            [share[layer * half : (layer + 1) * half] for layer in range(depth)], strip
         )
         down = lambda value: jnp.sum(value, 0, keepdims=True)
         sums = [down(curve), down(weight), down(mask)]
@@ -499,9 +525,12 @@
             base = target * sum_rows
             for index, value in enumerate(sums):
                 sum_ref[base + index : base + index + 1] = value
-            sum_ref[base + 3 : base + sum_rows] = share[target * half : (target + 1) * half]
-
-    disp, cube, geometry, zeroth, first, dens_filtered, sums = call(
+            sum_ref[base + 3 : base + 3 + half] = share[target]
+            sum_ref[base + 3 + half : base + sum_rows] = filtered[
+                target * half : (target + 1) * half
+            ]
+
+    disp, cube, geometry, zeroth, first, sums = call(
         residual_body,
         (
             block(comps),
@@ -509,12 +538,10 @@
             block(3),
             block(comps),
             block(comps),
-            flat(rows_x),
             flat(slabs * sum_rows),
         ),
         received,
         right_side,
-        design,
         name="residual",
         flops=1 << 26,
     )
@@ -588,41 +615,32 @@
                 values.append(free * value)
             modes = row_modes(values, above)
             if lower is not None:
-                weak_ref[(row - 1 - HALO_LOW) * depth : (row - HALO_LOW) * depth] = (
+                weak_ref[pl.ds(row - 1 - HALO_LOW, depth, stride=strip), :] = (
                     (3.0 * (1.0 - STIFF_VOID))
                     * cube_ref[0, row - 1]
                     * element_energy(element_modes(lower, modes))
                 )
             lower = modes
         disp_out_ref[pl.ds(out_rows - 1, depth, stride=out_rows), :] = jnp.zeros(plane, F32)
-        weak = weak_ref[...]
-        smooth = jnp.zeros((depth * half, width), F32)
-        for part in range(strip // half):
-            shape = (depth * half, strip * depth)
-            to, source = iota(shape, 0), iota(shape, 1)
-            table = jnp.where(
-                to % half + part * half == source // depth,
-                gauss(to // half - source % depth),
-                0.0,
+        shape = (rows_x, width)
+        table_x = gauss(iota(shape, 0) - iota(shape, 1) % rows_x)
+        across_x = dot(table_x, weak_ref[...], turned=True)
+        smooth = dot(across_x, depth_table(depth, strip))
+        weighted = jnp.zeros((1, width), F32)
+        for source in range(slabs):
+            base = source * sum_rows + 3
+            weighted = weighted + jnp.sum(
+                across_x[source * half : (source + 1) * half] * sums_ref[base : base + half],
+                0,
+                keepdims=True,
             )
-            shape = (width, width)
-            to, source = iota(shape, 1), iota(shape, 0)
-            table_x = jnp.where(
-                to // rows_x == part, gauss(to % rows_x - source % rows_x), 0.0
-            )
-            smooth = smooth + dot(dot(table, weak), table_x)
-        weighted = jnp.zeros((1, width), F32)
+        pieces = swap_blocks(
+            [smooth[index * half : (index + 1) * half] for index in range(slabs)], strip
+        )
         for layer in range(depth):
-            piece = smooth[layer * half : (layer + 1) * half]
-            base = layer * sum_rows
-            weighted = weighted + jnp.sum(
-                piece * sums_ref[base + 3 : base + sum_rows], 0, keepdims=True
-            )
-        for layer in range(depth):
-            piece = smooth[layer * half : (layer + 1) * half]
             for part in range(parts):
                 base = (part * slabs + layer) * numer_rows
-                numer_ref[base : base + half] = piece
+                numer_ref[base : base + half] = pieces[layer]
                 numer_ref[base + half : base + numer_rows] = weighted
 
     disp_message, numer_message, count = call(
@@ -643,24 +661,24 @@
     numer_pieces = exchange(numer_message, ("load", "slab"))
 
     def trial_body(
-        numer_ref, dens_ref, filtered_ref, design_ref, count_ref, disp_ref, trial_ref, out_ref, plane_ref
+        numer_ref, dens_ref, sums_ref, design_ref, count_ref, disp_ref, trial_ref, out_ref,
+        plane_ref, filtered_ref,
     ):
         weighted = jnp.zeros((1, width), F32)
+        totals = []
         for source in range(slabs):
             total = jnp.zeros((half, width), F32)
             for part in range(parts):
                 base = (part * slabs + source) * numer_rows
                 total = total + numer_ref[base : base + half]
                 weighted = weighted + numer_ref[base + half : base + numer_rows]
-            plane_ref[source * half : (source + 1) * half] = total
+            totals.append(total)
+            base = source * sum_rows + 3 + half
+            filtered_ref[source * half : (source + 1) * half] = sums_ref[base : base + half]
+        for index, value in enumerate(swap_blocks(totals, strip)):
+            plane_ref[index * half : (index + 1) * half] = value
         mean = jnp.sum(weighted, 1, keepdims=True) / count_ref[0:1] + EPSILON
-        packed = plane_ref[...].T
-        numer = jnp.zeros((rows_x, cols_y), F32)
-        for part in range(strip // half):
-            shape = (slabs * half, cols_y)
-            row = iota(shape, 0)
-            table = gauss(row // half * strip + part * half + row % half - iota(shape, 1))
-            numer = numer + dot(packed[part * rows_x : (part + 1) * rows_x], table)
+        numer = dot(plane_ref[...], gauss_table(cols_y))
         mask = design_ref[0].astype(F32)
         dens = dens_ref[0]
         ratio = mask * (numer / filtered_ref[...]) / mean
@@ -677,11 +695,11 @@
         (flat(rows_x), flat(slabs * out_rows)),
         numer_pieces,
         density,
-        dens_filtered,
+        all_sums,
         design,
         count,
         disp_message,
-        scratch=[pltpu.VMEM((slabs * half, width), F32)],
+        scratch=[pltpu.VMEM((rows_x, cols_y), F32)] * 2,
         name="trial",
     )
     out_pieces = exchange(out_message, "slab")

time: 64.4 us -> 60.7 us (0.943)
  waiting for transfers between devices: 18.3 us -> 14.3 us
    all_to_all x2, waiting for transfers between devices: 18.3 us -> 14.3 us  [exchange(): lax.all_to_all(message.reshape(rows, 1, message.shape[1]), axes, split_ax...]
  transfers between devices with their start and end apart: 2 -> 2, of which waited for: 2 -> 2; matrix products, arithmetic and copies ran while one was open for 0% -> 0% of each run, Pallas kernels for 8% -> 9%
where the time goes in v4:
time: 60.7 us; the launch traced here: 60.2 us
  blocking collectives  21.3 us (35%)
  waiting for transfers between devices  14.3 us (24%)
  Pallas kernels  12.1 us (20%)
  starting transfers between devices  11.1 us (18%)
  local copies, waits for them, and re-layouts  0.72 us (1%)
  between operations  0.71 us (1%)
    all_to_all x2, blocking collectives, exchange(): lax.all_to_all(message.reshape(rows, 1, message.shape[1]), axes, split_ax...  21.3 us
    all_to_all x2, waiting for transfers between devices, exchange(): lax.all_to_all(message.reshape(rows, 1, message.shape[1]), axes, split_ax...  14.3 us
    pallas_call x7, Pallas kernels, call(): pl.pallas_call(body, out_shape=outs, in_specs=[pl.BlockSpec(memory_space=...  12.1 us
    all_to_all x2, starting transfers between devices, exchange(): lax.all_to_all(message.reshape(rows, 1, message.shape[1]), axes, split_ax...  11.1 us
  transfers between devices with their start and end apart: 2, of which 2 were waited for; matrix products, arithmetic and copies ran while one was open for 0% of the time, Pallas kernels for 9%

profile of v4, /device:TPU:0, one launch (start us, length us, event | category | flops | bytes accessed | tf_op | source)
XLA Modules:
  0.0 60.2 jit_solution(5978624081417140278)
XLA Ops:
  0.6 2.0 %pack.1 = f32[928,128]{1,0:T(8,128)} custom-call(f32[2,3,1,64,128]{4,3,2,1,0:T(8,128)} %disp_ref.1, f32[1,64,128]{2,1,0:T(8,128)} %dens_ref.3, s32[1,64,128]{2,1,0:T(8,128)} %design_ref.5, s32[1,64,128]{2,1,0:T(8,128)} %support_ref.1), custom_call_target="tpu_custom_call" | custom-call | bytes 1048576 | tf_op jit(solution)/shard_map/pack/pallas_call | solution.py:297
  2.6 0.0 copy-start.3
  2.6 7.4 %all-to-all-start = ((f32[928,1,128]{2,1,0:T(1,128)}), f32[928,1,128]{2,1,0:T(1,128)S(1)}, u32[]{:S(2)}, u32[]{:S(2)}) async-start(f32[928,1,128]{2,1,0:T(1,128)} %bitcast.1), calls=%async_computation | async-start | bytes 950272 | tf_op jit(solution)/shard_map/all_to_all | solution.py:311
  10.1 0.0 copy-done.3
  10.1 0.0 copy-start.2
  10.1 0.7 %copy-done.2 = s32[2,2048]{1,0:T(2,128)S(1)} copy-done((s32[2,2048]{1,0:T(2,128)S(1)}, s32[2,2048]{1,0:T(2,128)}, u32[]{:S(2)}) %copy-start.2) | copy-done | bytes 16408
  10.8 4.1 %point_loads.1.rhs_ref = f32[3,208,128]{2,1,0:T(8,128)S(1)} custom-call(s32[2,2048]{1,0:T(2,128)S(1)} %copy-done.2, f32[2,3,2048]{2,1,0:T(4,128)S(1)} %copy.10.forces_ref), custom_call_target="tpu_custom_call" | custom-call | flops 268435456 | bytes 1048576 | tf_op jit(solution)/shard_map/point_loads/pallas_call | solution.py:297
  15.0 8.5 %all-to-all-done = f32[928,1,128]{2,1,0:T(1,128)S(1)} async-done(((f32[928,1,128]{2,1,0:T(1,128)}), f32[928,1,128]{2,1,0:T(1,128)S(1)}, u32[]{:S(2)}, u32[]{:S(2)}) %all-to-all-start) | async-done | bytes 475168 | tf_op jit(solution)/shard_map/all_to_all | solution.py:311
  23.5 2.5 %residual.1 = (f32[3,25,8,128]{3,2,1,0:T(8,128)S(1)}, f32[1,25,8,128]{3,2,1,0:T(8,128)S(1)}, f32[3,25,8,128]{3,2,1,0:T(8,128)S(1)}, f32[3,25,8,128]{3,2,1,0:T(8,...) custom-call(f32[928,128]{1,0:T(8,128)S(1)} %bitcast.16, f32[3,208,128]{2,1,0:T(8,128)S(1)} %point_loads.1.rhs_ref), custom_call_target="tpu_custom_call" | custom-call | flops 67108864 | bytes 1048576 | tf_op jit(solution)/shard_map/residual/pallas_call | solution.py:297
  26.0 3.6 %all-to-all-start.1 = ((f32[152,1,128]{2,1,0:T(1,128)}), f32[152,1,128]{2,1,0:T(1,128)S(1)}, u32[]{:S(2)}, u32[]{:S(2)}) async-start(f32[152,1,128]{2,1,0:T(1,128)} %bitcast.4), calls=%async_computation.1 | async-start | bytes 155648 | tf_op jit(solution)/shard_map/all_to_all | solution.py:311
  29.7 1.3 %powers.1 = (f32[3,25,8,128]{3,2,1,0:T(8,128)S(1)}, f32[3,25,8,128]{3,2,1,0:T(8,128)S(1)}) custom-call(f32[3,25,8,128]{3,2,1,0:T(8,128)S(1)} %get-tuple-element.18.geo_ref, f32[3,25,8,128]{3,2,1,0:T(8,128)S(1)} %get-tuple-element.20.one_ref), custom_call_target="tpu_custom_call" | custom-call | flops 67108864 | bytes 1048576 | tf_op jit(solution)/shard_map/powers/pallas_call | solution.py:297
  30.9 5.7 %all-to-all-done.1 = f32[152,1,128]{2,1,0:T(1,128)S(1)} async-done(((f32[152,1,128]{2,1,0:T(1,128)}), f32[152,1,128]{2,1,0:T(1,128)S(1)}, u32[]{:S(2)}, u32[]{:S(2)}) %all-to-all-start.1) | async-done | bytes 77856 | tf_op jit(solution)/shard_map/all_to_all | solution.py:311
  36.6 1.0 %energy.1 = (f32[392,128]{1,0:T(8,128)S(1)}, f32[288,128]{1,0:T(8,128)S(1)}, f32[8,128]{1,0:T(8,128)S(1)}) custom-call(f32[152,128]{1,0:T(8,128)S(1)} %bitcast.18, f32[3,25,8,128]{3,2,1,0:T(8,128)S(1)} %get-tuple-element.16.disp_ref, f32[1,25,8,128]{3,2,1,0:T(8,128)S(1)} %get-tuple-element.17.cube_ref, f32[3,25,8,128]{3,2,1,0:T(8,128)S(1)} %get-tuple-element.18.geo_ref, ...), custom_call_target="tpu_custom_call" | custom-call | flops 16777216 | bytes 1048576 | tf_op jit(solution)/shard_map/energy/pallas_call | solution.py:297
  37.7 0.0 copy-start
  37.7 0.0 copy-start.1
  37.7 9.8 %all_to_all.20 = f32[288,1,128]{2,1,0:T(1,128)S(1)} all-to-all(f32[288,1,128]{2,1,0:T(1,128)S(1)} %bitcast.22), channel_id=1, replica_groups=mesh['slab'=8,'load'=4] {'load','slab'}, dimensions={0} | all-to-all | bytes 294912 | tf_op jit(solution)/shard_map/all_to_all | solution.py:311
  47.5 0.0 copy-done
  47.5 0.0 copy-done.1
  47.5 0.4 trial.1
  47.9 11.5 %all_to_all.21 = f32[392,1,128]{2,1,0:T(1,128)S(1)} all-to-all(f32[392,1,128]{2,1,0:T(1,128)S(1)} %bitcast.21), channel_id=1, replica_groups=mesh['slab'=8,'load'=4] {'slab'}, dimensions={0} | all-to-all | bytes 401408 | tf_op jit(solution)/shard_map/all_to_all | solution.py:311
  59.4 0.8 %final.1 = (f32[2,3,1,64,128]{4,3,2,1,0:T(8,128)}, f32[1,64,128]{2,1,0:T(8,128)}) custom-call(f32[392,128]{1,0:T(8,128)S(1)} %bitcast.17, f32[64,128]{1,0:T(8,128)S(1)} %get-tuple-element.27.trial_ref, s32[1,64,128]{2,1,0:T(8,128)S(1)} %copy-done, f32[8,128]{1,0:T(8,128)S(1)} %get-tuple-element.24.count_ref), custom_call_target="tpu_custom_call" | custom-call | bytes 1048576 | tf_op jit(solution)/shard_map/final/pallas_call | solution.py:297
  (1 shorter events, 0.0 us)
Async XLA Ops:
  2.6 7.4 %copy-start.3 = (f32[2,3,2048]{2,0,1:T(2,128)S(1)}, f32[2,3,2048]{2,0,1:T(2,128)}, u32[]{:S(2)}) copy-start(f32[2,3,2048]{2,0,1:T(2,128)} %param.11) | copy-start | bytes 147460
  2.6 20.9 %all-to-all-start = ((f32[928,1,128]{2,1,0:T(1,128)}), f32[928,1,128]{2,1,0:T(1,128)S(1)}, u32[]{:S(2)}, u32[]{:S(2)}) async-start(f32[928,1,128]{2,1,0:T(1,128)} %bitcast.1), calls=%async_computation | async-start | bytes 950272 | tf_op jit(solution)/shard_map/all_to_all | solution.py:311
  10.1 0.7 %copy-start.2 = (s32[2,2048]{1,0:T(2,128)S(1)}, s32[2,2048]{1,0:T(2,128)}, u32[]{:S(2)}) copy-start(s32[2,2048]{1,0:T(2,128)} %nodes_ref.1) | copy-start | bytes 49156
  26.0 10.6 %all-to-all-start.1 = ((f32[152,1,128]{2,1,0:T(1,128)}), f32[152,1,128]{2,1,0:T(1,128)S(1)}, u32[]{:S(2)}, u32[]{:S(2)}) async-start(f32[152,1,128]{2,1,0:T(1,128)} %bitcast.4), calls=%async_computation.1 | async-start | bytes 155648 | tf_op jit(solution)/shard_map/all_to_all | solution.py:311
  37.7 9.8 %copy-start = (s32[1,64,128]{2,1,0:T(8,128)S(1)}, s32[1,64,128]{2,1,0:T(8,128)}, u32[]{:S(2)}) copy-start(s32[1,64,128]{2,1,0:T(8,128)} %design_ref.5) | copy-start | bytes 98308
  37.7 9.8 %copy-start.1 = (f32[1,64,128]{2,1,0:T(8,128)S(1)}, f32[1,64,128]{2,1,0:T(8,128)}, u32[]{:S(2)}) copy-start(f32[1,64,128]{2,1,0:T(8,128)} %dens_ref.3) | copy-start | bytes 98308

commit v5 on v4

--- a/solution.py
+++ b/solution.py
@@ -293,7 +293,7 @@
     return jnp.where(to % inner == source % inner, gauss(to // inner - source // inner), 0.0)
 
 
-def call(body, outs, *args, scratch=(), name=None, flops=0, space=pltpu.VMEM):
+def call(body, outs, *args, scratch=(), name=None, flops=0, space=pltpu.VMEM, aliases=None):
     return pl.pallas_call(
         body,
         out_shape=outs,
@@ -302,6 +302,7 @@
         scratch_shapes=list(scratch),
         compiler_params=pltpu.CompilerParams(vmem_limit_bytes=VMEM_LIMIT),
         cost_estimate=pl.CostEstimate(flops=flops, bytes_accessed=1 << 20, transcendentals=0),
+        input_output_aliases=aliases or {},
         name=name,
     )(*args)
 
@@ -441,6 +442,24 @@
         in_ref, rhs_ref, disp_ref, cube_ref, geo_ref, zero_ref, one_ref, sum_ref
     ):
         above, below = shifts(plane, rows_x)
+        def gather(offset):
+            offset = offset + (comps + 1) * span
+            return jnp.concatenate(
+                [
+                    in_ref[layer * in_rows + offset : layer * in_rows + offset + half]
+                    for layer in range(depth)
+                ],
+                0,
+            )
+
+        table_z = depth_table(depth, half)
+        table_y = gauss_table(cols_y)
+        mask = gather(half)
+        filtered = dot(table_z, dot(gather(0), table_y))
+        share = dot(table_z, dot(mask / filtered, table_y))
+        share = swap_blocks(
+            [share[layer * half : (layer + 1) * half] for layer in range(depth)], strip
+        )
         cube_side = iota(plane, 1) < rows_x
         for row in range(span):
             pick = lambda field: in_ref[pl.ds(field * span + row, depth, stride=in_rows), :]
@@ -501,24 +520,6 @@
             1, span - 2, zero_row, scale_row, emit_one, above, below, jnp.zeros(plane, F32)
         )
 
-        def gather(offset):
-            offset = offset + (comps + 1) * span
-            return jnp.concatenate(
-                [
-                    in_ref[layer * in_rows + offset : layer * in_rows + offset + half]
-                    for layer in range(depth)
-                ],
-                0,
-            )
-
-        table_z = depth_table(depth, half)
-        table_y = gauss_table(cols_y)
-        mask = gather(half)
-        filtered = dot(table_z, dot(gather(0), table_y))
-        share = dot(table_z, dot(mask / filtered, table_y))
-        share = swap_blocks(
-            [share[layer * half : (layer + 1) * half] for layer in range(depth)], strip
-        )
         down = lambda value: jnp.sum(value, 0, keepdims=True)
         sums = [down(curve), down(weight), down(mask)]
         for target in range(slabs):
@@ -624,8 +625,11 @@
         disp_out_ref[pl.ds(out_rows - 1, depth, stride=out_rows), :] = jnp.zeros(plane, F32)
         shape = (rows_x, width)
         table_x = gauss(iota(shape, 0) - iota(shape, 1) % rows_x)
-        across_x = dot(table_x, weak_ref[...], turned=True)
-        smooth = dot(across_x, depth_table(depth, strip))
+        weak = weak_ref[...]
+        across_x = dot(table_x, weak, turned=True)
+        shape = (width, width)
+        table_x = gauss(iota(shape, 0) % rows_x - iota(shape, 1) % rows_x)
+        smooth = dot(depth_table(depth, strip), dot(weak, table_x))
         weighted = jnp.zeros((1, width), F32)
         for source in range(slabs):
             base = source * sum_rows + 3
@@ -634,13 +638,15 @@
                 0,
                 keepdims=True,
             )
-        pieces = swap_blocks(
-            [smooth[index * half : (index + 1) * half] for index in range(slabs)], strip
-        )
+        block_of = iota((half, width), 1) // rows_x
         for layer in range(depth):
+            piece = smooth[layer * strip : layer * strip + half]
+            for block_at in range(1, strip // half):
+                rows = layer * strip + block_at * half
+                piece = jnp.where(block_of == block_at, smooth[rows : rows + half], piece)
             for part in range(parts):
                 base = (part * slabs + layer) * numer_rows
-                numer_ref[base : base + half] = pieces[layer]
+                numer_ref[base : base + half] = piece
                 numer_ref[base + half : base + numer_rows] = weighted
 
     disp_message, numer_message, count = call(
@@ -665,26 +671,28 @@
         plane_ref, filtered_ref,
     ):
         weighted = jnp.zeros((1, width), F32)
-        totals = []
         for source in range(slabs):
             total = jnp.zeros((half, width), F32)
             for part in range(parts):
                 base = (part * slabs + source) * numer_rows
                 total = total + numer_ref[base : base + half]
                 weighted = weighted + numer_ref[base + half : base + numer_rows]
-            totals.append(total)
             base = source * sum_rows + 3 + half
             filtered_ref[source * half : (source + 1) * half] = sums_ref[base : base + half]
-        for index, value in enumerate(swap_blocks(totals, strip)):
-            plane_ref[index * half : (index + 1) * half] = value
+            plane_ref[source * half : (source + 1) * half] = total
         mean = jnp.sum(weighted, 1, keepdims=True) / count_ref[0:1] + EPSILON
-        numer = dot(plane_ref[...], gauss_table(cols_y))
+        packed = plane_ref[...].T
+        numer = 0.0
+        for block_at in range(strip // half):
+            shape = (slabs * half, cols_y)
+            row = iota(shape, 0)
+            table = gauss(row // half * strip + block_at * half + row % half - iota(shape, 1))
+            numer = numer + dot(packed[block_at * rows_x : (block_at + 1) * rows_x], table)
         mask = design_ref[0].astype(F32)
         dens = dens_ref[0]
         ratio = mask * (numer / filtered_ref[...]) / mean
         trial = jnp.clip(dens * jnp.sqrt(ratio), dens - MOVE_LIMIT, dens + MOVE_LIMIT)
         trial_ref[...] = trial
-        out_ref[...] = disp_ref[...]
         volume = jnp.sum(mask * trial, 0, keepdims=True)
         for target in range(slabs):
             base = (target + 1) * out_rows - 1
@@ -701,6 +709,7 @@
         disp_message,
         scratch=[pltpu.VMEM((rows_x, cols_y), F32)] * 2,
         name="trial",
+        aliases={5: 1},
     )
     out_pieces = exchange(out_message, "slab")
 

time: 60.7 us -> 60.2 us (level)
  no operation moved by 1% of the time
where the time goes in v5:
time: 60.2 us; the launch traced here: 59.7 us
  blocking collectives  21.3 us (35%)
  waiting for transfers between devices  14.3 us (24%)
  Pallas kernels  11.7 us (19%)
  starting transfers between devices  11.1 us (18%)
  local copies, waits for them, and re-layouts  0.72 us (1%)
  between operations  0.71 us (1%)
    all_to_all x2, blocking collectives, exchange(): lax.all_to_all(message.reshape(rows, 1, message.shape[1]), axes, split_ax...  21.3 us
    all_to_all x2, waiting for transfers between devices, exchange(): lax.all_to_all(message.reshape(rows, 1, message.shape[1]), axes, split_ax...  14.3 us
    pallas_call x7, Pallas kernels, call(): pl.pallas_call(body, out_shape=outs, in_specs=[pl.BlockSpec(memory_space=...  11.7 us
    all_to_all x2, starting transfers between devices, exchange(): lax.all_to_all(message.reshape(rows, 1, message.shape[1]), axes, split_ax...  11.1 us
  transfers between devices with their start and end apart: 2, of which 2 were waited for; matrix products, arithmetic and copies ran while one was open for 0% of the time, Pallas kernels for 9%

profile of v5, /device:TPU:0, one launch (start us, length us, event | category | flops | bytes accessed | tf_op | source)
XLA Modules:
  0.0 59.7 jit_solution(6831116190167493143)
XLA Ops:
  0.6 2.0 %pack.1 = f32[928,128]{1,0:T(8,128)} custom-call(f32[2,3,1,64,128]{4,3,2,1,0:T(8,128)} %disp_ref.1, f32[1,64,128]{2,1,0:T(8,128)} %dens_ref.3, s32[1,64,128]{2,1,0:T(8,128)} %design_ref.5, s32[1,64,128]{2,1,0:T(8,128)} %support_ref.1), custom_call_target="tpu_custom_call" | custom-call | bytes 1048576 | tf_op jit(solution)/shard_map/pack/pallas_call | solution.py:297
  2.6 0.0 copy-start.3
  2.6 7.4 %all-to-all-start = ((f32[928,1,128]{2,1,0:T(1,128)}), f32[928,1,128]{2,1,0:T(1,128)S(1)}, u32[]{:S(2)}, u32[]{:S(2)}) async-start(f32[928,1,128]{2,1,0:T(1,128)} %bitcast.1), calls=%async_computation | async-start | bytes 950272 | tf_op jit(solution)/shard_map/all_to_all | solution.py:312
  10.1 0.0 copy-done.3
  10.1 0.0 copy-start.2
  10.1 0.7 %copy-done.2 = s32[2,2048]{1,0:T(2,128)S(1)} copy-done((s32[2,2048]{1,0:T(2,128)S(1)}, s32[2,2048]{1,0:T(2,128)}, u32[]{:S(2)}) %copy-start.2) | copy-done | bytes 16408
  10.8 4.1 %point_loads.1.rhs_ref = f32[3,208,128]{2,1,0:T(8,128)S(1)} custom-call(s32[2,2048]{1,0:T(2,128)S(1)} %copy-done.2, f32[2,3,2048]{2,1,0:T(4,128)S(1)} %copy.11.forces_ref), custom_call_target="tpu_custom_call" | custom-call | flops 268435456 | bytes 1048576 | tf_op jit(solution)/shard_map/point_loads/pallas_call | solution.py:297
  15.0 8.5 %all-to-all-done = f32[928,1,128]{2,1,0:T(1,128)S(1)} async-done(((f32[928,1,128]{2,1,0:T(1,128)}), f32[928,1,128]{2,1,0:T(1,128)S(1)}, u32[]{:S(2)}, u32[]{:S(2)}) %all-to-all-start) | async-done | bytes 475168 | tf_op jit(solution)/shard_map/all_to_all | solution.py:312
  23.5 2.3 %residual.1 = (f32[3,25,8,128]{3,2,1,0:T(8,128)S(1)}, f32[1,25,8,128]{3,2,1,0:T(8,128)S(1)}, f32[3,25,8,128]{3,2,1,0:T(8,128)S(1)}, f32[3,25,8,128]{3,2,1,0:T(8,...) custom-call(f32[928,128]{1,0:T(8,128)S(1)} %bitcast.16, f32[3,208,128]{2,1,0:T(8,128)S(1)} %point_loads.1.rhs_ref), custom_call_target="tpu_custom_call" | custom-call | flops 67108864 | bytes 1048576 | tf_op jit(solution)/shard_map/residual/pallas_call | solution.py:297
  25.8 3.6 %all-to-all-start.1 = ((f32[152,1,128]{2,1,0:T(1,128)}), f32[152,1,128]{2,1,0:T(1,128)S(1)}, u32[]{:S(2)}, u32[]{:S(2)}) async-start(f32[152,1,128]{2,1,0:T(1,128)} %bitcast.4), calls=%async_computation.1 | async-start | bytes 155648 | tf_op jit(solution)/shard_map/all_to_all | solution.py:312
  29.5 1.3 %powers.1 = (f32[3,25,8,128]{3,2,1,0:T(8,128)S(1)}, f32[3,25,8,128]{3,2,1,0:T(8,128)S(1)}) custom-call(f32[3,25,8,128]{3,2,1,0:T(8,128)S(1)} %get-tuple-element.18.geo_ref, f32[3,25,8,128]{3,2,1,0:T(8,128)S(1)} %get-tuple-element.20.one_ref), custom_call_target="tpu_custom_call" | custom-call | flops 67108864 | bytes 1048576 | tf_op jit(solution)/shard_map/powers/pallas_call | solution.py:297
  30.7 5.7 %all-to-all-done.1 = f32[152,1,128]{2,1,0:T(1,128)S(1)} async-done(((f32[152,1,128]{2,1,0:T(1,128)}), f32[152,1,128]{2,1,0:T(1,128)S(1)}, u32[]{:S(2)}, u32[]{:S(2)}) %all-to-all-start.1) | async-done | bytes 77856 | tf_op jit(solution)/shard_map/all_to_all | solution.py:312
  36.5 0.8 %energy.1 = (f32[392,128]{1,0:T(8,128)S(1)}, f32[288,128]{1,0:T(8,128)S(1)}, f32[8,128]{1,0:T(8,128)S(1)}) custom-call(f32[152,128]{1,0:T(8,128)S(1)} %bitcast.19, f32[3,25,8,128]{3,2,1,0:T(8,128)S(1)} %get-tuple-element.16.disp_ref, f32[1,25,8,128]{3,2,1,0:T(8,128)S(1)} %get-tuple-element.17.cube_ref, f32[3,25,8,128]{3,2,1,0:T(8,128)S(1)} %get-tuple-element.18.geo_ref, ...), custom_call_target="tpu_custom_call" | custom-call | flops 16777216 | bytes 1048576 | tf_op jit(solution)/shard_map/energy/pallas_call | solution.py:297
  37.3 0.0 copy-start
  37.3 0.0 copy-start.1
  37.3 9.8 %all_to_all.20 = f32[288,1,128]{2,1,0:T(1,128)S(1)} all-to-all(f32[288,1,128]{2,1,0:T(1,128)S(1)} %bitcast.22), channel_id=1, replica_groups=mesh['slab'=8,'load'=4] {'load','slab'}, dimensions={0} | all-to-all | bytes 294912 | tf_op jit(solution)/shard_map/all_to_all | solution.py:312
  47.1 0.0 copy-done
  47.1 0.0 copy-done.1
  47.1 0.3 trial.1
  47.4 11.5 %all_to_all.21 = f32[392,1,128]{2,1,0:T(1,128)S(1)} all-to-all(f32[392,1,128]{2,1,0:T(1,128)S(1)} %bitcast.18), channel_id=1, replica_groups=mesh['slab'=8,'load'=4] {'slab'}, dimensions={0} | all-to-all | bytes 401408 | tf_op jit(solution)/shard_map/all_to_all | solution.py:312
  58.9 0.8 %final.1 = (f32[2,3,1,64,128]{4,3,2,1,0:T(8,128)}, f32[1,64,128]{2,1,0:T(8,128)}) custom-call(f32[392,128]{1,0:T(8,128)S(1)} %bitcast.17, f32[64,128]{1,0:T(8,128)S(1)} %get-tuple-element.27.trial_ref, s32[1,64,128]{2,1,0:T(8,128)S(1)} %copy-done, f32[8,128]{1,0:T(8,128)S(1)} %get-tuple-element.24.count_ref), custom_call_target="tpu_custom_call" | custom-call | bytes 1048576 | tf_op jit(solution)/shard_map/final/pallas_call | solution.py:297
  (1 shorter events, 0.0 us)
Async XLA Ops:
  2.6 7.4 %copy-start.3 = (f32[2,3,2048]{2,0,1:T(2,128)S(1)}, f32[2,3,2048]{2,0,1:T(2,128)}, u32[]{:S(2)}) copy-start(f32[2,3,2048]{2,0,1:T(2,128)} %param.11) | copy-start | bytes 147460
  2.6 20.9 %all-to-all-start = ((f32[928,1,128]{2,1,0:T(1,128)}), f32[928,1,128]{2,1,0:T(1,128)S(1)}, u32[]{:S(2)}, u32[]{:S(2)}) async-start(f32[928,1,128]{2,1,0:T(1,128)} %bitcast.1), calls=%async_computation | async-start | bytes 950272 | tf_op jit(solution)/shard_map/all_to_all | solution.py:312
  10.1 0.7 %copy-start.2 = (s32[2,2048]{1,0:T(2,128)S(1)}, s32[2,2048]{1,0:T(2,128)}, u32[]{:S(2)}) copy-start(s32[2,2048]{1,0:T(2,128)} %nodes_ref.1) | copy-start | bytes 49156
  25.8 10.6 %all-to-all-start.1 = ((f32[152,1,128]{2,1,0:T(1,128)}), f32[152,1,128]{2,1,0:T(1,128)S(1)}, u32[]{:S(2)}, u32[]{:S(2)}) async-start(f32[152,1,128]{2,1,0:T(1,128)} %bitcast.4), calls=%async_computation.1 | async-start | bytes 155648 | tf_op jit(solution)/shard_map/all_to_all | solution.py:312
  37.3 9.8 %copy-start = (s32[1,64,128]{2,1,0:T(8,128)S(1)}, s32[1,64,128]{2,1,0:T(8,128)}, u32[]{:S(2)}) copy-start(s32[1,64,128]{2,1,0:T(8,128)} %design_ref.5) | copy-start | bytes 98308
  37.3 9.8 %copy-start.1 = (f32[1,64,128]{2,1,0:T(8,128)S(1)}, f32[1,64,128]{2,1,0:T(8,128)}, u32[]{:S(2)}) copy-start(f32[1,64,128]{2,1,0:T(8,128)} %dens_ref.3) | copy-start | bytes 98308

commit v6 on v5

--- a/solution.py
+++ b/solution.py
@@ -124,10 +124,10 @@
     return gauss(iota((count, count), 0) - iota((count, count), 1))
 
 
-def shifts(shape, rows_x):
+def shifts(shape, rows_x, first):
     inner = {}
-    for axis, count in ((0, shape[0]), (1, rows_x)):
-        index = iota(shape, axis) % count
+    for axis, start, count in ((0, first, shape[0]), (1, 0, rows_x)):
+        index = (iota(shape, axis) + start) % count
         inner[axis] = (index < count - 1, index > 0)
 
     def above(value, axis):
@@ -287,10 +287,20 @@
     return values
 
 
-def depth_table(depth, inner):
-    shape = (depth * inner, depth * inner)
+def filter_depth(layers):
+    depth = len(layers)
+    if depth <= 16:
+        weights = [float(np.exp(-((step / RADIUS) ** 2))) for step in range(depth)]
+        return [
+            sum(weights[abs(to - source)] * layers[source] for source in range(depth))
+            for to in range(depth)
+        ]
+    rows = layers[0].shape[0]
+    shape = (depth * rows, depth * rows)
     to, source = iota(shape, 0), iota(shape, 1)
-    return jnp.where(to % inner == source % inner, gauss(to // inner - source // inner), 0.0)
+    table = jnp.where(to % rows == source % rows, gauss(to // rows - source // rows), 0.0)
+    mixed = dot(table, jnp.concatenate(layers, 0))
+    return [mixed[layer * rows : (layer + 1) * rows] for layer in range(depth)]
 
 
 def call(body, outs, *args, scratch=(), name=None, flops=0, space=pltpu.VMEM, aliases=None):
@@ -307,10 +317,15 @@
     )(*args)
 
 
-def exchange(message, axes):
+def exchange(message, axes, order=None):
     rows = message.shape[0]
     return lax.all_to_all(
-        message.reshape(rows, 1, message.shape[1]), axes, split_axis=0, concat_axis=0, tiled=True
+        message.reshape(rows, 1, message.shape[1]),
+        axes,
+        split_axis=0,
+        concat_axis=0,
+        tiled=True,
+        axis_index_groups=order and [order],
     ).reshape(message.shape)
 
 
@@ -332,6 +347,9 @@
     block = lambda count: jax.ShapeDtypeStruct((count, span) + plane, F32)
     flat = lambda rows: jax.ShapeDtypeStruct((rows, width), F32)
     smoother = smoother_factors()
+    ring_start = slabs // 2 - 1
+    ring = [(at + ring_start) % slabs for at in range(slabs)]
+    place = lambda index: (index - ring_start) % slabs
 
     def pack_body(
         disp_ref, dens_ref, design_ref, support_ref, out_ref,
@@ -361,7 +379,7 @@
             )
         for copy in copies[:3]:
             copy.wait()
-        spread = dot(gauss_table(rows_x), dens_in[...])
+        spread = dot(dot(gauss_table(rows_x), dens_in[...]), gauss_table(cols_y))
         solid = design_in[...].astype(F32) * dens_in[...]
         both = jnp.concatenate([solid * solid * solid, support_in[...].astype(F32)], 0)
         pad_ref[comps, HALO_LOW : HALO_LOW + cols_y] = both.T
@@ -370,7 +388,7 @@
         for comp in range(comps):
             pad_ref[comp, HALO_LOW : HALO_LOW + cols_y] = stage_ref[comp].T
         for target in range(slabs):
-            base = target * in_rows
+            base = place(target) * in_rows
             for field in range(comps + 1):
                 out_ref[base + field * span : base + (field + 1) * span] = pad_ref[
                     field, target * strip : target * strip + span
@@ -398,7 +416,7 @@
         name="pack",
         space=pltpu.HBM,
     )
-    received = exchange(message, "slab")
+    received = exchange(message, "slab", ring)
 
     cells = -(-span * depth // 16) * 16
     chunk = min(256, points)
@@ -412,7 +430,7 @@
                 node = nodes_ref[load : load + 1, part]
                 row = node % cols_y - first
                 lane = load * rows_x + (node // cols_y) % rows_x
-                layer = node // (cols_y * rows_x)
+                layer = (node // (cols_y * rows_x) + depth - ring_start) % depth
                 cell = jnp.where((row >= 0) & (row < span), row * depth + layer, -1)
                 hit = iota((cells, chunk), 0) == cell
                 spot = (iota((width, chunk), 0) == lane).astype(F32).astype(jnp.bfloat16)
@@ -441,25 +459,19 @@
     def residual_body(
         in_ref, rhs_ref, disp_ref, cube_ref, geo_ref, zero_ref, one_ref, sum_ref
     ):
-        above, below = shifts(plane, rows_x)
+        above, below = shifts(plane, rows_x, ring_start)
         def gather(offset):
             offset = offset + (comps + 1) * span
-            return jnp.concatenate(
-                [
-                    in_ref[layer * in_rows + offset : layer * in_rows + offset + half]
-                    for layer in range(depth)
-                ],
-                0,
-            )
-
-        table_z = depth_table(depth, half)
-        table_y = gauss_table(cols_y)
-        mask = gather(half)
-        filtered = dot(table_z, dot(gather(0), table_y))
-        share = dot(table_z, dot(mask / filtered, table_y))
-        share = swap_blocks(
-            [share[layer * half : (layer + 1) * half] for layer in range(depth)], strip
-        )
+            return [
+                in_ref[place(layer) * in_rows + offset : place(layer) * in_rows + offset + half]
+                for layer in range(depth)
+            ]
+
+        mask = jnp.concatenate(gather(half), 0)
+        filtered = jnp.concatenate(filter_depth(gather(0)), 0)
+        share = dot(mask / filtered, gauss_table(cols_y))
+        share = filter_depth([share[layer * half : (layer + 1) * half] for layer in range(depth)])
+        share = swap_blocks([share[layer] for layer in ring], strip)
         cube_side = iota(plane, 1) < rows_x
         for row in range(span):
             pick = lambda field: in_ref[pl.ds(field * span + row, depth, stride=in_rows), :]
@@ -523,7 +535,7 @@
         down = lambda value: jnp.sum(value, 0, keepdims=True)
         sums = [down(curve), down(weight), down(mask)]
         for target in range(slabs):
-            base = target * sum_rows
+            base = place(target) * sum_rows
             for index, value in enumerate(sums):
                 sum_ref[base + index : base + index + 1] = value
             sum_ref[base + 3 : base + 3 + half] = share[target]
@@ -546,10 +558,10 @@
         name="residual",
         flops=1 << 26,
     )
-    all_sums = exchange(sums, "slab")
+    all_sums = exchange(sums, "slab", ring)
 
     def powers_body(geo_ref, one_ref, two_ref, three_ref):
-        above, below = shifts(plane, rows_x)
+        above, below = shifts(plane, rows_x, ring_start)
         scale_row = lambda row: geo_ref[0, row]
         for source, target, edge in ((one_ref, two_ref, 2), (two_ref, three_ref, 3)):
 
@@ -583,7 +595,7 @@
         sums_ref, disp_ref, cube_ref, geo_ref, zero_ref, one_ref, two_ref, three_ref,
         disp_out_ref, numer_ref, count_ref, weak_ref,
     ):
-        above, below = shifts(plane, rows_x)
+        above, below = shifts(plane, rows_x, ring_start)
         gather = lambda index: sum(
             sums_ref[layer * sum_rows + index : layer * sum_rows + index + 1]
             for layer in range(slabs)
@@ -611,8 +623,8 @@
                 value = smoother[0] * zero_ref[comp, row] + inverse * value
                 value = disp_ref[comp, row] + inverse * value
                 if row < HALO_LOW + strip:
-                    place = comp * strip + row - HALO_LOW
-                    disp_out_ref[pl.ds(place, depth, stride=out_rows), :] = value
+                    start = comp * strip + row - HALO_LOW
+                    disp_out_ref[pl.ds(start, depth, stride=out_rows), :] = value
                 values.append(free * value)
             modes = row_modes(values, above)
             if lower is not None:
@@ -629,21 +641,25 @@
         across_x = dot(table_x, weak, turned=True)
         shape = (width, width)
         table_x = gauss(iota(shape, 0) % rows_x - iota(shape, 1) % rows_x)
-        smooth = dot(depth_table(depth, strip), dot(weak, table_x))
+        smooth = dot(weak, table_x)
         weighted = jnp.zeros((1, width), F32)
         for source in range(slabs):
-            base = source * sum_rows + 3
+            base = place(source) * sum_rows + 3
             weighted = weighted + jnp.sum(
                 across_x[source * half : (source + 1) * half] * sums_ref[base : base + half],
                 0,
                 keepdims=True,
             )
         block_of = iota((half, width), 1) // rows_x
+        pieces = []
         for layer in range(depth):
-            piece = smooth[layer * strip : layer * strip + half]
+            rows = place(layer) * strip
+            piece = smooth[rows : rows + half]
             for block_at in range(1, strip // half):
-                rows = layer * strip + block_at * half
+                rows = rows + half
                 piece = jnp.where(block_of == block_at, smooth[rows : rows + half], piece)
+            pieces.append(piece)
+        for layer, piece in enumerate(filter_depth(pieces)):
             for part in range(parts):
                 base = (part * slabs + layer) * numer_rows
                 numer_ref[base : base + half] = piece
@@ -677,7 +693,7 @@
                 base = (part * slabs + source) * numer_rows
                 total = total + numer_ref[base : base + half]
                 weighted = weighted + numer_ref[base + half : base + numer_rows]
-            base = source * sum_rows + 3 + half
+            base = place(source) * sum_rows + 3 + half
             filtered_ref[source * half : (source + 1) * half] = sums_ref[base : base + half]
             plane_ref[source * half : (source + 1) * half] = total
         mean = jnp.sum(weighted, 1, keepdims=True) / count_ref[0:1] + EPSILON
@@ -711,15 +727,15 @@
         name="trial",
         aliases={5: 1},
     )
-    out_pieces = exchange(out_message, "slab")
+    out_pieces = exchange(out_message, "slab", ring)
 
     def final_body(pieces_ref, trial_ref, design_ref, count_ref, disp_ref, dens_ref, whole_ref):
         volume = jnp.zeros((1, width), F32)
         for source in range(slabs):
-            base = (source + 1) * out_rows
+            base = (place(source) + 1) * out_rows
             volume = volume + pieces_ref[base - 1 : base]
             for comp in range(comps):
-                base = source * out_rows + comp * strip
+                base = place(source) * out_rows + comp * strip
                 whole_ref[comp, source * strip : (source + 1) * strip] = pieces_ref[
                     base : base + strip
                 ]

time: 60.2 us -> 57.5 us (0.955)
  waiting for transfers between devices: 14.3 us -> 10.5 us
  starting transfers between devices: 11.1 us -> 12.2 us
    all_to_all x2, waiting for transfers between devices: 14.3 us -> 10.5 us  [exchange(): lax.all_to_all(message.reshape(rows, 1, message.shape[1]), axes, split_ax...]
    all_to_all x2, starting transfers between devices: 11.1 us -> 12.2 us  [exchange(): lax.all_to_all(message.reshape(rows, 1, message.shape[1]), axes, split_ax...]
where the time goes in v6:
time: 57.5 us; the launch traced here: 57 us
  blocking collectives  21.4 us (37%)
  starting transfers between devices  12.2 us (21%)
  Pallas kernels  11.5 us (20%)
  waiting for transfers between devices  10.5 us (18%)
  local copies, waits for them, and re-layouts  0.73 us (1%)
  between operations  0.69 us (1%)
    all_to_all x2, blocking collectives, exchange(): lax.all_to_all(message.reshape(rows, 1, message.shape[1]), axes, split_ax...  21.4 us
    all_to_all x2, starting transfers between devices, exchange(): lax.all_to_all(message.reshape(rows, 1, message.shape[1]), axes, split_ax...  12.2 us
    pallas_call x7, Pallas kernels, call(): pl.pallas_call(body, out_shape=outs, in_specs=[pl.BlockSpec(memory_space=...  11.5 us
    all_to_all x2, waiting for transfers between devices, exchange(): lax.all_to_all(message.reshape(rows, 1, message.shape[1]), axes, split_ax...  10.5 us
  transfers between devices with their start and end apart: 2, of which 2 were waited for; matrix products, arithmetic and copies ran while one was open for 0% of the time, Pallas kernels for 9%

profile of v6, /device:TPU:0, one launch (start us, length us, event | category | flops | bytes accessed | tf_op | source)
XLA Modules:
  0.0 57.0 jit_solution(8080812560021332841)
XLA Ops:
  0.6 2.1 %pack.1 = f32[928,128]{1,0:T(8,128)} custom-call(f32[2,3,1,64,128]{4,3,2,1,0:T(8,128)} %disp_ref.1, f32[1,64,128]{2,1,0:T(8,128)} %dens_ref.3, s32[1,64,128]{2,1,0:T(8,128)} %design_ref.5, s32[1,64,128]{2,1,0:T(8,128)} %support_ref.1), custom_call_target="tpu_custom_call" | custom-call | bytes 1048576 | tf_op jit(solution)/shard_map/pack/pallas_call | solution.py:307
  2.7 0.0 copy-start.3
  2.7 8.0 %all-to-all-start = ((f32[928,1,128]{2,1,0:T(1,128)}), f32[928,1,128]{2,1,0:T(1,128)S(1)}, u32[]{:S(2)}, u32[]{:S(2)}) async-start(f32[928,1,128]{2,1,0:T(1,128)} %bitcast.1), calls=%async_computation | async-start | bytes 950272 | tf_op jit(solution)/shard_map/all_to_all | solution.py:322
  10.7 0.0 copy-done.3
  10.7 0.0 copy-start.2
  10.8 0.7 %copy-done.2 = s32[2,2048]{1,0:T(2,128)S(1)} copy-done((s32[2,2048]{1,0:T(2,128)S(1)}, s32[2,2048]{1,0:T(2,128)}, u32[]{:S(2)}) %copy-start.2) | copy-done | bytes 16408
  11.4 4.1 %point_loads.1.rhs_ref = f32[3,208,128]{2,1,0:T(8,128)S(1)} custom-call(s32[2,2048]{1,0:T(2,128)S(1)} %copy-done.2, f32[2,3,2048]{2,1,0:T(4,128)S(1)} %copy.11.forces_ref), custom_call_target="tpu_custom_call" | custom-call | flops 268435456 | bytes 1048576 | tf_op jit(solution)/shard_map/point_loads/pallas_call | solution.py:307
  15.6 7.1 %all-to-all-done = f32[928,1,128]{2,1,0:T(1,128)S(1)} async-done(((f32[928,1,128]{2,1,0:T(1,128)}), f32[928,1,128]{2,1,0:T(1,128)S(1)}, u32[]{:S(2)}, u32[]{:S(2)}) %all-to-all-start) | async-done | bytes 475168 | tf_op jit(solution)/shard_map/all_to_all | solution.py:322
  22.7 2.3 %residual.1 = (f32[3,25,8,128]{3,2,1,0:T(8,128)S(1)}, f32[1,25,8,128]{3,2,1,0:T(8,128)S(1)}, f32[3,25,8,128]{3,2,1,0:T(8,128)S(1)}, f32[3,25,8,128]{3,2,1,0:T(8,...) custom-call(f32[928,128]{1,0:T(8,128)S(1)} %bitcast.16, f32[3,208,128]{2,1,0:T(8,128)S(1)} %point_loads.1.rhs_ref), custom_call_target="tpu_custom_call" | custom-call | flops 67108864 | bytes 1048576 | tf_op jit(solution)/shard_map/residual/pallas_call | solution.py:307
  24.9 4.2 %all-to-all-start.1 = ((f32[152,1,128]{2,1,0:T(1,128)}), f32[152,1,128]{2,1,0:T(1,128)S(1)}, u32[]{:S(2)}, u32[]{:S(2)}) async-start(f32[152,1,128]{2,1,0:T(1,128)} %bitcast.4), calls=%async_computation.1 | async-start | bytes 155648 | tf_op jit(solution)/shard_map/all_to_all | solution.py:322
  29.2 1.3 %powers.1 = (f32[3,25,8,128]{3,2,1,0:T(8,128)S(1)}, f32[3,25,8,128]{3,2,1,0:T(8,128)S(1)}) custom-call(f32[3,25,8,128]{3,2,1,0:T(8,128)S(1)} %get-tuple-element.18.geo_ref, f32[3,25,8,128]{3,2,1,0:T(8,128)S(1)} %get-tuple-element.20.one_ref), custom_call_target="tpu_custom_call" | custom-call | flops 67108864 | bytes 1048576 | tf_op jit(solution)/shard_map/powers/pallas_call | solution.py:307
  30.4 3.4 %all-to-all-done.1 = f32[152,1,128]{2,1,0:T(1,128)S(1)} async-done(((f32[152,1,128]{2,1,0:T(1,128)}), f32[152,1,128]{2,1,0:T(1,128)S(1)}, u32[]{:S(2)}, u32[]{:S(2)}) %all-to-all-start.1) | async-done | bytes 77856 | tf_op jit(solution)/shard_map/all_to_all | solution.py:322
  33.8 0.7 %energy.1 = (f32[392,128]{1,0:T(8,128)S(1)}, f32[288,128]{1,0:T(8,128)S(1)}, f32[8,128]{1,0:T(8,128)S(1)}) custom-call(f32[152,128]{1,0:T(8,128)S(1)} %bitcast.19, f32[3,25,8,128]{3,2,1,0:T(8,128)S(1)} %get-tuple-element.16.disp_ref, f32[1,25,8,128]{3,2,1,0:T(8,128)S(1)} %get-tuple-element.17.cube_ref, f32[3,25,8,128]{3,2,1,0:T(8,128)S(1)} %get-tuple-element.18.geo_ref, ...), custom_call_target="tpu_custom_call" | custom-call | flops 16777216 | bytes 1048576 | tf_op jit(solution)/shard_map/energy/pallas_call | solution.py:307
  34.5 0.0 copy-start
  34.5 0.0 copy-start.1
  34.5 10.9 %all_to_all.20 = f32[288,1,128]{2,1,0:T(1,128)S(1)} all-to-all(f32[288,1,128]{2,1,0:T(1,128)S(1)} %bitcast.22), channel_id=1, replica_groups=mesh['slab'=8,'load'=4] {'load','slab'}, dimensions={0} | all-to-all | bytes 294912 | tf_op jit(solution)/shard_map/all_to_all | solution.py:322
  45.4 0.0 copy-done
  45.4 0.0 copy-done.1
  45.4 0.3 trial.1
  45.7 10.5 %all_to_all.21 = f32[392,1,128]{2,1,0:T(1,128)S(1)} all-to-all(f32[392,1,128]{2,1,0:T(1,128)S(1)} %bitcast.18), channel_id=1, replica_groups={{12,16,20,24,28,0,4,8},{13,17,21,25,29,1,5,9},{14,18,22,26,30,2,6,10},{..., dimensions={0} | all-to-all | bytes 401408 | tf_op jit(solution)/shard_map/all_to_all | solution.py:322
  56.2 0.8 %final.1 = (f32[2,3,1,64,128]{4,3,2,1,0:T(8,128)}, f32[1,64,128]{2,1,0:T(8,128)}) custom-call(f32[392,128]{1,0:T(8,128)S(1)} %bitcast.17, f32[64,128]{1,0:T(8,128)S(1)} %get-tuple-element.27.trial_ref, s32[1,64,128]{2,1,0:T(8,128)S(1)} %copy-done, f32[8,128]{1,0:T(8,128)S(1)} %get-tuple-element.24.count_ref), custom_call_target="tpu_custom_call" | custom-call | bytes 1048576 | tf_op jit(solution)/shard_map/final/pallas_call | solution.py:307
  (1 shorter events, 0.0 us)
Async XLA Ops:
  2.7 8.0 %copy-start.3 = (f32[2,3,2048]{2,0,1:T(2,128)S(1)}, f32[2,3,2048]{2,0,1:T(2,128)}, u32[]{:S(2)}) copy-start(f32[2,3,2048]{2,0,1:T(2,128)} %param.11) | copy-start | bytes 147460
  2.7 20.0 %all-to-all-start = ((f32[928,1,128]{2,1,0:T(1,128)}), f32[928,1,128]{2,1,0:T(1,128)S(1)}, u32[]{:S(2)}, u32[]{:S(2)}) async-start(f32[928,1,128]{2,1,0:T(1,128)} %bitcast.1), calls=%async_computation | async-start | bytes 950272 | tf_op jit(solution)/shard_map/all_to_all | solution.py:322
  10.7 0.7 %copy-start.2 = (s32[2,2048]{1,0:T(2,128)S(1)}, s32[2,2048]{1,0:T(2,128)}, u32[]{:S(2)}) copy-start(s32[2,2048]{1,0:T(2,128)} %nodes_ref.1) | copy-start | bytes 49156
  24.9 8.8 %all-to-all-start.1 = ((f32[152,1,128]{2,1,0:T(1,128)}), f32[152,1,128]{2,1,0:T(1,128)S(1)}, u32[]{:S(2)}, u32[]{:S(2)}) async-start(f32[152,1,128]{2,1,0:T(1,128)} %bitcast.4), calls=%async_computation.1 | async-start | bytes 155648 | tf_op jit(solution)/shard_map/all_to_all | solution.py:322
  34.5 10.9 %copy-start = (s32[1,64,128]{2,1,0:T(8,128)S(1)}, s32[1,64,128]{2,1,0:T(8,128)}, u32[]{:S(2)}) copy-start(s32[1,64,128]{2,1,0:T(8,128)} %design_ref.5) | copy-start | bytes 98308
  34.5 10.9 %copy-start.1 = (f32[1,64,128]{2,1,0:T(8,128)S(1)}, f32[1,64,128]{2,1,0:T(8,128)}, u32[]{:S(2)}) copy-start(f32[1,64,128]{2,1,0:T(8,128)} %dens_ref.3) | copy-start | bytes 98308

commit v7 on v6

--- a/solution.py
+++ b/solution.py
@@ -350,6 +350,9 @@
     ring_start = slabs // 2 - 1
     ring = [(at + ring_start) % slabs for at in range(slabs)]
     place = lambda index: (index - ring_start) % slabs
+    sums_start = slabs // 2 - 2
+    sums_ring = [(at + sums_start) % slabs for at in range(slabs)]
+    sums_place = lambda index: (index - sums_start) % slabs
 
     def pack_body(
         disp_ref, dens_ref, design_ref, support_ref, out_ref,
@@ -454,12 +457,84 @@
     )
 
     def own_row(row):
-        return (row >= HALO_LOW) & (row < HALO_LOW + strip)
+        return HALO_LOW <= row < HALO_LOW + strip
+
+    last_row = HALO_LOW + strip
+    near_nodes = range(HALO_LOW - 2, last_row + 3)
+    near_zero = range(HALO_LOW - 1, last_row + 2)
+    near_one = range(HALO_LOW, last_row + 1)
+
+    def strip_rows(disp, geo, inverse, zero, one, in_ref, rhs_ref):
+        above, below = shifts(plane, rows_x, ring_start)
+        cube_side = iota(plane, 1) < rows_x
+        scale_row = lambda row: geo(row)[0, row]
+
+        def read(rows, cube_ref=None):
+            for row in rows:
+                pick = lambda field: in_ref[pl.ds(field * span + row, depth, stride=in_rows), :]
+                for comp in range(comps):
+                    disp(row)[comp, row] = pick(comp)
+                both = pick(comps)
+                other = pltpu.roll(both, rows_x, 1)
+                cube = jnp.where(cube_side, both, other)
+                if cube_ref is not None:
+                    cube_ref[0, row] = cube
+                geo(row)[0, row] = jnp.where(
+                    cube < 0.0, 0.0, STIFF_VOID + (1.0 - STIFF_VOID) * cube
+                )
+                geo(row)[1, row] = 1.0 - jnp.where(cube_side, other, both)
+
+        def invert(rows):
+            for row in rows:
+                beside = geo(row)[0, row] + geo(row - 1)[0, row - 1]
+                beside = beside + below(beside, 0)
+                beside = beside + below(beside, 1)
+                free = geo(row)[1, row]
+                inverse(row)[0, row] = 1.0 / (free * DIAG_ENTRY * beside + (1.0 - free))
+
+        def masked(source):
+            def load_row(row):
+                free = geo(row)[1, row]
+                return [free * source(row)[comp, row] for comp in range(comps)]
+
+            return load_row
+
+        def residual(first, last):
+            def emit(row, forces, carried):
+                free, inverted = geo(row)[1, row], inverse(row)[0, row]
+                total = jnp.zeros(plane, F32)
+                for comp, force in enumerate(forces):
+                    load_row = rhs_ref[comp, row * depth : (row + 1) * depth, :]
+                    rest = free * (load_row - force) - (1.0 - free) * disp(row)[comp, row]
+                    value = rest * inverted
+                    zero(row)[comp, row] = value
+                    total = total + value * rest
+                return carried + total if own_row(row) else carried
+
+            return apply_rows(
+                first, last, masked(disp), scale_row, emit, above, below, jnp.zeros(plane, F32)
+            )
+
+        def power(source, target, first, last):
+            def emit(row, forces, carried):
+                free, inverted = geo(row)[1, row], inverse(row)[0, row]
+                total = jnp.zeros(plane, F32)
+                for comp, force in enumerate(forces):
+                    value = source(row)[comp, row]
+                    applied = free * force + (1.0 - free) * value
+                    target(row)[comp, row] = applied * inverted
+                    total = total + value * applied
+                return carried + total if own_row(row) else carried
+
+            return apply_rows(
+                first, last, masked(source), scale_row, emit, above, below, jnp.zeros(plane, F32)
+            )
+
+        return read, invert, residual, power
 
     def residual_body(
-        in_ref, rhs_ref, disp_ref, cube_ref, geo_ref, zero_ref, one_ref, sum_ref
+        in_ref, rhs_ref, disp_ref, cube_ref, geo_ref, inv_ref, zero_ref, one_ref, sum_ref
     ):
-        above, below = shifts(plane, rows_x, ring_start)
         def gather(offset):
             offset = offset + (comps + 1) * span
             return [
@@ -472,70 +547,19 @@
         share = dot(mask / filtered, gauss_table(cols_y))
         share = filter_depth([share[layer * half : (layer + 1) * half] for layer in range(depth)])
         share = swap_blocks([share[layer] for layer in ring], strip)
-        cube_side = iota(plane, 1) < rows_x
-        for row in range(span):
-            pick = lambda field: in_ref[pl.ds(field * span + row, depth, stride=in_rows), :]
-            for comp in range(comps):
-                disp_ref[comp, row] = pick(comp)
-            both = pick(comps)
-            other = pltpu.roll(both, rows_x, 1)
-            cube = jnp.where(cube_side, both, other)
-            cube_ref[0, row] = cube
-            geo_ref[0, row] = jnp.where(
-                cube < 0.0, 0.0, STIFF_VOID + (1.0 - STIFF_VOID) * cube
-            )
-            geo_ref[1, row] = 1.0 - jnp.where(cube_side, other, both)
-        for row in range(1, span - 1):
-            beside = geo_ref[0, row] + geo_ref[0, row - 1]
-            beside = beside + below(beside, 0)
-            beside = beside + below(beside, 1)
-            free = geo_ref[1, row]
-            geo_ref[2, row] = 1.0 / (free * DIAG_ENTRY * beside + (1.0 - free))
-
-        scale_row = lambda row: geo_ref[0, row]
-
-        def start_row(row):
-            free = geo_ref[1, row]
-            return [free * disp_ref[comp, row] for comp in range(comps)]
-
-        def emit_residual(row, forces, carried):
-            free, inverse = geo_ref[1, row], geo_ref[2, row]
-            total = jnp.zeros(plane, F32)
-            for comp, force in enumerate(forces):
-                load_row = rhs_ref[comp, pl.ds(row * depth, depth), :]
-                rest = free * (load_row - force) - (1.0 - free) * disp_ref[comp, row]
-                value = rest * inverse
-                zero_ref[comp, row] = value
-                total = total + value * rest
-            return carried + total if own_row(row) else carried
-
-        weight = apply_rows(
-            0, span - 1, start_row, scale_row, emit_residual, above, below,
-            jnp.zeros(plane, F32),
+        here = lambda ref: lambda row: ref
+        zero = here(zero_ref)
+        read, invert, residual, power = strip_rows(
+            here(disp_ref), here(geo_ref), here(inv_ref), zero, here(one_ref), in_ref, rhs_ref
         )
-
-        def zero_row(row):
-            free = geo_ref[1, row]
-            return [free * zero_ref[comp, row] for comp in range(comps)]
-
-        def emit_one(row, forces, carried):
-            free, inverse = geo_ref[1, row], geo_ref[2, row]
-            total = jnp.zeros(plane, F32)
-            for comp, force in enumerate(forces):
-                value = zero_ref[comp, row]
-                applied = free * force + (1.0 - free) * value
-                one_ref[comp, row] = applied * inverse
-                total = total + value * applied
-            return carried + total if own_row(row) else carried
-
-        curve = apply_rows(
-            1, span - 2, zero_row, scale_row, emit_one, above, below, jnp.zeros(plane, F32)
-        )
-
+        read(near_nodes, cube_ref)
+        invert(near_zero)
+        weight = residual(near_zero[0] - 1, near_zero[-1] + 1)
+        curve = power(zero, here(one_ref), near_one[0] - 1, near_one[-1] + 1)
         down = lambda value: jnp.sum(value, 0, keepdims=True)
         sums = [down(curve), down(weight), down(mask)]
         for target in range(slabs):
-            base = place(target) * sum_rows
+            base = sums_place(target) * sum_rows
             for index, value in enumerate(sums):
                 sum_ref[base + index : base + index + 1] = value
             sum_ref[base + 3 : base + 3 + half] = share[target]
@@ -543,12 +567,13 @@
                 target * half : (target + 1) * half
             ]
 
-    disp, cube, geometry, zeroth, first, sums = call(
+    disp, cube, geometry, inverses, zeroth, first, sums = call(
         residual_body,
         (
             block(comps),
             block(1),
-            block(3),
+            block(2),
+            block(1),
             block(comps),
             block(comps),
             flat(slabs * sum_rows),
@@ -558,35 +583,46 @@
         name="residual",
         flops=1 << 26,
     )
-    all_sums = exchange(sums, "slab", ring)
-
-    def powers_body(geo_ref, one_ref, two_ref, three_ref):
-        above, below = shifts(plane, rows_x, ring_start)
-        scale_row = lambda row: geo_ref[0, row]
-        for source, target, edge in ((one_ref, two_ref, 2), (two_ref, three_ref, 3)):
-
-            def load_row(row):
-                free = geo_ref[1, row]
-                return [free * source[comp, row] for comp in range(comps)]
-
-            def emit(row, forces, carried):
-                free, inverse = geo_ref[1, row], geo_ref[2, row]
-                for comp, force in enumerate(forces):
-                    target[comp, row] = (
-                        free * force + (1.0 - free) * source[comp, row]
-                    ) * inverse
-                return carried
-
-            apply_rows(
-                edge, span - 1 - edge, load_row, scale_row, emit, above, below,
-                jnp.zeros((1, 1), F32),
-            )
+    all_sums = exchange(sums, "slab", sums_ring)
+
+    def powers_body(
+        in_ref, rhs_ref, disp_ref, geo_ref, inv_ref, zero_ref, one_ref, two_ref, three_ref,
+        far_disp, far_geo, far_inv, far_zero, far_one,
+    ):
+        choose = lambda near, far, rows: lambda row: near if row in rows else far
+        zero = choose(zero_ref, far_zero, near_zero)
+        one = choose(one_ref, far_one, near_one)
+        read, invert, residual, power = strip_rows(
+            choose(disp_ref, far_disp, near_nodes),
+            choose(geo_ref, far_geo, near_nodes),
+            choose(inv_ref, far_inv, near_zero),
+            zero,
+            one,
+            in_ref,
+            rhs_ref,
+        )
+        read([row for row in range(span) if row not in near_nodes])
+        invert([row for row in range(1, span - 1) if row not in near_zero])
+        residual(0, near_zero[0])
+        residual(near_zero[-1], span - 1)
+        power(zero, one, 1, near_one[0])
+        power(zero, one, near_one[-1], span - 2)
+        power(one, lambda row: two_ref, 2, span - 3)
+        power(lambda row: two_ref, lambda row: three_ref, 3, span - 4)
 
     second, third = call(
         powers_body,
         (block(comps), block(comps)),
+        received,
+        right_side,
+        disp,
         geometry,
+        inverses,
+        zeroth,
         first,
+        scratch=[
+            pltpu.VMEM((count, span) + plane, F32) for count in (comps, 2, 1, comps, comps)
+        ],
         name="powers",
         flops=1 << 26,
     )
@@ -644,7 +680,7 @@
         smooth = dot(weak, table_x)
         weighted = jnp.zeros((1, width), F32)
         for source in range(slabs):
-            base = place(source) * sum_rows + 3
+            base = sums_place(source) * sum_rows + 3
             weighted = weighted + jnp.sum(
                 across_x[source * half : (source + 1) * half] * sums_ref[base : base + half],
                 0,
@@ -693,7 +729,7 @@
                 base = (part * slabs + source) * numer_rows
                 total = total + numer_ref[base : base + half]
                 weighted = weighted + numer_ref[base + half : base + numer_rows]
-            base = place(source) * sum_rows + 3 + half
+            base = sums_place(source) * sum_rows + 3 + half
             filtered_ref[source * half : (source + 1) * half] = sums_ref[base : base + half]
             plane_ref[source * half : (source + 1) * half] = total
         mean = jnp.sum(weighted, 1, keepdims=True) / count_ref[0:1] + EPSILON

time: 57.5 us -> 57 us (level)
  starting transfers between devices: 12.2 us -> 11.6 us
  blocking collectives: 21.4 us -> 20.8 us
    all_to_all x2, starting transfers between devices: 12.2 us -> 11.6 us  [exchange(): lax.all_to_all(message.reshape(rows, 1, message.shape[1]), axes, split_ax...]
    all_to_all x2, blocking collectives: 21.4 us -> 20.8 us  [exchange(): lax.all_to_all(message.reshape(rows, 1, message.shape[1]), axes, split_ax...]
  transfers between devices with their start and end apart: 2 -> 2, of which waited for: 2 -> 2; matrix products, arithmetic and copies ran while one was open for 0% -> 0% of each run, Pallas kernels for 9% -> 11%
where the time goes in v7:
time: 57 us; the launch traced here: 56.4 us
  blocking collectives  20.8 us (36%)
  Pallas kernels  12 us (21%)
  starting transfers between devices  11.6 us (20%)
  waiting for transfers between devices  10.7 us (19%)
  local copies, waits for them, and re-layouts  0.73 us (1%)
  between operations  0.69 us (1%)
    all_to_all x2, blocking collectives, exchange(): lax.all_to_all(message.reshape(rows, 1, message.shape[1]), axes, split_ax...  20.8 us
    pallas_call x7, Pallas kernels, call(): pl.pallas_call(body, out_shape=outs, in_specs=[pl.BlockSpec(memory_space=...  12 us
    all_to_all x2, starting transfers between devices, exchange(): lax.all_to_all(message.reshape(rows, 1, message.shape[1]), axes, split_ax...  11.6 us
    all_to_all x2, waiting for transfers between devices, exchange(): lax.all_to_all(message.reshape(rows, 1, message.shape[1]), axes, split_ax...  10.7 us
  transfers between devices with their start and end apart: 2, of which 2 were waited for; matrix products, arithmetic and copies ran while one was open for 0% of the time, Pallas kernels for 11%

profile of v7, /device:TPU:0, one launch (start us, length us, event | category | flops | bytes accessed | tf_op | source)
XLA Modules:
  0.0 56.4 jit_solution(16568157355198174844)
XLA Ops:
  0.6 2.1 %pack.1 = f32[928,128]{1,0:T(8,128)} custom-call(f32[2,3,1,64,128]{4,3,2,1,0:T(8,128)} %disp_ref.1, f32[1,64,128]{2,1,0:T(8,128)} %dens_ref.3, s32[1,64,128]{2,1,0:T(8,128)} %design_ref.5, s32[1,64,128]{2,1,0:T(8,128)} %support_ref.1), custom_call_target="tpu_custom_call" | custom-call | bytes 1048576 | tf_op jit(solution)/shard_map/pack/pallas_call | solution.py:307
  2.7 0.0 copy-start.3
  2.7 8.0 %all-to-all-start = ((f32[928,1,128]{2,1,0:T(1,128)}), f32[928,1,128]{2,1,0:T(1,128)S(1)}, u32[]{:S(2)}, u32[]{:S(2)}) async-start(f32[928,1,128]{2,1,0:T(1,128)} %bitcast.1), calls=%async_computation | async-start | bytes 950272 | tf_op jit(solution)/shard_map/all_to_all | solution.py:322
  10.7 0.0 copy-done.3
  10.7 0.0 copy-start.2
  10.8 0.7 %copy-done.2 = s32[2,2048]{1,0:T(2,128)S(1)} copy-done((s32[2,2048]{1,0:T(2,128)S(1)}, s32[2,2048]{1,0:T(2,128)}, u32[]{:S(2)}) %copy-start.2) | copy-done | bytes 16408
  11.4 4.1 %point_loads.1.rhs_ref = f32[3,208,128]{2,1,0:T(8,128)S(1)} custom-call(s32[2,2048]{1,0:T(2,128)S(1)} %copy-done.2, f32[2,3,2048]{2,1,0:T(4,128)S(1)} %copy.11.forces_ref), custom_call_target="tpu_custom_call" | custom-call | flops 268435456 | bytes 1048576 | tf_op jit(solution)/shard_map/point_loads/pallas_call | solution.py:307
  15.6 7.1 %all-to-all-done = f32[928,1,128]{2,1,0:T(1,128)S(1)} async-done(((f32[928,1,128]{2,1,0:T(1,128)}), f32[928,1,128]{2,1,0:T(1,128)S(1)}, u32[]{:S(2)}, u32[]{:S(2)}) %all-to-all-start) | async-done | bytes 475168 | tf_op jit(solution)/shard_map/all_to_all | solution.py:322
  22.7 2.0 %residual.1 = (f32[3,25,8,128]{3,2,1,0:T(8,128)S(1)}, f32[1,25,8,128]{3,2,1,0:T(8,128)S(1)}, f32[2,25,8,128]{3,2,1,0:T(8,128)S(1)}, f32[1,25,8,128]{3,2,1,0:T(8,...) custom-call(f32[928,128]{1,0:T(8,128)S(1)} %bitcast.16, ...), custom_call_target="tpu_custom_call" | custom-call | flops 67108864 | bytes 1048576 | tf_op jit(solution)/shard_map/residual/pallas_call | solution.py:307
  24.7 3.6 %all-to-all-start.1 = ((f32[152,1,128]{2,1,0:T(1,128)}), f32[152,1,128]{2,1,0:T(1,128)S(1)}, u32[]{:S(2)}, u32[]{:S(2)}) async-start(f32[152,1,128]{2,1,0:T(1,128)} %bitcast.4), calls=%async_computation.1 | async-start | bytes 155648 | tf_op jit(solution)/shard_map/all_to_all | solution.py:322
  28.3 1.9 %powers.1 = (f32[3,25,8,128]{3,2,1,0:T(8,128)S(1)}, f32[3,25,8,128]{3,2,1,0:T(8,128)S(1)}) custom-call(f32[928,128]{1,0:T(8,128)S(1)} %bitcast.17, f32[3,208,128]{2,1,0:T(8,128)S(1)} %point_loads.1.rhs_ref, f32[3,25,8,128]{3,2,1,0:T(8,128)S(1)} %get-tuple-element.17.disp_ref, f32[2,25,8,128]{3,2,1,0:T(8,128)S(1)} %get-tuple-element.19.geo_ref, ...), custom_call_target="tpu_custom_call" | custom-call | flops 67108864 | bytes 1048576 | tf_op jit(solution)/shard_map/powers/pallas_call | solution.py:307
  30.2 3.6 %all-to-all-done.1 = f32[152,1,128]{2,1,0:T(1,128)S(1)} async-done(((f32[152,1,128]{2,1,0:T(1,128)}), f32[152,1,128]{2,1,0:T(1,128)S(1)}, u32[]{:S(2)}, u32[]{:S(2)}) %all-to-all-start.1) | async-done | bytes 77856 | tf_op jit(solution)/shard_map/all_to_all | solution.py:322
  33.8 0.7 %energy.1 = (f32[392,128]{1,0:T(8,128)S(1)}, f32[288,128]{1,0:T(8,128)S(1)}, f32[8,128]{1,0:T(8,128)S(1)}) custom-call(f32[152,128]{1,0:T(8,128)S(1)} %bitcast.20, f32[3,25,8,128]{3,2,1,0:T(8,128)S(1)} %get-tuple-element.17.disp_ref, f32[1,25,8,128]{3,2,1,0:T(8,128)S(1)} %get-tuple-element.18.cube_ref, f32[2,25,8,128]{3,2,1,0:T(8,128)S(1)} %get-tuple-element.19.geo_ref, ...), custom_call_target="tpu_custom_call" | custom-call | flops 16777216 | bytes 1048576 | tf_op jit(solution)/shard_map/energy/pallas_call | solution.py:307
  34.5 0.0 copy-start
  34.5 0.0 copy-start.1
  34.5 10.3 %all_to_all.20 = f32[288,1,128]{2,1,0:T(1,128)S(1)} all-to-all(f32[288,1,128]{2,1,0:T(1,128)S(1)} %bitcast.23), channel_id=1, replica_groups=mesh['slab'=8,'load'=4] {'load','slab'}, dimensions={0} | all-to-all | bytes 294912 | tf_op jit(solution)/shard_map/all_to_all | solution.py:322
  44.8 0.0 copy-done
  44.8 0.0 copy-done.1
  44.8 0.3 trial.1
  45.1 10.5 %all_to_all.21 = f32[392,1,128]{2,1,0:T(1,128)S(1)} all-to-all(f32[392,1,128]{2,1,0:T(1,128)S(1)} %bitcast.19), channel_id=1, replica_groups={{12,16,20,24,28,0,4,8},{13,17,21,25,29,1,5,9},{14,18,22,26,30,2,6,10},{..., dimensions={0} | all-to-all | bytes 401408 | tf_op jit(solution)/shard_map/all_to_all | solution.py:322
  55.6 0.8 %final.1 = (f32[2,3,1,64,128]{4,3,2,1,0:T(8,128)}, f32[1,64,128]{2,1,0:T(8,128)}) custom-call(f32[392,128]{1,0:T(8,128)S(1)} %bitcast.18, f32[64,128]{1,0:T(8,128)S(1)} %get-tuple-element.29.trial_ref, s32[1,64,128]{2,1,0:T(8,128)S(1)} %copy-done, f32[8,128]{1,0:T(8,128)S(1)} %get-tuple-element.26.count_ref), custom_call_target="tpu_custom_call" | custom-call | bytes 1048576 | tf_op jit(solution)/shard_map/final/pallas_call | solution.py:307
  (1 shorter events, 0.0 us)
Async XLA Ops:
  2.7 8.0 %copy-start.3 = (f32[2,3,2048]{2,0,1:T(2,128)S(1)}, f32[2,3,2048]{2,0,1:T(2,128)}, u32[]{:S(2)}) copy-start(f32[2,3,2048]{2,0,1:T(2,128)} %param.11) | copy-start | bytes 147460
  2.7 20.0 %all-to-all-start = ((f32[928,1,128]{2,1,0:T(1,128)}), f32[928,1,128]{2,1,0:T(1,128)S(1)}, u32[]{:S(2)}, u32[]{:S(2)}) async-start(f32[928,1,128]{2,1,0:T(1,128)} %bitcast.1), calls=%async_computation | async-start | bytes 950272 | tf_op jit(solution)/shard_map/all_to_all | solution.py:322
  10.7 0.7 %copy-start.2 = (s32[2,2048]{1,0:T(2,128)S(1)}, s32[2,2048]{1,0:T(2,128)}, u32[]{:S(2)}) copy-start(s32[2,2048]{1,0:T(2,128)} %nodes_ref.1) | copy-start | bytes 49156
  24.7 9.1 %all-to-all-start.1 = ((f32[152,1,128]{2,1,0:T(1,128)}), f32[152,1,128]{2,1,0:T(1,128)S(1)}, u32[]{:S(2)}, u32[]{:S(2)}) async-start(f32[152,1,128]{2,1,0:T(1,128)} %bitcast.4), calls=%async_computation.1 | async-start | bytes 155648 | tf_op jit(solution)/shard_map/all_to_all | solution.py:322
  34.5 10.3 %copy-start = (s32[1,64,128]{2,1,0:T(8,128)S(1)}, s32[1,64,128]{2,1,0:T(8,128)}, u32[]{:S(2)}) copy-start(s32[1,64,128]{2,1,0:T(8,128)} %design_ref.5) | copy-start | bytes 98308
  34.5 10.3 %copy-start.1 = (f32[1,64,128]{2,1,0:T(8,128)S(1)}, f32[1,64,128]{2,1,0:T(8,128)}, u32[]{:S(2)}) copy-start(f32[1,64,128]{2,1,0:T(8,128)} %dens_ref.3) | copy-start | bytes 98308

commit v8 on v7

--- a/solution.py
+++ b/solution.py
@@ -460,11 +460,10 @@
         return HALO_LOW <= row < HALO_LOW + strip
 
     last_row = HALO_LOW + strip
-    near_nodes = range(HALO_LOW - 2, last_row + 3)
-    near_zero = range(HALO_LOW - 1, last_row + 2)
-    near_one = range(HALO_LOW, last_row + 1)
-
-    def strip_rows(disp, geo, inverse, zero, one, in_ref, rhs_ref):
+    near_nodes = range(HALO_LOW - 1, last_row + 2)
+    near_zero = range(HALO_LOW, last_row + 1)
+
+    def strip_rows(disp, geo, inverse, zero, in_ref, rhs_ref):
         above, below = shifts(plane, rows_x, ring_start)
         cube_side = iota(plane, 1) < rows_x
         scale_row = lambda row: geo(row)[0, row]
@@ -515,26 +514,33 @@
                 first, last, masked(disp), scale_row, emit, above, below, jnp.zeros(plane, F32)
             )
 
+        def curvature():
+            total, lower = jnp.zeros(plane, F32), None
+            for row in near_zero:
+                modes = row_modes(masked(zero)(row), above)
+                if lower is not None:
+                    total = total + scale_row(row - 1) * element_energy(
+                        element_modes(lower, modes)
+                    )
+                if own_row(row):
+                    fixed = 1.0 - geo(row)[1, row]
+                    values = [zero(row)[comp, row] for comp in range(comps)]
+                    total = total + fixed * sum(value * value for value in values)
+                lower = modes
+            return total
+
         def power(source, target, first, last):
             def emit(row, forces, carried):
                 free, inverted = geo(row)[1, row], inverse(row)[0, row]
-                total = jnp.zeros(plane, F32)
                 for comp, force in enumerate(forces):
-                    value = source(row)[comp, row]
-                    applied = free * force + (1.0 - free) * value
+                    applied = free * force + (1.0 - free) * source(row)[comp, row]
                     target(row)[comp, row] = applied * inverted
-                    total = total + value * applied
-                return carried + total if own_row(row) else carried
-
-            return apply_rows(
-                first, last, masked(source), scale_row, emit, above, below, jnp.zeros(plane, F32)
-            )
-
-        return read, invert, residual, power
-
-    def residual_body(
-        in_ref, rhs_ref, disp_ref, cube_ref, geo_ref, inv_ref, zero_ref, one_ref, sum_ref
-    ):
+
+            apply_rows(first, last, masked(source), scale_row, emit, above, below)
+
+        return read, invert, residual, curvature, power
+
+    def residual_body(in_ref, rhs_ref, disp_ref, cube_ref, geo_ref, inv_ref, zero_ref, sum_ref):
         def gather(offset):
             offset = offset + (comps + 1) * span
             return [
@@ -548,14 +554,13 @@
         share = filter_depth([share[layer * half : (layer + 1) * half] for layer in range(depth)])
         share = swap_blocks([share[layer] for layer in ring], strip)
         here = lambda ref: lambda row: ref
-        zero = here(zero_ref)
-        read, invert, residual, power = strip_rows(
-            here(disp_ref), here(geo_ref), here(inv_ref), zero, here(one_ref), in_ref, rhs_ref
+        read, invert, residual, curvature, _ = strip_rows(
+            here(disp_ref), here(geo_ref), here(inv_ref), here(zero_ref), in_ref, rhs_ref
         )
         read(near_nodes, cube_ref)
         invert(near_zero)
         weight = residual(near_zero[0] - 1, near_zero[-1] + 1)
-        curve = power(zero, here(one_ref), near_one[0] - 1, near_one[-1] + 1)
+        curve = curvature()
         down = lambda value: jnp.sum(value, 0, keepdims=True)
         sums = [down(curve), down(weight), down(mask)]
         for target in range(slabs):
@@ -567,14 +572,13 @@
                 target * half : (target + 1) * half
             ]
 
-    disp, cube, geometry, inverses, zeroth, first, sums = call(
+    disp, cube, geometry, inverses, zeroth, sums = call(
         residual_body,
         (
             block(comps),
             block(1),
             block(2),
             block(1),
-            block(comps),
             block(comps),
             flat(slabs * sum_rows),
         ),
@@ -587,17 +591,15 @@
 
     def powers_body(
         in_ref, rhs_ref, disp_ref, geo_ref, inv_ref, zero_ref, one_ref, two_ref, three_ref,
-        far_disp, far_geo, far_inv, far_zero, far_one,
+        far_disp, far_geo, far_inv, far_zero,
     ):
         choose = lambda near, far, rows: lambda row: near if row in rows else far
         zero = choose(zero_ref, far_zero, near_zero)
-        one = choose(one_ref, far_one, near_one)
-        read, invert, residual, power = strip_rows(
+        read, invert, residual, _, power = strip_rows(
             choose(disp_ref, far_disp, near_nodes),
             choose(geo_ref, far_geo, near_nodes),
             choose(inv_ref, far_inv, near_zero),
             zero,
-            one,
             in_ref,
             rhs_ref,
         )
@@ -605,24 +607,20 @@
         invert([row for row in range(1, span - 1) if row not in near_zero])
         residual(0, near_zero[0])
         residual(near_zero[-1], span - 1)
-        power(zero, one, 1, near_one[0])
-        power(zero, one, near_one[-1], span - 2)
-        power(one, lambda row: two_ref, 2, span - 3)
+        power(zero, lambda row: one_ref, 1, span - 2)
+        power(lambda row: one_ref, lambda row: two_ref, 2, span - 3)
         power(lambda row: two_ref, lambda row: three_ref, 3, span - 4)
 
-    second, third = call(
+    first, second, third = call(
         powers_body,
-        (block(comps), block(comps)),
+        (block(comps), block(comps), block(comps)),
         received,
         right_side,
         disp,
         geometry,
         inverses,
         zeroth,
-        first,
-        scratch=[
-            pltpu.VMEM((count, span) + plane, F32) for count in (comps, 2, 1, comps, comps)
-        ],
+        scratch=[pltpu.VMEM((count, span) + plane, F32) for count in (comps, 2, 1, comps)],
         name="powers",
         flops=1 << 26,
     )

time: 57 us -> 56.6 us (level)
  waiting for transfers between devices: 10.7 us -> 10 us
    all_to_all x2, waiting for transfers between devices: 10.7 us -> 10 us  [exchange(): lax.all_to_all(message.reshape(rows, 1, message.shape[1]), axes, split_ax...]
  transfers between devices with their start and end apart: 2 -> 2, of which waited for: 2 -> 2; matrix products, arithmetic and copies ran while one was open for 0% -> 0% of each run, Pallas kernels for 11% -> 12%
where the time goes in v8:
time: 56.6 us; the launch traced here: 56.1 us
  blocking collectives  20.8 us (37%)
  Pallas kernels  12.3 us (22%)
  starting transfers between devices  11.6 us (20%)
  waiting for transfers between devices  10 us (18%)
  local copies, waits for them, and re-layouts  0.73 us (1%)
  between operations  0.69 us (1%)
    all_to_all x2, blocking collectives, exchange(): lax.all_to_all(message.reshape(rows, 1, message.shape[1]), axes, split_ax...  20.8 us
    pallas_call x7, Pallas kernels, call(): pl.pallas_call(body, out_shape=outs, in_specs=[pl.BlockSpec(memory_space=...  12.3 us
    all_to_all x2, starting transfers between devices, exchange(): lax.all_to_all(message.reshape(rows, 1, message.shape[1]), axes, split_ax...  11.6 us
    all_to_all x2, waiting for transfers between devices, exchange(): lax.all_to_all(message.reshape(rows, 1, message.shape[1]), axes, split_ax...  10 us
  transfers between devices with their start and end apart: 2, of which 2 were waited for; matrix products, arithmetic and copies ran while one was open for 0% of the time, Pallas kernels for 12%

profile of v8, /device:TPU:0, one launch (start us, length us, event | category | flops | bytes accessed | tf_op | source)
XLA Modules:
  0.0 56.1 jit_solution(17730016246732265136)
XLA Ops:
  0.6 2.1 %pack.1 = f32[928,128]{1,0:T(8,128)} custom-call(f32[2,3,1,64,128]{4,3,2,1,0:T(8,128)} %disp_ref.1, f32[1,64,128]{2,1,0:T(8,128)} %dens_ref.3, s32[1,64,128]{2,1,0:T(8,128)} %design_ref.5, s32[1,64,128]{2,1,0:T(8,128)} %support_ref.1), custom_call_target="tpu_custom_call" | custom-call | bytes 1048576 | tf_op jit(solution)/shard_map/pack/pallas_call | solution.py:307
  2.7 0.0 copy-start.3
  2.7 8.0 %all-to-all-start = ((f32[928,1,128]{2,1,0:T(1,128)}), f32[928,1,128]{2,1,0:T(1,128)S(1)}, u32[]{:S(2)}, u32[]{:S(2)}) async-start(f32[928,1,128]{2,1,0:T(1,128)} %bitcast.1), calls=%async_computation | async-start | bytes 950272 | tf_op jit(solution)/shard_map/all_to_all | solution.py:322
  10.7 0.0 copy-done.3
  10.7 0.0 copy-start.2
  10.8 0.7 %copy-done.2 = s32[2,2048]{1,0:T(2,128)S(1)} copy-done((s32[2,2048]{1,0:T(2,128)S(1)}, s32[2,2048]{1,0:T(2,128)}, u32[]{:S(2)}) %copy-start.2) | copy-done | bytes 16408
  11.4 4.1 %point_loads.1.rhs_ref = f32[3,208,128]{2,1,0:T(8,128)S(1)} custom-call(s32[2,2048]{1,0:T(2,128)S(1)} %copy-done.2, f32[2,3,2048]{2,1,0:T(4,128)S(1)} %copy.11.forces_ref), custom_call_target="tpu_custom_call" | custom-call | flops 268435456 | bytes 1048576 | tf_op jit(solution)/shard_map/point_loads/pallas_call | solution.py:307
  15.6 7.1 %all-to-all-done = f32[928,1,128]{2,1,0:T(1,128)S(1)} async-done(((f32[928,1,128]{2,1,0:T(1,128)}), f32[928,1,128]{2,1,0:T(1,128)S(1)}, u32[]{:S(2)}, u32[]{:S(2)}) %all-to-all-start) | async-done | bytes 475168 | tf_op jit(solution)/shard_map/all_to_all | solution.py:322
  22.7 1.6 %residual.1 = (f32[3,25,8,128]{3,2,1,0:T(8,128)S(1)}, f32[1,25,8,128]{3,2,1,0:T(8,128)S(1)}, f32[2,25,8,128]{3,2,1,0:T(8,128)S(1)}, f32[1,25,8,128]{3,2,1,0:T(8,...) custom-call(f32[928,128]{1,0:T(8,128)S(1)} %bitcast.16, f32[3,208,128]{2,1,0:T(8,128)S(1)} %point_loads.1.rhs_ref), custom_call_target="tpu_custom_call" | custom-call | flops 67108864 | bytes 1048576 | tf_op jit(solution)/shard_map/residual/pallas_call | solution.py:307
  24.3 3.6 %all-to-all-start.1 = ((f32[152,1,128]{2,1,0:T(1,128)}), f32[152,1,128]{2,1,0:T(1,128)S(1)}, u32[]{:S(2)}, u32[]{:S(2)}) async-start(f32[152,1,128]{2,1,0:T(1,128)} %bitcast.4), calls=%async_computation.1 | async-start | bytes 155648 | tf_op jit(solution)/shard_map/all_to_all | solution.py:322
  27.9 2.6 %powers.1 = (f32[3,25,8,128]{3,2,1,0:T(8,128)S(1)}, f32[3,25,8,128]{3,2,1,0:T(8,128)S(1)}, f32[3,25,8,128]{3,2,1,0:T(8,128)S(1)}) custom-call(f32[928,128]{1,0:T(8,128)S(1)} %bitcast.17, f32[3,208,128]{2,1,0:T(8,128)S(1)} %point_loads.1.rhs_ref, f32[3,25,8,128]{3,2,1,0:T(8,128)S(1)} %get-tuple-element.17.disp_ref, ...), custom_call_target="tpu_custom_call" | custom-call | flops 67108864 | bytes 1048576 | tf_op jit(solution)/shard_map/powers/pallas_call | solution.py:307
  30.5 3.0 %all-to-all-done.1 = f32[152,1,128]{2,1,0:T(1,128)S(1)} async-done(((f32[152,1,128]{2,1,0:T(1,128)}), f32[152,1,128]{2,1,0:T(1,128)S(1)}, u32[]{:S(2)}, u32[]{:S(2)}) %all-to-all-start.1) | async-done | bytes 77856 | tf_op jit(solution)/shard_map/all_to_all | solution.py:322
  33.4 0.7 %energy.1 = (f32[392,128]{1,0:T(8,128)S(1)}, f32[288,128]{1,0:T(8,128)S(1)}, f32[8,128]{1,0:T(8,128)S(1)}) custom-call(f32[152,128]{1,0:T(8,128)S(1)} %bitcast.20, f32[3,25,8,128]{3,2,1,0:T(8,128)S(1)} %get-tuple-element.17.disp_ref, f32[1,25,8,128]{3,2,1,0:T(8,128)S(1)} %get-tuple-element.18.cube_ref, f32[2,25,8,128]{3,2,1,0:T(8,128)S(1)} %get-tuple-element.19.geo_ref, ...), custom_call_target="tpu_custom_call" | custom-call | flops 16777216 | bytes 1048576 | tf_op jit(solution)/shard_map/energy/pallas_call | solution.py:307
  34.2 0.0 copy-start
  34.2 0.0 copy-start.1
  34.2 10.3 %all_to_all.20 = f32[288,1,128]{2,1,0:T(1,128)S(1)} all-to-all(f32[288,1,128]{2,1,0:T(1,128)S(1)} %bitcast.23), channel_id=1, replica_groups=mesh['slab'=8,'load'=4] {'load','slab'}, dimensions={0} | all-to-all | bytes 294912 | tf_op jit(solution)/shard_map/all_to_all | solution.py:322
  44.5 0.0 copy-done
  44.5 0.0 copy-done.1
  44.5 0.3 trial.1
  44.7 10.5 %all_to_all.21 = f32[392,1,128]{2,1,0:T(1,128)S(1)} all-to-all(f32[392,1,128]{2,1,0:T(1,128)S(1)} %bitcast.19), channel_id=1, replica_groups={{12,16,20,24,28,0,4,8},{13,17,21,25,29,1,5,9},{14,18,22,26,30,2,6,10},{..., dimensions={0} | all-to-all | bytes 401408 | tf_op jit(solution)/shard_map/all_to_all | solution.py:322
  55.3 0.8 %final.1 = (f32[2,3,1,64,128]{4,3,2,1,0:T(8,128)}, f32[1,64,128]{2,1,0:T(8,128)}) custom-call(f32[392,128]{1,0:T(8,128)S(1)} %bitcast.18, f32[64,128]{1,0:T(8,128)S(1)} %get-tuple-element.29.trial_ref, s32[1,64,128]{2,1,0:T(8,128)S(1)} %copy-done, f32[8,128]{1,0:T(8,128)S(1)} %get-tuple-element.26.count_ref), custom_call_target="tpu_custom_call" | custom-call | bytes 1048576 | tf_op jit(solution)/shard_map/final/pallas_call | solution.py:307
  (1 shorter events, 0.0 us)
Async XLA Ops:
  2.7 8.0 %copy-start.3 = (f32[2,3,2048]{2,0,1:T(2,128)S(1)}, f32[2,3,2048]{2,0,1:T(2,128)}, u32[]{:S(2)}) copy-start(f32[2,3,2048]{2,0,1:T(2,128)} %param.11) | copy-start | bytes 147460
  2.7 20.0 %all-to-all-start = ((f32[928,1,128]{2,1,0:T(1,128)}), f32[928,1,128]{2,1,0:T(1,128)S(1)}, u32[]{:S(2)}, u32[]{:S(2)}) async-start(f32[928,1,128]{2,1,0:T(1,128)} %bitcast.1), calls=%async_computation | async-start | bytes 950272 | tf_op jit(solution)/shard_map/all_to_all | solution.py:322
  10.7 0.7 %copy-start.2 = (s32[2,2048]{1,0:T(2,128)S(1)}, s32[2,2048]{1,0:T(2,128)}, u32[]{:S(2)}) copy-start(s32[2,2048]{1,0:T(2,128)} %nodes_ref.1) | copy-start | bytes 49156
  24.3 9.1 %all-to-all-start.1 = ((f32[152,1,128]{2,1,0:T(1,128)}), f32[152,1,128]{2,1,0:T(1,128)S(1)}, u32[]{:S(2)}, u32[]{:S(2)}) async-start(f32[152,1,128]{2,1,0:T(1,128)} %bitcast.4), calls=%async_computation.1 | async-start | bytes 155648 | tf_op jit(solution)/shard_map/all_to_all | solution.py:322
  34.2 10.3 %copy-start = (s32[1,64,128]{2,1,0:T(8,128)S(1)}, s32[1,64,128]{2,1,0:T(8,128)}, u32[]{:S(2)}) copy-start(s32[1,64,128]{2,1,0:T(8,128)} %design_ref.5) | copy-start | bytes 98308
  34.2 10.3 %copy-start.1 = (f32[1,64,128]{2,1,0:T(8,128)S(1)}, f32[1,64,128]{2,1,0:T(8,128)}, u32[]{:S(2)}) copy-start(f32[1,64,128]{2,1,0:T(8,128)} %dens_ref.3) | copy-start | bytes 98308

commit v9 on v8

--- a/solution.py
+++ b/solution.py
@@ -303,7 +303,7 @@
     return [mixed[layer * rows : (layer + 1) * rows] for layer in range(depth)]
 
 
-def call(body, outs, *args, scratch=(), name=None, flops=0, space=pltpu.VMEM, aliases=None):
+def call(body, outs, *args, scratch=(), name=None, flops=0, space=pltpu.VMEM):
     return pl.pallas_call(
         body,
         out_shape=outs,
@@ -312,7 +312,6 @@
         scratch_shapes=list(scratch),
         compiler_params=pltpu.CompilerParams(vmem_limit_bytes=VMEM_LIMIT),
         cost_estimate=pl.CostEstimate(flops=flops, bytes_accessed=1 << 20, transcendentals=0),
-        input_output_aliases=aliases or {},
         name=name,
     )(*args)
 
@@ -743,6 +742,7 @@
         ratio = mask * (numer / filtered_ref[...]) / mean
         trial = jnp.clip(dens * jnp.sqrt(ratio), dens - MOVE_LIMIT, dens + MOVE_LIMIT)
         trial_ref[...] = trial
+        out_ref[...] = disp_ref[...]
         volume = jnp.sum(mask * trial, 0, keepdims=True)
         for target in range(slabs):
             base = (target + 1) * out_rows - 1
@@ -759,7 +759,6 @@
         disp_message,
         scratch=[pltpu.VMEM((rows_x, cols_y), F32)] * 2,
         name="trial",
-        aliases={5: 1},
     )
     out_pieces = exchange(out_message, "slab", ring)
 

time: 56.6 us -> 56.6 us (level)
  no operation moved by 1% of the time
where the time goes in v9:
time: 56.6 us; the launch traced here: 56.1 us
  blocking collectives  20.8 us (37%)
  Pallas kernels  12.3 us (22%)
  starting transfers between devices  11.6 us (20%)
  waiting for transfers between devices  10 us (18%)
  local copies, waits for them, and re-layouts  0.73 us (1%)
  between operations  0.69 us (1%)
    all_to_all x2, blocking collectives, exchange(): lax.all_to_all(message.reshape(rows, 1, message.shape[1]), axes, split_ax...  20.8 us
    pallas_call x7, Pallas kernels, call(): pl.pallas_call(body, out_shape=outs, in_specs=[pl.BlockSpec(memory_space=...  12.3 us
    all_to_all x2, starting transfers between devices, exchange(): lax.all_to_all(message.reshape(rows, 1, message.shape[1]), axes, split_ax...  11.6 us
    all_to_all x2, waiting for transfers between devices, exchange(): lax.all_to_all(message.reshape(rows, 1, message.shape[1]), axes, split_ax...  10 us
  transfers between devices with their start and end apart: 2, of which 2 were waited for; matrix products, arithmetic and copies ran while one was open for 0% of the time, Pallas kernels for 12%

profile of v9, /device:TPU:0, one launch (start us, length us, event | category | flops | bytes accessed | tf_op | source)
XLA Modules:
  0.0 56.1 jit_solution(3406889164014239473)
XLA Ops:
  0.6 2.1 %pack.1 = f32[928,128]{1,0:T(8,128)} custom-call(f32[2,3,1,64,128]{4,3,2,1,0:T(8,128)} %disp_ref.1, f32[1,64,128]{2,1,0:T(8,128)} %dens_ref.3, s32[1,64,128]{2,1,0:T(8,128)} %design_ref.5, s32[1,64,128]{2,1,0:T(8,128)} %support_ref.1), custom_call_target="tpu_custom_call" | custom-call | bytes 1048576 | tf_op jit(solution)/shard_map/pack/pallas_call | solution.py:307
  2.7 0.0 copy-start.3
  2.7 8.0 %all-to-all-start = ((f32[928,1,128]{2,1,0:T(1,128)}), f32[928,1,128]{2,1,0:T(1,128)S(1)}, u32[]{:S(2)}, u32[]{:S(2)}) async-start(f32[928,1,128]{2,1,0:T(1,128)} %bitcast.1), calls=%async_computation | async-start | bytes 950272 | tf_op jit(solution)/shard_map/all_to_all | solution.py:321
  10.7 0.0 copy-done.3
  10.7 0.0 copy-start.2
  10.8 0.7 %copy-done.2 = s32[2,2048]{1,0:T(2,128)S(1)} copy-done((s32[2,2048]{1,0:T(2,128)S(1)}, s32[2,2048]{1,0:T(2,128)}, u32[]{:S(2)}) %copy-start.2) | copy-done | bytes 16408
  11.4 4.1 %point_loads.1.rhs_ref = f32[3,208,128]{2,1,0:T(8,128)S(1)} custom-call(s32[2,2048]{1,0:T(2,128)S(1)} %copy-done.2, f32[2,3,2048]{2,1,0:T(4,128)S(1)} %copy.10.forces_ref), custom_call_target="tpu_custom_call" | custom-call | flops 268435456 | bytes 1048576 | tf_op jit(solution)/shard_map/point_loads/pallas_call | solution.py:307
  15.6 7.1 %all-to-all-done = f32[928,1,128]{2,1,0:T(1,128)S(1)} async-done(((f32[928,1,128]{2,1,0:T(1,128)}), f32[928,1,128]{2,1,0:T(1,128)S(1)}, u32[]{:S(2)}, u32[]{:S(2)}) %all-to-all-start) | async-done | bytes 475168 | tf_op jit(solution)/shard_map/all_to_all | solution.py:321
  22.7 1.6 %residual.1 = (f32[3,25,8,128]{3,2,1,0:T(8,128)S(1)}, f32[1,25,8,128]{3,2,1,0:T(8,128)S(1)}, f32[2,25,8,128]{3,2,1,0:T(8,128)S(1)}, f32[1,25,8,128]{3,2,1,0:T(8,...) custom-call(f32[928,128]{1,0:T(8,128)S(1)} %bitcast.16, f32[3,208,128]{2,1,0:T(8,128)S(1)} %point_loads.1.rhs_ref), custom_call_target="tpu_custom_call" | custom-call | flops 67108864 | bytes 1048576 | tf_op jit(solution)/shard_map/residual/pallas_call | solution.py:307
  24.3 3.6 %all-to-all-start.1 = ((f32[152,1,128]{2,1,0:T(1,128)}), f32[152,1,128]{2,1,0:T(1,128)S(1)}, u32[]{:S(2)}, u32[]{:S(2)}) async-start(f32[152,1,128]{2,1,0:T(1,128)} %bitcast.4), calls=%async_computation.1 | async-start | bytes 155648 | tf_op jit(solution)/shard_map/all_to_all | solution.py:321
  27.9 2.6 %powers.1 = (f32[3,25,8,128]{3,2,1,0:T(8,128)S(1)}, f32[3,25,8,128]{3,2,1,0:T(8,128)S(1)}, f32[3,25,8,128]{3,2,1,0:T(8,128)S(1)}) custom-call(f32[928,128]{1,0:T(8,128)S(1)} %bitcast.17, f32[3,208,128]{2,1,0:T(8,128)S(1)} %point_loads.1.rhs_ref, f32[3,25,8,128]{3,2,1,0:T(8,128)S(1)} %get-tuple-element.17.disp_ref, ...), custom_call_target="tpu_custom_call" | custom-call | flops 67108864 | bytes 1048576 | tf_op jit(solution)/shard_map/powers/pallas_call | solution.py:307
  30.5 3.0 %all-to-all-done.1 = f32[152,1,128]{2,1,0:T(1,128)S(1)} async-done(((f32[152,1,128]{2,1,0:T(1,128)}), f32[152,1,128]{2,1,0:T(1,128)S(1)}, u32[]{:S(2)}, u32[]{:S(2)}) %all-to-all-start.1) | async-done | bytes 77856 | tf_op jit(solution)/shard_map/all_to_all | solution.py:321
  33.4 0.7 %energy.1 = (f32[392,128]{1,0:T(8,128)S(1)}, f32[288,128]{1,0:T(8,128)S(1)}, f32[8,128]{1,0:T(8,128)S(1)}) custom-call(f32[152,128]{1,0:T(8,128)S(1)} %bitcast.19, f32[3,25,8,128]{3,2,1,0:T(8,128)S(1)} %get-tuple-element.17.disp_ref, f32[1,25,8,128]{3,2,1,0:T(8,128)S(1)} %get-tuple-element.18.cube_ref, f32[2,25,8,128]{3,2,1,0:T(8,128)S(1)} %get-tuple-element.19.geo_ref, ...), custom_call_target="tpu_custom_call" | custom-call | flops 16777216 | bytes 1048576 | tf_op jit(solution)/shard_map/energy/pallas_call | solution.py:307
  34.2 0.0 copy-start
  34.2 0.0 copy-start.1
  34.2 10.3 %all_to_all.20 = f32[288,1,128]{2,1,0:T(1,128)S(1)} all-to-all(f32[288,1,128]{2,1,0:T(1,128)S(1)} %bitcast.23), channel_id=1, replica_groups=mesh['slab'=8,'load'=4] {'load','slab'}, dimensions={0} | all-to-all | bytes 294912 | tf_op jit(solution)/shard_map/all_to_all | solution.py:321
  44.5 0.0 copy-done
  44.5 0.0 copy-done.1
  44.5 0.3 trial.1
  44.7 10.5 %all_to_all.21 = f32[392,1,128]{2,1,0:T(1,128)S(1)} all-to-all(f32[392,1,128]{2,1,0:T(1,128)S(1)} %bitcast.22), channel_id=1, replica_groups={{12,16,20,24,28,0,4,8},{13,17,21,25,29,1,5,9},{14,18,22,26,30,2,6,10},{..., dimensions={0} | all-to-all | bytes 401408 | tf_op jit(solution)/shard_map/all_to_all | solution.py:321
  55.3 0.8 %final.1 = (f32[2,3,1,64,128]{4,3,2,1,0:T(8,128)}, f32[1,64,128]{2,1,0:T(8,128)}) custom-call(f32[392,128]{1,0:T(8,128)S(1)} %bitcast.18, f32[64,128]{1,0:T(8,128)S(1)} %get-tuple-element.29.trial_ref, s32[1,64,128]{2,1,0:T(8,128)S(1)} %copy-done, f32[8,128]{1,0:T(8,128)S(1)} %get-tuple-element.26.count_ref), custom_call_target="tpu_custom_call" | custom-call | bytes 1048576 | tf_op jit(solution)/shard_map/final/pallas_call | solution.py:307
  (1 shorter events, 0.0 us)
Async XLA Ops:
  2.7 8.0 %copy-start.3 = (f32[2,3,2048]{2,0,1:T(2,128)S(1)}, f32[2,3,2048]{2,0,1:T(2,128)}, u32[]{:S(2)}) copy-start(f32[2,3,2048]{2,0,1:T(2,128)} %param.11) | copy-start | bytes 147460
  2.7 20.0 %all-to-all-start = ((f32[928,1,128]{2,1,0:T(1,128)}), f32[928,1,128]{2,1,0:T(1,128)S(1)}, u32[]{:S(2)}, u32[]{:S(2)}) async-start(f32[928,1,128]{2,1,0:T(1,128)} %bitcast.1), calls=%async_computation | async-start | bytes 950272 | tf_op jit(solution)/shard_map/all_to_all | solution.py:321
  10.7 0.7 %copy-start.2 = (s32[2,2048]{1,0:T(2,128)S(1)}, s32[2,2048]{1,0:T(2,128)}, u32[]{:S(2)}) copy-start(s32[2,2048]{1,0:T(2,128)} %nodes_ref.1) | copy-start | bytes 49156
  24.3 9.1 %all-to-all-start.1 = ((f32[152,1,128]{2,1,0:T(1,128)}), f32[152,1,128]{2,1,0:T(1,128)S(1)}, u32[]{:S(2)}, u32[]{:S(2)}) async-start(f32[152,1,128]{2,1,0:T(1,128)} %bitcast.4), calls=%async_computation.1 | async-start | bytes 155648 | tf_op jit(solution)/shard_map/all_to_all | solution.py:321
  34.2 10.3 %copy-start = (s32[1,64,128]{2,1,0:T(8,128)S(1)}, s32[1,64,128]{2,1,0:T(8,128)}, u32[]{:S(2)}) copy-start(s32[1,64,128]{2,1,0:T(8,128)} %design_ref.5) | copy-start | bytes 98308
  34.2 10.3 %copy-start.1 = (f32[1,64,128]{2,1,0:T(8,128)S(1)}, f32[1,64,128]{2,1,0:T(8,128)}, u32[]{:S(2)}) copy-start(f32[1,64,128]{2,1,0:T(8,128)} %dens_ref.3) | copy-start | bytes 98308

commit v10 on v9

--- a/solution.py
+++ b/solution.py
@@ -303,12 +303,12 @@
     return [mixed[layer * rows : (layer + 1) * rows] for layer in range(depth)]
 
 
-def call(body, outs, *args, scratch=(), name=None, flops=0, space=pltpu.VMEM):
+def call(body, outs, *args, scratch=(), name=None, flops=0, space=pltpu.VMEM, out_space=pltpu.VMEM):
     return pl.pallas_call(
         body,
         out_shape=outs,
         in_specs=[pl.BlockSpec(memory_space=space)] * len(args),
-        out_specs=jax.tree.map(lambda _: pl.BlockSpec(memory_space=pltpu.VMEM), outs),
+        out_specs=jax.tree.map(lambda _: pl.BlockSpec(memory_space=out_space), outs),
         scratch_shapes=list(scratch),
         compiler_params=pltpu.CompilerParams(vmem_limit_bytes=VMEM_LIMIT),
         cost_estimate=pl.CostEstimate(flops=flops, bytes_accessed=1 << 20, transcendentals=0),
@@ -354,9 +354,10 @@
     sums_place = lambda index: (index - sums_start) % slabs
 
     def pack_body(
-        disp_ref, dens_ref, design_ref, support_ref, out_ref,
-        stage_ref, dens_in, design_in, support_in, pad_ref, sems,
+        disp_ref, dens_ref, design_ref, support_ref, message_ref,
+        stage_ref, dens_in, design_in, support_in, pad_ref, sems, out_ref, out_sems,
     ):
+        sent = []
         copies = [
             pltpu.make_async_copy(dens_ref.at[0], dens_in, sems.at[0]),
             pltpu.make_async_copy(design_ref.at[0], design_in, sems.at[1]),
@@ -399,6 +400,15 @@
             base = base + (comps + 1) * span
             out_ref[base : base + half] = spread[rows]
             out_ref[base + half : base + 2 * half] = design_in[rows].astype(F32)
+            part = pl.ds(place(target) * in_rows, in_rows)
+            sent.append(
+                pltpu.make_async_copy(
+                    out_ref.at[part], message_ref.at[part], out_sems.at[target]
+                )
+            )
+            sent[-1].start()
+        for copy in sent:
+            copy.wait()
 
     message = call(
         pack_body,
@@ -414,9 +424,12 @@
             pltpu.VMEM((rows_x, cols_y), jnp.int32),
             pltpu.VMEM((comps + 1, cols_y + 2 * 8, width), F32),
             pltpu.SemaphoreType.DMA((3 + loads,)),
+            pltpu.VMEM((slabs * in_rows, width), F32),
+            pltpu.SemaphoreType.DMA((slabs,)),
         ],
         name="pack",
         space=pltpu.HBM,
+        out_space=pltpu.HBM,
     )
     received = exchange(message, "slab", ring)
 

time: 56.6 us -> 56.6 us (level)
  no operation moved by 1% of the time
where the time goes in v10:
time: 56.6 us; the launch traced here: 56.1 us
  blocking collectives  20.8 us (37%)
  Pallas kernels  12.3 us (22%)
  starting transfers between devices  11.6 us (20%)
  waiting for transfers between devices  10 us (18%)
  local copies, waits for them, and re-layouts  0.73 us (1%)
  between operations  0.69 us (1%)
    all_to_all x2, blocking collectives, exchange(): lax.all_to_all(message.reshape(rows, 1, message.shape[1]), axes, split_ax...  20.8 us
    pallas_call x7, Pallas kernels, call(): pl.pallas_call(body, out_shape=outs, in_specs=[pl.BlockSpec(memory_space=...  12.3 us
    all_to_all x2, starting transfers between devices, exchange(): lax.all_to_all(message.reshape(rows, 1, message.shape[1]), axes, split_ax...  11.6 us
    all_to_all x2, waiting for transfers between devices, exchange(): lax.all_to_all(message.reshape(rows, 1, message.shape[1]), axes, split_ax...  10 us
  transfers between devices with their start and end apart: 2, of which 2 were waited for; matrix products, arithmetic and copies ran while one was open for 0% of the time, Pallas kernels for 12%

profile of v10, /device:TPU:0, one launch (start us, length us, event | category | flops | bytes accessed | tf_op | source)
XLA Modules:
  0.0 56.1 jit_solution(17899862531023990523)
XLA Ops:
  0.6 2.1 %pack.1 = f32[928,128]{1,0:T(8,128)} custom-call(f32[2,3,1,64,128]{4,3,2,1,0:T(8,128)} %disp_ref.1, f32[1,64,128]{2,1,0:T(8,128)} %dens_ref.3, s32[1,64,128]{2,1,0:T(8,128)} %design_ref.5, s32[1,64,128]{2,1,0:T(8,128)} %support_ref.1), custom_call_target="tpu_custom_call" | custom-call | bytes 1048576 | tf_op jit(solution)/shard_map/pack/pallas_call | solution.py:307
  2.7 0.0 copy-start.3
  2.8 8.0 %all-to-all-start = ((f32[928,1,128]{2,1,0:T(1,128)}), f32[928,1,128]{2,1,0:T(1,128)S(1)}, u32[]{:S(2)}, u32[]{:S(2)}) async-start(f32[928,1,128]{2,1,0:T(1,128)} %bitcast.1), calls=%async_computation | async-start | bytes 950272 | tf_op jit(solution)/shard_map/all_to_all | solution.py:321
  10.7 0.0 copy-done.3
  10.7 0.0 copy-start.2
  10.8 0.7 %copy-done.2 = s32[2,2048]{1,0:T(2,128)S(1)} copy-done((s32[2,2048]{1,0:T(2,128)S(1)}, s32[2,2048]{1,0:T(2,128)}, u32[]{:S(2)}) %copy-start.2) | copy-done | bytes 16408
  11.5 4.1 %point_loads.1.rhs_ref = f32[3,208,128]{2,1,0:T(8,128)S(1)} custom-call(s32[2,2048]{1,0:T(2,128)S(1)} %copy-done.2, f32[2,3,2048]{2,1,0:T(4,128)S(1)} %copy.10.forces_ref), custom_call_target="tpu_custom_call" | custom-call | flops 268435456 | bytes 1048576 | tf_op jit(solution)/shard_map/point_loads/pallas_call | solution.py:307
  15.6 7.1 %all-to-all-done = f32[928,1,128]{2,1,0:T(1,128)S(1)} async-done(((f32[928,1,128]{2,1,0:T(1,128)}), f32[928,1,128]{2,1,0:T(1,128)S(1)}, u32[]{:S(2)}, u32[]{:S(2)}) %all-to-all-start) | async-done | bytes 475168 | tf_op jit(solution)/shard_map/all_to_all | solution.py:321
  22.7 1.6 %residual.1 = (f32[3,25,8,128]{3,2,1,0:T(8,128)S(1)}, f32[1,25,8,128]{3,2,1,0:T(8,128)S(1)}, f32[2,25,8,128]{3,2,1,0:T(8,128)S(1)}, f32[1,25,8,128]{3,2,1,0:T(8,...) custom-call(f32[928,128]{1,0:T(8,128)S(1)} %bitcast.16, f32[3,208,128]{2,1,0:T(8,128)S(1)} %point_loads.1.rhs_ref), custom_call_target="tpu_custom_call" | custom-call | flops 67108864 | bytes 1048576 | tf_op jit(solution)/shard_map/residual/pallas_call | solution.py:307
  24.4 3.6 %all-to-all-start.1 = ((f32[152,1,128]{2,1,0:T(1,128)}), f32[152,1,128]{2,1,0:T(1,128)S(1)}, u32[]{:S(2)}, u32[]{:S(2)}) async-start(f32[152,1,128]{2,1,0:T(1,128)} %bitcast.4), calls=%async_computation.1 | async-start | bytes 155648 | tf_op jit(solution)/shard_map/all_to_all | solution.py:321
  27.9 2.6 %powers.1 = (f32[3,25,8,128]{3,2,1,0:T(8,128)S(1)}, f32[3,25,8,128]{3,2,1,0:T(8,128)S(1)}, f32[3,25,8,128]{3,2,1,0:T(8,128)S(1)}) custom-call(f32[928,128]{1,0:T(8,128)S(1)} %bitcast.17, f32[3,208,128]{2,1,0:T(8,128)S(1)} %point_loads.1.rhs_ref, f32[3,25,8,128]{3,2,1,0:T(8,128)S(1)} %get-tuple-element.17.disp_ref, ...), custom_call_target="tpu_custom_call" | custom-call | flops 67108864 | bytes 1048576 | tf_op jit(solution)/shard_map/powers/pallas_call | solution.py:307
  30.5 3.0 %all-to-all-done.1 = f32[152,1,128]{2,1,0:T(1,128)S(1)} async-done(((f32[152,1,128]{2,1,0:T(1,128)}), f32[152,1,128]{2,1,0:T(1,128)S(1)}, u32[]{:S(2)}, u32[]{:S(2)}) %all-to-all-start.1) | async-done | bytes 77856 | tf_op jit(solution)/shard_map/all_to_all | solution.py:321
  33.5 0.7 %energy.1 = (f32[392,128]{1,0:T(8,128)S(1)}, f32[288,128]{1,0:T(8,128)S(1)}, f32[8,128]{1,0:T(8,128)S(1)}) custom-call(f32[152,128]{1,0:T(8,128)S(1)} %bitcast.19, f32[3,25,8,128]{3,2,1,0:T(8,128)S(1)} %get-tuple-element.17.disp_ref, f32[1,25,8,128]{3,2,1,0:T(8,128)S(1)} %get-tuple-element.18.cube_ref, f32[2,25,8,128]{3,2,1,0:T(8,128)S(1)} %get-tuple-element.19.geo_ref, ...), custom_call_target="tpu_custom_call" | custom-call | flops 16777216 | bytes 1048576 | tf_op jit(solution)/shard_map/energy/pallas_call | solution.py:307
  34.2 0.0 copy-start
  34.2 0.0 copy-start.1
  34.2 10.3 %all_to_all.20 = f32[288,1,128]{2,1,0:T(1,128)S(1)} all-to-all(f32[288,1,128]{2,1,0:T(1,128)S(1)} %bitcast.23), channel_id=1, replica_groups=mesh['slab'=8,'load'=4] {'load','slab'}, dimensions={0} | all-to-all | bytes 294912 | tf_op jit(solution)/shard_map/all_to_all | solution.py:321
  44.5 0.0 copy-done
  44.5 0.0 copy-done.1
  44.5 0.3 trial.1
  44.8 10.5 %all_to_all.21 = f32[392,1,128]{2,1,0:T(1,128)S(1)} all-to-all(f32[392,1,128]{2,1,0:T(1,128)S(1)} %bitcast.22), channel_id=1, replica_groups={{12,16,20,24,28,0,4,8},{13,17,21,25,29,1,5,9},{14,18,22,26,30,2,6,10},{..., dimensions={0} | all-to-all | bytes 401408 | tf_op jit(solution)/shard_map/all_to_all | solution.py:321
  55.3 0.8 %final.1 = (f32[2,3,1,64,128]{4,3,2,1,0:T(8,128)}, f32[1,64,128]{2,1,0:T(8,128)}) custom-call(f32[392,128]{1,0:T(8,128)S(1)} %bitcast.18, f32[64,128]{1,0:T(8,128)S(1)} %get-tuple-element.29.trial_ref, s32[1,64,128]{2,1,0:T(8,128)S(1)} %copy-done, f32[8,128]{1,0:T(8,128)S(1)} %get-tuple-element.26.count_ref), custom_call_target="tpu_custom_call" | custom-call | bytes 1048576 | tf_op jit(solution)/shard_map/final/pallas_call | solution.py:307
  (1 shorter events, 0.0 us)
Async XLA Ops:
  2.7 8.0 %copy-start.3 = (f32[2,3,2048]{2,0,1:T(2,128)S(1)}, f32[2,3,2048]{2,0,1:T(2,128)}, u32[]{:S(2)}) copy-start(f32[2,3,2048]{2,0,1:T(2,128)} %param.11) | copy-start | bytes 147460
  2.8 20.0 %all-to-all-start = ((f32[928,1,128]{2,1,0:T(1,128)}), f32[928,1,128]{2,1,0:T(1,128)S(1)}, u32[]{:S(2)}, u32[]{:S(2)}) async-start(f32[928,1,128]{2,1,0:T(1,128)} %bitcast.1), calls=%async_computation | async-start | bytes 950272 | tf_op jit(solution)/shard_map/all_to_all | solution.py:321
  10.7 0.7 %copy-start.2 = (s32[2,2048]{1,0:T(2,128)S(1)}, s32[2,2048]{1,0:T(2,128)}, u32[]{:S(2)}) copy-start(s32[2,2048]{1,0:T(2,128)} %nodes_ref.1) | copy-start | bytes 49156
  24.4 9.1 %all-to-all-start.1 = ((f32[152,1,128]{2,1,0:T(1,128)}), f32[152,1,128]{2,1,0:T(1,128)S(1)}, u32[]{:S(2)}, u32[]{:S(2)}) async-start(f32[152,1,128]{2,1,0:T(1,128)} %bitcast.4), calls=%async_computation.1 | async-start | bytes 155648 | tf_op jit(solution)/shard_map/all_to_all | solution.py:321
  34.2 10.3 %copy-start = (s32[1,64,128]{2,1,0:T(8,128)S(1)}, s32[1,64,128]{2,1,0:T(8,128)}, u32[]{:S(2)}) copy-start(s32[1,64,128]{2,1,0:T(8,128)} %design_ref.5) | copy-start | bytes 98308
  34.2 10.3 %copy-start.1 = (f32[1,64,128]{2,1,0:T(8,128)S(1)}, f32[1,64,128]{2,1,0:T(8,128)}, u32[]{:S(2)}) copy-start(f32[1,64,128]{2,1,0:T(8,128)} %dens_ref.3) | copy-start | bytes 98308
